TPU v7x, 128 devices: a whole 4x4x4 slice. The times are simulated.
128 devices in a mesh: seq: 32 (over x_lo, y, z), res: 4 (over x_hi, core).
Axes of the slice: x: 4 (x_hi: 2, x_lo: 2; x = x_hi * 2 + x_lo), y: 4, z: 4, core: 2. Of those that a mesh axis runs over, the one named last changes fastest.
Arguments:
- alignment_embedding: bfloat16 [256, 512, 768], P('seq', 'res'), may hold values from -6 to 6
- horizontal_scale_vector: float32 [768], replicated, may hold values from 0.1 to 1.9
- horizontal_probe_matrix: bfloat16 [768, 768], replicated, may hold values from -0.21875 to 0.21875
- horizontal_lookup_matrix: bfloat16 [768, 768], replicated, may hold values from -0.21875 to 0.21875
- horizontal_content_matrix: bfloat16 [768, 768], replicated, may hold values from -0.21875 to 0.21875
- horizontal_emit_matrix: bfloat16 [768, 768], replicated, may hold values from -0.21875 to 0.21875
- vertical_scale_vector: float32 [768], replicated, may hold values from 0.1 to 1.9
- vertical_probe_matrix: bfloat16 [768, 768], replicated, may hold values from -0.21875 to 0.21875
- vertical_lookup_matrix: bfloat16 [768, 768], replicated, may hold values from -0.21875 to 0.21875
- vertical_content_matrix: bfloat16 [768, 768], replicated, may hold values from -0.21875 to 0.21875
- vertical_emit_matrix: bfloat16 [768, 768], replicated, may hold values from -0.21875 to 0.21875
Outputs:
- layer_out: bfloat16 [256, 512, 768], P('seq', 'res')
All inputs are finite; a program needn't handle non-finite values.
Results may differ from a plain program's by a relative error of at most 0.02.
Values may be sent and summed in bfloat16 or wider, within the bound.
No kernel may reach another device: no remote copies, remote signals or barrier semaphores. Data moves between devices by JAX's collectives and lax.ppermute only.
A program may use at most 128 MiB of HBM per device.

v0:
```python
import functools
import math

import jax
import jax.numpy as jnp
from jax import lax
from jax.experimental import pallas as pl
from jax.experimental.pallas import tpu as pltpu
from jax.sharding import PartitionSpec as P

HEADS = 12
D = 64
SEQ = 32
CORE_SWAP = [(0, 1), (1, 0), (2, 3), (3, 2)]
XHI_SWAP = [(0, 2), (1, 3), (2, 0), (3, 1)]
F32 = jnp.float32
BF16 = jnp.bfloat16
PARAMS = pltpu.CompilerParams(vmem_limit_bytes=56 * 1024 * 1024)


def norm(x, gain):
    v = x.astype(F32)
    c = v - jnp.mean(v, axis=-1, keepdims=True)
    var = jnp.mean(c * c, axis=-1, keepdims=True)
    return (c * lax.rsqrt(var + 1e-05) * gain).astype(BF16)


def mm(a, b):
    return lax.dot_general(a, b, (((1,), (0,)), ((), ())), preferred_element_type=F32)


def mm_t(a, b):
    return lax.dot_general(a, b, (((1,), (1,)), ((), ())), preferred_element_type=F32)


def head(x, h):
    return x[:, h * D : (h + 1) * D]


def pair_store(ref, y0, y1, lane):
    for h in range(HEADS):
        ref[h, :, pl.ds(lane, 2 * D)] = jnp.concatenate([head(y0, h), head(y1, h)], axis=1)


def whole(shape):
    return pl.BlockSpec(shape, lambda *_: (0,) * len(shape))


def logits_kernel(first, *refs):
    if first:
        xa, xb, g, wk, wq, q, out, ks = refs
    else:
        xa, xb, g, wk, q, out, ks = refs
    t = pl.program_id(0)
    n = xa.shape[1]
    lane = pl.multiple_of(t * 2 * D, 2 * D)
    f = xa.shape[2]
    na = norm(xa[...].reshape(2 * n, f), g[...])
    nb = norm(xb[...].reshape(2 * n, f), g[...])
    ka = mm(na, wk[...]).astype(BF16)
    kb = mm(nb, wk[...]).astype(BF16)
    for h in range(HEADS):
        ks[h, 0:n, pl.ds(lane, 2 * D)] = jnp.concatenate([head(ka[:n], h), head(ka[n:], h)], axis=1)
        ks[h, n : 2 * n, pl.ds(lane, 2 * D)] = jnp.concatenate([head(kb[:n], h), head(kb[n:], h)], axis=1)
    if first:
        qq = mm(na, wq[...]).astype(BF16)
        pair_store(q, qq[:n], qq[n:], lane)

    @pl.when(t == pl.num_programs(0) - 1)
    def _():
        for h in range(HEADS):
            out[h] = mm_t(q[h], ks[h]).astype(BF16)


def logits(xa, xb, g, wk, wq=None, q=None):
    s, n, f = xa.shape
    first = q is None
    xs = pl.BlockSpec((2, n, f), lambda t: (t, 0, 0))
    in_specs = [xs, xs, whole(g.shape), whole(wk.shape)]
    qshape = (HEADS, n, s * D)
    lshape = (HEADS, n, 2 * n)
    in_specs += [whole(wq.shape)] if first else [whole(qshape)]
    ospecs = [whole(qshape), whole(lshape)] if first else [whole(lshape)]
    oshape = [jax.ShapeDtypeStruct(qshape, BF16), jax.ShapeDtypeStruct(lshape, BF16)]
    return pl.pallas_call(
        functools.partial(logits_kernel, first),
        grid=(s // 2,),
        in_specs=in_specs,
        out_specs=ospecs,
        out_shape=oshape if first else oshape[1:],
        scratch_shapes=[pltpu.VMEM((HEADS, 2 * n, s * D), BF16)],
        compiler_params=PARAMS,
        name="logits",
    )(xa, xb, g, wk, wq if first else q)


def values_kernel(xa, xb, g, wv, out):
    n, f = xa.shape[1], xa.shape[2]
    va = mm(norm(xa[...].reshape(2 * n, f), g[...]), wv[...]).astype(BF16)
    vb = mm(norm(xb[...].reshape(2 * n, f), g[...]), wv[...]).astype(BF16)
    for h in range(HEADS):
        out[h, 0:n] = jnp.concatenate([head(va[:n], h), head(va[n:], h)], axis=1)
        out[h, n : 2 * n] = jnp.concatenate([head(vb[:n], h), head(vb[n:], h)], axis=1)


def values(xa, xb, g, wv):
    s, n, f = xa.shape
    xs = pl.BlockSpec((2, n, f), lambda t: (t, 0, 0))
    return pl.pallas_call(
        values_kernel,
        grid=(s // 2,),
        in_specs=[xs, xs, whole(g.shape), whole(wv.shape)],
        out_specs=pl.BlockSpec((HEADS, 2 * n, 2 * D), lambda t: (0, 0, t)),
        out_shape=jax.ShapeDtypeStruct((HEADS, 2 * n, s * D), BF16),
        compiler_params=PARAMS,
        name="values",
    )(xa, xb, g, wv)


def mix_kernel(p, v1, v2, x, wo, out, ms):
    t = pl.program_id(0)
    n = p.shape[1]
    s = x.shape[0]
    lane = pl.multiple_of(t * 2 * D, 2 * D)
    o = []
    for h in range(2):
        o.append((mm(p[h, :, : 2 * n], v1[h]) + mm(p[h, :, 2 * n :], v2[h])).astype(BF16))
    for r in range(s):
        ms[r, :, pl.ds(lane, 2 * D)] = jnp.concatenate([head(o[0], r), head(o[1], r)], axis=1)

    @pl.when(t == pl.num_programs(0) - 1)
    def _():
        for r in range(s):
            out[r] = (x[r].astype(F32) + mm(ms[r], wo[...])).astype(BF16)


def mix(p, v1, v2, x, wo):
    s, n, f = x.shape
    vs = pl.BlockSpec((2, 2 * n, s * D), lambda t: (t, 0, 0))
    return pl.pallas_call(
        mix_kernel,
        grid=(HEADS // 2,),
        in_specs=[pl.BlockSpec((2, n, 4 * n), lambda t: (t, 0, 0)), vs, vs, whole(x.shape), whole(wo.shape)],
        out_specs=whole(x.shape),
        out_shape=jax.ShapeDtypeStruct(x.shape, BF16),
        scratch_shapes=[pltpu.VMEM((s, n, f), BF16)],
        compiler_params=PARAMS,
        name="mix",
    )(p, v1, v2, x, wo)


def column_kernel(h_ref, g, wq, wk, wv, wo, out, ms):
    x = h_ref[0].astype(F32)
    n = norm(x, g[...])
    q = (mm(n, wq[...]) * (1.0 / (math.sqrt(D) * math.log(2.0)))).astype(BF16)
    k = mm(n, wk[...]).astype(BF16)
    v = mm(n, wv[...]).astype(BF16)
    for hp in range(HEADS // 2):
        pair = []
        for h in (2 * hp, 2 * hp + 1):
            l = mm_t(head(q, h), head(k, h))
            e = jnp.exp2(l - jnp.max(l, axis=-1, keepdims=True))
            d = jnp.sum(e, axis=-1, keepdims=True)
            pair.append((mm(e.astype(BF16), head(v, h)) / d).astype(BF16))
        ms[:, hp * 2 * D : (hp + 1) * 2 * D] = jnp.concatenate(pair, axis=1)
    out[0] = (x + mm(ms[...], wo[...])).astype(BF16)


def column(hc, g, wq, wk, wv, wo):
    c, a, f = hc.shape
    xs = pl.BlockSpec((1, a, f), lambda t: (t, 0, 0))
    return pl.pallas_call(
        column_kernel,
        grid=(c,),
        in_specs=[xs, whole(g.shape)] + [whole(w.shape) for w in (wq, wk, wv, wo)],
        out_specs=xs,
        out_shape=jax.ShapeDtypeStruct(hc.shape, BF16),
        scratch_shapes=[pltpu.VMEM((a, f), BF16)],
        compiler_params=PARAMS,
        name="column",
    )(hc, g, wq, wk, wv, wo)


def a2a(x):
    return lax.all_to_all(x, "seq", split_axis=0, concat_axis=0, tiled=True)


def shards(x, hg, wq, wk, wv, wo, vg, cq, ck, cv, co):
    S, N, F = x.shape
    hg = hg.reshape(1, F)
    vg = vg.reshape(1, F)
    xh = lax.ppermute(x, "res", XHI_SWAP)
    sib = lax.ppermute(x, "res", CORE_SWAP)
    xhs = lax.ppermute(xh, "res", CORE_SWAP)

    def reduce(l):
        return jnp.sum(a2a(l.reshape(SEQ, HEADS * N // SEQ, 2 * N)).astype(F32), axis=0)

    q, l1 = logits(x, sib, hg, wk, wq=wq)
    r1 = reduce(l1)
    v1 = values(x, sib, hg, wv)
    (l2,) = logits(xh, xhs, hg, wk, q=q)
    r2 = reduce(l2)
    v2 = values(xh, xhs, hg, wv)
    scale = 1.0 / (math.sqrt(D) * math.sqrt(S * SEQ))
    probs = jax.nn.softmax(jnp.concatenate([r1, r2], axis=-1) * scale, axis=-1).astype(BF16)
    probs = a2a(jnp.broadcast_to(probs[None], (SEQ,) + probs.shape)).reshape(HEADS, N, 4 * N)
    hid = mix(probs, v1, v2, x, wo)
    G = N // SEQ
    t = a2a(jnp.transpose(hid.reshape(S, SEQ, G, F), (1, 2, 0, 3)))
    hc = jnp.transpose(t, (1, 0, 2, 3)).reshape(G, SEQ * S, F)
    o = column(hc, vg, cq, ck, cv, co).reshape(G, SEQ, S, F)
    o = a2a(jnp.transpose(o, (1, 0, 2, 3)))
    return jnp.transpose(o, (2, 0, 1, 3)).reshape(S, N, F)


def solution(mesh):
    in_specs = (P("seq", "res", None),) + (P(),) * 10
    return jax.shard_map(shards, mesh=mesh, in_specs=in_specs, out_specs=P("seq", "res", None), check_vma=False)
```

profile of v0, /device:TPU:1, one launch (start us, length us, event | category | flops | bytes accessed | tf_op | source)
XLA Modules:
  0.0 208.6 jit_solution(10179587622169500747)
XLA Ops:
  0.0 3.6 %collective-permute-start.1 = (bf16[8,128,768]{2,1,0:T(8,128)(2,1)}, bf16[8,128,768]{2,1,0:T(8,128)(2,1)S(1)}, u32[]{:S(2)}, u32[]{:S(2)}) collective-permute-start(bf16[8,128,768]{2,1,0:T(8,128)(2,1)} %x.1), channel_id=1, source_target_pairs={{0,2},{1,3},{2,0},{3,1},{4,6},{5,7},{6,4},{7,5},{8,10},{9,11},{10,... | collective-permute-start | bytes 4718600 | tf_op jit(solution)/shard_map/ppermute | solution.py:192
  3.6 1.0 collective-permute-start
  4.5 32.9 %collective-permute-done.1.refs_0_.xa = bf16[8,128,768]{2,1,0:T(8,128)(2,1)S(1)} collective-permute-done((bf16[8,128,768]{2,1,0:T(8,128)(2,1)}, bf16[8,128,768]{2,1,0:T(8,128)(2,1)S(1)}, u32[]{:S(2)}, u32[]{:S(2)}) %collective-permute-start.1) | collective-permute-done | bytes 1572896 | tf_op jit(solution)/shard_map/ppermute | solution.py:192
  37.4 1.7 collective-permute-start.2
  39.1 1.3 reshape.68.refs_2_.g
  40.4 1.2 copy-done.2
  41.6 10.1 %logits.2 = (bf16[12,128,512]{2,1,0:T(8,128)(2,1)}, bf16[12,128,256]{2,1,0:T(8,128)(2,1)}) custom-call(bf16[8,128,768]{2,1,0:T(8,128)(2,1)} %x.1, bf16[8,128,768]{2,1,0:T(8,128)(2,1)} %copy-done.2, f32[1,768]{1,0:T(1,128)} %reshape.68.refs_2_.g, bf16[768,768]{1,0:T(8,128)(2,1)} %refs_3_.3, bf16[768,768]{1,0:T(8,128)(2,1)} %refs_4_.1), custom_call_target="tpu_custom_call" | custom-call | tf_op jit(solution)/shard_map/logits/pallas_call | solution.py:85
  51.7 9.3 %all-to-all-start = ((bf16[32,48,256]{2,1,0:T(8,128)(2,1)}), bf16[32,48,256]{2,1,0:T(8,128)(2,1)}, u32[]{:S(2)}, u32[]{:S(2)}) async-start(bf16[32,48,256]{2,1,0:T(8,128)(2,1)} %bitcast.22), calls=%async_computation | async-start | bytes 1572864 | tf_op jit(solution)/shard_map/all_to_all | solution.py:185
  61.0 1.1 copy-done.3
  62.1 8.8 %logits.3 = bf16[12,128,256]{2,1,0:T(8,128)(2,1)} custom-call(bf16[8,128,768]{2,1,0:T(8,128)(2,1)} %copy-done.1, bf16[8,128,768]{2,1,0:T(8,128)(2,1)} %copy-done.3, f32[1,768]{1,0:T(1,128)} %reshape.68.refs_2_.g, bf16[768,768]{1,0:T(8,128)(2,1)} %refs_3_.3, bf16[12,128,512]{2,1,0:T(8,128)(2,1)} %get-tuple-element.8.refs_4_), custom_call_target="tpu_custom_call" | custom-call | tf_op jit(solution)/shard_map/logits/pallas_call | solution.py:85
  70.9 2.9 %all-to-all-done = bf16[32,48,256]{2,1,0:T(8,128)(2,1)} async-done(((bf16[32,48,256]{2,1,0:T(8,128)(2,1)}), bf16[32,48,256]{2,1,0:T(8,128)(2,1)}, u32[]{:S(2)}, u32[]{:S(2)}) %all-to-all-start) | async-done | bytes 786464 | tf_op jit(solution)/shard_map/all_to_all | solution.py:185
  73.8 5.3 %all-to-all-start.1 = ((bf16[32,48,256]{2,1,0:T(8,128)(2,1)}), bf16[32,48,256]{2,1,0:T(8,128)(2,1)S(1)}, u32[]{:S(2)}, u32[]{:S(2)}) async-start(bf16[32,48,256]{2,1,0:T(8,128)(2,1)} %bitcast.21), calls=%async_computation.1 | async-start | bytes 1572864 | tf_op jit(solution)/shard_map/all_to_all | solution.py:185
  79.1 1.3 convert_reduce_fusion.1
  80.4 10.7 %all-to-all-done.1 = bf16[32,48,256]{2,1,0:T(8,128)(2,1)S(1)} async-done(((bf16[32,48,256]{2,1,0:T(8,128)(2,1)}), bf16[32,48,256]{2,1,0:T(8,128)(2,1)S(1)}, u32[]{:S(2)}, u32[]{:S(2)}) %all-to-all-start.1) | async-done | bytes 786464 | tf_op jit(solution)/shard_map/all_to_all | solution.py:185
  91.0 0.1 convert_reduce_fusion
  91.2 0.2 fusion
  91.6 1.4 broadcast_in_dim.2
  93.0 4.8 %all-to-all-start.2 = ((bf16[32,48,512]{2,1,0:T(8,128)(2,1)}), bf16[32,48,512]{2,1,0:T(8,128)(2,1)S(1)}, u32[]{:S(2)}, u32[]{:S(2)}) async-start(bf16[32,48,512]{2,1,0:T(8,128)(2,1)} %broadcast_in_dim.2), calls=%async_computation.2 | async-start | bytes 3145728 | tf_op jit(solution)/shard_map/all_to_all | solution.py:185
  97.8 7.5 %values.2.v1 = bf16[12,256,512]{2,1,0:T(8,128)(2,1)} custom-call(bf16[8,128,768]{2,1,0:T(8,128)(2,1)} %x.1, bf16[8,128,768]{2,1,0:T(8,128)(2,1)} %copy-done.2, f32[1,768]{1,0:T(1,128)} %reshape.68.refs_2_.g, bf16[768,768]{1,0:T(8,128)(2,1)} %wv.4), custom_call_target="tpu_custom_call" | custom-call | tf_op jit(solution)/shard_map/values/pallas_call | solution.py:109
  105.2 7.5 %values.3.v2 = bf16[12,256,512]{2,1,0:T(8,128)(2,1)} custom-call(bf16[8,128,768]{2,1,0:T(8,128)(2,1)} %copy-done.1, bf16[8,128,768]{2,1,0:T(8,128)(2,1)} %copy-done.3, f32[1,768]{1,0:T(1,128)} %reshape.68.refs_2_.g, bf16[768,768]{1,0:T(8,128)(2,1)} %wv.4), custom_call_target="tpu_custom_call" | custom-call | tf_op jit(solution)/shard_map/values/pallas_call | solution.py:109
  112.7 3.3 %all-to-all-done.2 = bf16[32,48,512]{2,1,0:T(8,128)(2,1)S(1)} async-done(((bf16[32,48,512]{2,1,0:T(8,128)(2,1)}), bf16[32,48,512]{2,1,0:T(8,128)(2,1)S(1)}, u32[]{:S(2)}, u32[]{:S(2)}) %all-to-all-start.2) | async-done | bytes 1572896 | tf_op jit(solution)/shard_map/all_to_all | solution.py:185
  116.0 1.1 copy-done
  117.1 9.2 %mix.1 = bf16[8,128,768]{2,1,0:T(8,128)(2,1)} custom-call(bf16[12,128,512]{2,1,0:T(8,128)(2,1)} %bitcast.19, bf16[12,256,512]{2,1,0:T(8,128)(2,1)} %values.2.v1, bf16[12,256,512]{2,1,0:T(8,128)(2,1)} %values.3.v2, bf16[8,128,768]{2,1,0:T(8,128)(2,1)} %x.1, bf16[768,768]{1,0:T(8,128)(2,1)} %wo.2), custom_call_target="tpu_custom_call" | custom-call | tf_op jit(solution)/shard_map/mix/pallas_call | solution.py:140
  126.3 3.4 %copy.18 = bf16[8,128,768]{2,0,1:T(8,128)(2,1)} copy(bf16[8,128,768]{2,1,0:T(8,128)(2,1)} %mix.1) | data formatting | bytes 3145728 | tf_op jit(solution)/shard_map/reshape | solution.py:210
  129.7 7.1 %all-to-all-start.3 = ((bf16[32,4,8,768]{3,2,1,0:T(8,128)(2,1)}), bf16[32,4,8,768]{3,2,1,0:T(8,128)(2,1)S(1)}, u32[]{:S(2)}, u32[]{:S(2)}) async-start(bf16[32,4,8,768]{3,2,1,0:T(8,128)(2,1)} %bitcast.4), calls=%async_computation.3 | async-start | bytes 3145728 | tf_op jit(solution)/shard_map/all_to_all | solution.py:185
  136.8 0.6 reshape.74.g
  137.4 17.4 %all-to-all-done.3 = bf16[32,4,8,768]{3,2,1,0:T(8,128)(2,1)S(1)} async-done(((bf16[32,4,8,768]{3,2,1,0:T(8,128)(2,1)}), bf16[32,4,8,768]{3,2,1,0:T(8,128)(2,1)S(1)}, u32[]{:S(2)}, u32[]{:S(2)}) %all-to-all-start.3) | async-done | bytes 1572896 | tf_op jit(solution)/shard_map/all_to_all | solution.py:185
  154.9 1.2 copy_bitcast_fusion.1.h_ref
  156.1 23.6 %column.1 = bf16[4,256,768]{2,1,0:T(8,128)(2,1)} custom-call(bf16[4,256,768]{2,1,0:T(8,128)(2,1)} %copy_bitcast_fusion.1.h_ref, f32[1,768]{1,0:T(1,128)} %reshape.74.g, bf16[768,768]{1,0:T(8,128)(2,1)} %wq.1, bf16[768,768]{1,0:T(8,128)(2,1)} %wk.1, bf16[768,768]{1,0:T(8,128)(2,1)} %wv.5, bf16[768,768]{1,0:T(8,128)(2,1)} %wo.3), custom_call_target="tpu_custom_call" | custom-call | tf_op jit(solution)/shard_map/column/pallas_call | solution.py:172
  179.7 1.6 copy_bitcast_fusion
  181.3 25.8 %all_to_all.25 = bf16[32,4,8,768]{3,2,1,0:T(8,128)(2,1)S(1)} all-to-all(bf16[32,4,8,768]{3,2,1,0:T(8,128)(2,1)S(1)} %copy_bitcast_fusion), channel_id=1, replica_groups=mesh['seq'=32,'res'=4] {'seq'}, dimensions={0} | all-to-all | bytes 3145728 | tf_op jit(solution)/shard_map/all_to_all | solution.py:185
  207.1 1.4 copy.17
  (11 shorter events, 0.2 us)
Async XLA Ops:
  0.0 37.4 %collective-permute-start.1 = (bf16[8,128,768]{2,1,0:T(8,128)(2,1)}, bf16[8,128,768]{2,1,0:T(8,128)(2,1)S(1)}, u32[]{:S(2)}, u32[]{:S(2)}) collective-permute-start(bf16[8,128,768]{2,1,0:T(8,128)(2,1)} %x.1), channel_id=1, source_target_pairs={{0,2},{1,3},{2,0},{3,1},{4,6},{5,7},{6,4},{7,5},{8,10},{9,11},{10,... | collective-permute-start | bytes 4718600 | tf_op jit(solution)/shard_map/ppermute | solution.py:192
  3.6 36.8 %collective-permute-start = (bf16[8,128,768]{2,1,0:T(8,128)(2,1)}, bf16[8,128,768]{2,1,0:T(8,128)(2,1)S(1)}, u32[]{:S(2)}, u32[]{:S(2)}) collective-permute-start(bf16[8,128,768]{2,1,0:T(8,128)(2,1)} %x.1), channel_id=1, source_target_pairs={{0,1},{1,0},{2,3},{3,2},{4,5},{5,4},{6,7},{7,6},{8,9},{9,8},{10,11... | collective-permute-start | bytes 4718600 | tf_op jit(solution)/shard_map/ppermute | solution.py:193
  37.4 14.2 %copy-start.1 = (bf16[8,128,768]{2,1,0:T(8,128)(2,1)}, bf16[8,128,768]{2,1,0:T(8,128)(2,1)S(1)}, u32[]{:S(2)}) copy-start(bf16[8,128,768]{2,1,0:T(8,128)(2,1)S(1)} %collective-permute-done.1.refs_0_.xa) | copy-start | bytes 4718596
  37.4 23.6 %collective-permute-start.2 = (bf16[8,128,768]{2,1,0:T(8,128)(2,1)S(1)}, bf16[8,128,768]{2,1,0:T(8,128)(2,1)S(1)}, u32[]{:S(2)}, u32[]{:S(2)}) collective-permute-start(bf16[8,128,768]{2,1,0:T(8,128)(2,1)S(1)} %collective-permute-done.1.refs_0_.xa), channel_id=1, source_target_pairs={{0,1},{1,0},{2,3},{3,2},{4,5},{5,4},{6,7},{7,6},{8,9},{9,8},{10,11... | collective-permute-start | bytes 4718600 | tf_op jit(solution)/shard_map/ppermute | solution.py:194
  40.4 1.2 copy-start.2
  51.7 22.1 %all-to-all-start = ((bf16[32,48,256]{2,1,0:T(8,128)(2,1)}), bf16[32,48,256]{2,1,0:T(8,128)(2,1)}, u32[]{:S(2)}, u32[]{:S(2)}) async-start(bf16[32,48,256]{2,1,0:T(8,128)(2,1)} %bitcast.22), calls=%async_computation | async-start | bytes 1572864 | tf_op jit(solution)/shard_map/all_to_all | solution.py:185
  61.0 1.2 copy-start.3
  73.8 17.2 %all-to-all-start.1 = ((bf16[32,48,256]{2,1,0:T(8,128)(2,1)}), bf16[32,48,256]{2,1,0:T(8,128)(2,1)S(1)}, u32[]{:S(2)}, u32[]{:S(2)}) async-start(bf16[32,48,256]{2,1,0:T(8,128)(2,1)} %bitcast.21), calls=%async_computation.1 | async-start | bytes 1572864 | tf_op jit(solution)/shard_map/all_to_all | solution.py:185
  93.0 23.0 %all-to-all-start.2 = ((bf16[32,48,512]{2,1,0:T(8,128)(2,1)}), bf16[32,48,512]{2,1,0:T(8,128)(2,1)S(1)}, u32[]{:S(2)}, u32[]{:S(2)}) async-start(bf16[32,48,512]{2,1,0:T(8,128)(2,1)} %broadcast_in_dim.2), calls=%async_computation.2 | async-start | bytes 3145728 | tf_op jit(solution)/shard_map/all_to_all | solution.py:185
  116.0 1.1 copy-start
  129.7 7.1 %copy-start.4 = (f32[768]{0:T(1024)S(1)}, f32[768]{0:T(1024)}, u32[]{:S(2)}) copy-start(f32[768]{0:T(1024)} %param.17) | copy-start | bytes 9220
  129.7 25.1 %all-to-all-start.3 = ((bf16[32,4,8,768]{3,2,1,0:T(8,128)(2,1)}), bf16[32,4,8,768]{3,2,1,0:T(8,128)(2,1)S(1)}, u32[]{:S(2)}, u32[]{:S(2)}) async-start(bf16[32,4,8,768]{3,2,1,0:T(8,128)(2,1)} %bitcast.4), calls=%async_computation.3 | async-start | bytes 3145728 | tf_op jit(solution)/shard_map/all_to_all | solution.py:185
where the time goes:
time: 212 us; the launch traced here: 209 us
  waiting for transfers between devices  67.1 us (32%)
  Pallas kernels  66.6 us (31%)
  starting transfers between devices  32.7 us (15%)
  blocking collectives  25.8 us (12%)
  local copies, waits for them, and re-layouts  14.4 us (7%)
    all_to_all x4, waiting for transfers between devices, a2a(): return lax.all_to_all(x, 'seq', split_axis=0, concat_axis=0, tiled=True)  34.2 us
    ppermute x1, waiting for transfers between devices, shards(): xh = lax.ppermute(x, 'res', XHI_SWAP)  32.9 us
    all_to_all x4, starting transfers between devices, a2a(): return lax.all_to_all(x, 'seq', split_axis=0, concat_axis=0, tiled=True)  26.5 us
    all_to_all x1, blocking collectives, a2a(): return lax.all_to_all(x, 'seq', split_axis=0, concat_axis=0, tiled=True)  25.8 us
    pallas_call x1, Pallas kernels, column(): pl.pallas_call(column_kernel, grid=(c,), in_specs=[xs, whole(g.shape)] +...  23.6 us
    pallas_call x2, Pallas kernels, logits(): pl.pallas_call(functools.partial(logits_kernel, first), grid=(s // 2,), i...  18.9 us
    pallas_call x2, Pallas kernels, values(): pl.pallas_call(values_kernel, grid=(s // 2,), in_specs=[xs, xs, whole(g.s...  14.9 us
    pallas_call x1, Pallas kernels, mix(): pl.pallas_call(mix_kernel, grid=(HEADS // 2,), in_specs=[pl.BlockSpec((2,...  9.22 us
  transfers between devices with their start and end apart: 7, of which 5 were waited for; matrix products, arithmetic and copies ran while one was open for 2% of the time, Pallas kernels for 16%

commit v1 on v0

v1 whole, which is shorter than its diff:
```python
import functools
import math

import jax
import jax.numpy as jnp
from jax import lax
from jax.experimental import pallas as pl
from jax.experimental.pallas import tpu as pltpu
from jax.sharding import PartitionSpec as P

HEADS = 12
D = 64
SEQ = 32
CORE_SWAP = [(0, 1), (1, 0), (2, 3), (3, 2)]
XHI_SWAP = [(0, 2), (1, 3), (2, 0), (3, 1)]
F32 = jnp.float32
BF16 = jnp.bfloat16
PARAMS = pltpu.CompilerParams(vmem_limit_bytes=56 * 1024 * 1024)


def norm(x, gain):
    v = x.astype(F32)
    c = v - jnp.mean(v, axis=-1, keepdims=True)
    var = jnp.mean(c * c, axis=-1, keepdims=True)
    return (c * lax.rsqrt(var + 1e-05) * gain).astype(BF16)


def mm(a, b):
    return lax.dot_general(a, b, (((1,), (0,)), ((), ())), preferred_element_type=F32)


def mm_t(a, b):
    return lax.dot_general(a, b, (((1,), (1,)), ((), ())), preferred_element_type=F32)


def head(x, h):
    return x[:, h * D : (h + 1) * D]


def whole(shape):
    return pl.BlockSpec(shape, lambda *_: (0,) * len(shape))


def pair(y, n, h):
    return jnp.concatenate([head(y[:n], h), head(y[n:], h)], axis=1)


def logits_kernel(first, *refs):
    if first:
        xa, xb, g, wk, wq, q, out, ks = refs
    else:
        xa, xb, g, wk, q, out, ks = refs
    t = pl.program_id(0)
    n, f = xa.shape[1:]
    lane = pl.multiple_of(t * 2 * D, 2 * D)
    na = norm(xa[...].reshape(2 * n, f), g[...])
    nb = norm(xb[...].reshape(2 * n, f), g[...])
    ka = mm(na, wk[...]).astype(BF16)
    kb = mm(nb, wk[...]).astype(BF16)
    for h in range(HEADS):
        ks[h, 0:n, pl.ds(lane, 2 * D)] = pair(ka, n, h)
        ks[h, n : 2 * n, pl.ds(lane, 2 * D)] = pair(kb, n, h)
    if first:
        qq = mm(na, wq[...]).astype(BF16)
        for h in range(HEADS):
            q[h, :, pl.ds(lane, 2 * D)] = pair(qq, n, h)

    @pl.when(t == pl.num_programs(0) - 1)
    def _():
        for h in range(HEADS):
            out[h] = mm_t(q[h], ks[h]).astype(BF16)


def logits(xa, xb, g, wk, wq=None, q=None):
    s, n, f = xa.shape
    first = q is None
    m = n if first else q.shape[1]
    xs = pl.BlockSpec((2, n, f), lambda t: (t, 0, 0))
    in_specs = [xs, xs, whole(g.shape), whole(wk.shape)]
    qshape = (HEADS, m, s * D)
    lshape = (HEADS, m, 2 * n)
    in_specs += [whole(wq.shape)] if first else [whole(qshape)]
    ospecs = [whole(qshape), whole(lshape)] if first else [whole(lshape)]
    oshape = [jax.ShapeDtypeStruct(qshape, BF16), jax.ShapeDtypeStruct(lshape, BF16)]
    return pl.pallas_call(
        functools.partial(logits_kernel, first),
        grid=(s // 2,),
        in_specs=in_specs,
        out_specs=ospecs,
        out_shape=oshape if first else oshape[1:],
        scratch_shapes=[pltpu.VMEM((HEADS, 2 * n, s * D), BF16)],
        compiler_params=PARAMS,
        name="logits",
    )(xa, xb, g, wk, wq if first else q)


def values_kernel(*refs):
    xs, (g, wv, out) = refs[:-3], refs[-3:]
    at = 0
    for x in xs:
        n, f = x.shape[1:]
        v = mm(norm(x[...].reshape(2 * n, f), g[...]), wv[...]).astype(BF16)
        for h in range(HEADS):
            out[h, at : at + n] = pair(v, n, h)
        at += n


def values(pieces, g, wv):
    s, _, f = pieces[0].shape
    total = sum(p.shape[1] for p in pieces)
    specs = [pl.BlockSpec((2, p.shape[1], f), lambda t: (t, 0, 0)) for p in pieces]
    return pl.pallas_call(
        values_kernel,
        grid=(s // 2,),
        in_specs=specs + [whole(g.shape), whole(wv.shape)],
        out_specs=pl.BlockSpec((HEADS, total, 2 * D), lambda t: (0, 0, t)),
        out_shape=jax.ShapeDtypeStruct((HEADS, total, s * D), BF16),
        compiler_params=PARAMS,
        name="values",
    )(*pieces, g, wv)


def mix_kernel(p, v, x, wo, out, ms):
    t = pl.program_id(0)
    s = x.shape[0]
    lane = pl.multiple_of(t * 2 * D, 2 * D)
    o = [mm(p[h], v[h]).astype(BF16) for h in range(2)]
    for r in range(s):
        ms[r, :, pl.ds(lane, 2 * D)] = jnp.concatenate([head(o[0], r), head(o[1], r)], axis=1)

    @pl.when(t == pl.num_programs(0) - 1)
    def _():
        for r in range(s):
            out[r] = (x[r].astype(F32) + mm(ms[r], wo[...])).astype(BF16)


def mix(p, v, x, wo):
    s, n, f = x.shape
    return pl.pallas_call(
        mix_kernel,
        grid=(HEADS // 2,),
        in_specs=[
            pl.BlockSpec((2,) + p.shape[1:], lambda t: (t, 0, 0)),
            pl.BlockSpec((2,) + v.shape[1:], lambda t: (t, 0, 0)),
            whole(x.shape),
            whole(wo.shape),
        ],
        out_specs=whole(x.shape),
        out_shape=jax.ShapeDtypeStruct(x.shape, BF16),
        scratch_shapes=[pltpu.VMEM((s, n, f), BF16)],
        compiler_params=PARAMS,
        name="mix",
    )(p, v, x, wo)


def column_kernel(h_ref, g, wq, wk, wv, wo, out, xs, ns, qs, ks, vs, ms):
    src, rows, f = h_ref.shape
    a = src * 8
    for i in range(0, rows, 16):
        y = h_ref[:, i : i + 16].astype(F32)
        for j in range(2):
            xs[pl.ds((i // 8 + j) * a, a)] = y[:, 8 * j : 8 * j + 8].reshape(a, f)

    def project(p, carry):
        r = pl.ds(pl.multiple_of(p * a, a), a)
        n = norm(xs[r], g[...])
        qs[r] = (mm(n, wq[...]) * (1.0 / (math.sqrt(D) * math.log(2.0)))).astype(BF16)
        ks[r] = mm(n, wk[...]).astype(BF16)
        vs[r] = mm(n, wv[...]).astype(BF16)
        return carry

    def attend(p, carry):
        r = pl.ds(pl.multiple_of(p * a, a), a)
        low = lax.broadcasted_iota(jnp.int32, (a, 2 * D), 1) < D
        zero = jnp.zeros((a, 2 * D), BF16)
        ones = jnp.ones((a, 2 * D), BF16)
        for hp in range(HEADS // 2):
            c = slice(hp * 2 * D, (hp + 1) * 2 * D)
            q, k = qs[r, c], ks[r, c]
            v = jnp.concatenate([vs[r, c], ones], axis=1)
            o = []
            for kh in (jnp.where(low, k, zero), jnp.where(low, zero, k)):
                l = mm_t(q, kh)
                e = jnp.exp2(l - jnp.max(l, axis=-1, keepdims=True)).astype(BF16)
                w = mm(e, v)
                o.append(w[:, : 2 * D] / w[:, 2 * D :])
            ms[r, c] = jnp.where(low, o[0], o[1]).astype(BF16)
        return carry

    def emit(p, carry):
        r = pl.ds(pl.multiple_of(p * a, a), a)
        xs[r] = xs[r] + mm(ms[r], wo[...])
        return carry

    lax.fori_loop(0, rows // 8, project, 0)
    lax.fori_loop(0, rows // 8, attend, 0)
    lax.fori_loop(0, rows // 8, emit, 0)
    for i in range(0, rows, 16):
        y = [xs[pl.ds((i // 8 + j) * a, a)].reshape(src, 8, f) for j in range(2)]
        out[:, i : i + 16] = jnp.concatenate(y, axis=1).astype(BF16)


def column(hc, g, wq, wk, wv, wo):
    src, rows, f = hc.shape
    m = src * rows
    return pl.pallas_call(
        column_kernel,
        out_shape=jax.ShapeDtypeStruct(hc.shape, BF16),
        scratch_shapes=[pltpu.VMEM((m, f), F32)] + [pltpu.VMEM((m, f), BF16)] * 5,
        compiler_params=PARAMS,
        name="column",
    )(hc, g, wq, wk, wv, wo)


def a2a(x):
    return lax.all_to_all(x, "seq", split_axis=0, concat_axis=0, tiled=True)


def shards(x, hg, wq, wk, wv, wo, vg, cq, ck, cv, co):
    S, N, F = x.shape
    hg = hg.reshape(1, F)
    vg = vg.reshape(1, F)
    barrier = lax.optimization_barrier

    def reduce(l):
        return a2a(l.reshape(SEQ, HEADS * N // SEQ, l.shape[-1]))

    xh = lax.ppermute(x, "res", XHI_SWAP)
    sib = lax.ppermute(x, "res", CORE_SWAP)
    q, l1 = logits(x, sib, hg, wk, wq=wq)
    r1 = jnp.sum(reduce(l1).astype(F32), axis=0)
    xh, r1 = barrier((xh, r1))
    xhs = lax.ppermute(xh, "res", CORE_SWAP)
    (l2,) = logits(xh, xhs, hg, wk, q=q)
    r2 = jnp.sum(reduce(l2).astype(F32), axis=0)
    x_late, l2 = barrier((x, l2))
    v = values((x_late, sib, xh, xhs), hg, wv)
    scale = 1.0 / (math.sqrt(D) * math.sqrt(S * SEQ))
    tied = jnp.concatenate([r1, r2], axis=-1) * scale
    probs = jax.nn.softmax(tied, axis=-1).astype(BF16)
    probs = a2a(jnp.broadcast_to(probs[None], (SEQ,) + probs.shape)).reshape(HEADS, N, 4 * N)
    hid = mix(probs, v, x, wo)
    G = N // SEQ
    t = jnp.transpose(hid.reshape(S, SEQ, G, F), (1, 2, 0, 3)).reshape(SEQ, G * S, F)
    o = a2a(column(a2a(t), vg, cq, ck, cv, co))
    return jnp.transpose(o.reshape(SEQ, G, S, F), (2, 0, 1, 3)).reshape(S, N, F)


def solution(mesh):
    in_specs = (P("seq", "res", None),) + (P(),) * 10
    return jax.shard_map(shards, mesh=mesh, in_specs=in_specs, out_specs=P("seq", "res", None), check_vma=False)
```

time: 212 us -> 199 us (0.939)
  blocking collectives: 25.8 us -> 79.3 us
  waiting for transfers between devices: 67.1 us -> 29.8 us
  starting transfers between devices: 32.7 us -> 18.3 us
  Pallas kernels: 66.6 us -> 54.8 us
    all_to_all x1 -> x3, blocking collectives: 25.8 us -> 79.3 us  [a2a(): return lax.all_to_all(x, 'seq', split_axis=0, concat_axis=0, tiled=True)]
    ppermute x1, waiting for transfers between devices: 32.9 us -> 0.01 us  [shards(): xh = lax.ppermute(x, 'res', XHI_SWAP)]
    all_to_all x4 -> x2, starting transfers between devices: 26.5 us -> 12.5 us  [a2a(): return lax.all_to_all(x, 'seq', split_axis=0, concat_axis=0, tiled=True)]
    pallas_call x3 -> x2, Pallas kernels: 38.5 us -> 26.8 us  [the longest x1 16.1 us: column(): pl.pallas_call(column_kernel, out_shape=jax.ShapeDtypeStruct(hc.shape, BF...]
    all_to_all x4 -> x2, waiting for transfers between devices: 34.2 us -> 26.8 us  [a2a(): return lax.all_to_all(x, 'seq', split_axis=0, concat_axis=0, tiled=True)]
    ppermute x1, waiting for transfers between devices: 0.01 us -> 3.04 us  [shards(): xhs = lax.ppermute(xh, 'res', CORE_SWAP)]
    reshape x3 -> x2, local copies, waits for them, and re-layouts: 6.09 us -> 4.85 us  [the longest x1 3.41 us: shards(): hid.reshape(S, SEQ, G, F)]
    unnamed x10 -> x12, local copies, waits for them, and re-layouts: 3.45 us -> 4.67 us
  transfers between devices with their start and end apart: 7 -> 5, of which waited for: 5 -> 3; matrix products, arithmetic and copies ran while one was open for 2% -> 1% of each run, Pallas kernels for 16% -> 11%
where the time goes in v1:
time: 199 us; the launch traced here: 196 us
  blocking collectives  79.3 us (40%)
  Pallas kernels  54.8 us (28%)
  waiting for transfers between devices  29.8 us (15%)
  starting transfers between devices  18.3 us (9%)
  local copies, waits for them, and re-layouts  12.7 us (6%)
    all_to_all x3, blocking collectives, a2a(): return lax.all_to_all(x, 'seq', split_axis=0, concat_axis=0, tiled=True)  79.3 us
    all_to_all x2, waiting for transfers between devices, a2a(): return lax.all_to_all(x, 'seq', split_axis=0, concat_axis=0, tiled=True)  26.8 us
    pallas_call x2, Pallas kernels, logits(): pl.pallas_call(functools.partial(logits_kernel, first), grid=(s // 2,), i...  18.9 us
    pallas_call x1, Pallas kernels, column(): pl.pallas_call(column_kernel, out_shape=jax.ShapeDtypeStruct(hc.shape, BF...  16.1 us
    all_to_all x2, starting transfers between devices, a2a(): return lax.all_to_all(x, 'seq', split_axis=0, concat_axis=0, tiled=True)  12.5 us
    pallas_call x1, Pallas kernels, values(): pl.pallas_call(values_kernel, grid=(s // 2,), in_specs=specs + [whole(g.s...  10.7 us
    pallas_call x1, Pallas kernels, mix(): pl.pallas_call(mix_kernel, grid=(HEADS // 2,), in_specs=[pl.BlockSpec((2,...  9.1 us
    unnamed x12, local copies, waits for them, and re-layouts  4.67 us
  transfers between devices with their start and end apart: 5, of which 3 were waited for; matrix products, arithmetic and copies ran while one was open for 1% of the time, Pallas kernels for 11%

profile of v1, /device:TPU:1, one launch (start us, length us, event | category | flops | bytes accessed | tf_op | source)
XLA Modules:
  0.0 195.7 jit_solution(14300224882047992059)
XLA Ops:
  0.0 1.4 collective-permute-start.1
  1.4 2.8 %collective-permute-start = (bf16[8,128,768]{2,1,0:T(8,128)(2,1)}, bf16[8,128,768]{2,1,0:T(8,128)(2,1)S(1)}, u32[]{:S(2)}, u32[]{:S(2)}) collective-permute-start(bf16[8,128,768]{2,1,0:T(8,128)(2,1)} %x.1), channel_id=1, source_target_pairs={{0,2},{1,3},{2,0},{3,1},{4,6},{5,7},{6,4},{7,5},{8,10},{9,11},{10,... | collective-permute-start | bytes 4718600 | tf_op jit(solution)/shard_map/ppermute | solution.py:228
  4.2 1.3 reshape.68.refs_2_.refs_4_
  5.5 0.0 collective-permute-done.1.refs_1_
  5.5 1.1 copy-done
  6.7 10.1 %logits.2 = (bf16[12,128,512]{2,1,0:T(8,128)(2,1)}, bf16[12,128,256]{2,1,0:T(8,128)(2,1)}) custom-call(bf16[8,128,768]{2,1,0:T(8,128)(2,1)} %x.1, bf16[8,128,768]{2,1,0:T(8,128)(2,1)} %copy-done, f32[1,768]{1,0:T(1,128)} %reshape.68.refs_2_.refs_4_, bf16[768,768]{1,0:T(8,128)(2,1)} %refs_3_.3, bf16[768,768]{1,0:T(8,128)(2,1)} %refs_4_.1), custom_call_target="tpu_custom_call" | custom-call | tf_op jit(solution)/shard_map/logits/pallas_call | solution.py:85
  16.8 34.7 %all_to_all.25 = bf16[32,48,256]{2,1,0:T(8,128)(2,1)S(1)} all-to-all(bf16[32,48,256]{2,1,0:T(8,128)(2,1)} %bitcast.16), channel_id=1, replica_groups=mesh['seq'=32,'res'=4] {'seq'}, dimensions={0} | all-to-all | bytes 1572864 | tf_op jit(solution)/shard_map/all_to_all | solution.py:216
  51.5 0.1 convert_reduce_fusion.1
  51.6 0.0 copy-start.1
  51.6 1.5 collective-permute-start.2
  53.1 3.0 %collective-permute-done.2.refs_1_.refs_3_ = bf16[8,128,768]{2,1,0:T(8,128)(2,1)S(1)} collective-permute-done((bf16[8,128,768]{2,1,0:T(8,128)(2,1)S(1)}, bf16[8,128,768]{2,1,0:T(8,128)(2,1)S(1)}, u32[]{:S(2)}, u32[]{:S(2)}) %collective-permute-start.2) | collective-permute-done | bytes 1572896 | tf_op jit(solution)/shard_map/ppermute | solution.py:233
  56.2 1.2 copy-done.2
  57.4 8.8 %logits.3 = bf16[12,128,256]{2,1,0:T(8,128)(2,1)} custom-call(bf16[8,128,768]{2,1,0:T(8,128)(2,1)} %copy-done.1, bf16[8,128,768]{2,1,0:T(8,128)(2,1)} %copy-done.2, f32[1,768]{1,0:T(1,128)} %reshape.68.refs_2_.refs_4_, bf16[768,768]{1,0:T(8,128)(2,1)} %refs_3_.3, bf16[12,128,512]{2,1,0:T(8,128)(2,1)} %get-tuple-element.13.refs_4_), custom_call_target="tpu_custom_call" | custom-call | tf_op jit(solution)/shard_map/logits/pallas_call | solution.py:85
  66.2 17.5 %all_to_all.26 = bf16[32,48,256]{2,1,0:T(8,128)(2,1)S(1)} all-to-all(bf16[32,48,256]{2,1,0:T(8,128)(2,1)} %bitcast.15), channel_id=1, replica_groups=mesh['seq'=32,'res'=4] {'seq'}, dimensions={0} | all-to-all | bytes 1572864 | tf_op jit(solution)/shard_map/all_to_all | solution.py:216
  83.7 0.1 convert_reduce_fusion
  83.8 0.1 fusion.1
  83.9 0.2 fusion
  84.1 0.1 divide_convert_fusion
  84.2 1.4 broadcast_in_dim.2
  85.6 5.3 %all-to-all-start.2 = ((bf16[32,48,512]{2,1,0:T(8,128)(2,1)}), bf16[32,48,512]{2,1,0:T(8,128)(2,1)S(1)}, u32[]{:S(2)}, u32[]{:S(2)}) async-start(bf16[32,48,512]{2,1,0:T(8,128)(2,1)} %broadcast_in_dim.2), calls=%async_computation.2 | async-start | bytes 3145728 | tf_op jit(solution)/shard_map/all_to_all | solution.py:216
  90.9 10.7 %values.1.v = bf16[12,512,512]{2,1,0:T(8,128)(2,1)} custom-call(bf16[8,128,768]{2,1,0:T(8,128)(2,1)} %x.1, bf16[8,128,768]{2,1,0:T(8,128)(2,1)} %copy-done, bf16[8,128,768]{2,1,0:T(8,128)(2,1)} %copy-done.1, bf16[8,128,768]{2,1,0:T(8,128)(2,1)} %copy-done.2, f32[1,768]{1,0:T(1,128)} %reshape.68.refs_2_.refs_4_, bf16[768,768]{1,0:T(8,128)(2,1)} %refs_5_.1), custom_call_target="tpu_custom_call" | custom-call | tf_op jit(solution)/shard_map/values/pallas_call | solution.py:112
  101.6 8.5 %all-to-all-done.2 = bf16[32,48,512]{2,1,0:T(8,128)(2,1)S(1)} async-done(((bf16[32,48,512]{2,1,0:T(8,128)(2,1)}), bf16[32,48,512]{2,1,0:T(8,128)(2,1)S(1)}, u32[]{:S(2)}, u32[]{:S(2)}) %all-to-all-start.2) | async-done | bytes 1572896 | tf_op jit(solution)/shard_map/all_to_all | solution.py:216
  110.1 1.1 copy-done.3
  111.2 9.1 %mix.1 = bf16[8,128,768]{2,1,0:T(8,128)(2,1)} custom-call(bf16[12,128,512]{2,1,0:T(8,128)(2,1)} %bitcast.13, bf16[12,512,512]{2,1,0:T(8,128)(2,1)} %values.1.v, bf16[8,128,768]{2,1,0:T(8,128)(2,1)} %x.1, bf16[768,768]{1,0:T(8,128)(2,1)} %wo.2), custom_call_target="tpu_custom_call" | custom-call | tf_op jit(solution)/shard_map/mix/pallas_call | solution.py:139
  120.3 3.4 %copy.14 = bf16[8,128,768]{2,0,1:T(8,128)(2,1)} copy(bf16[8,128,768]{2,1,0:T(8,128)(2,1)} %mix.1) | data formatting | bytes 3145728 | tf_op jit(solution)/shard_map/reshape | solution.py:244
  123.7 7.2 %all-to-all-start.3 = ((bf16[32,32,768]{2,1,0:T(8,128)(2,1)}), bf16[32,32,768]{2,1,0:T(8,128)(2,1)S(1)}, u32[]{:S(2)}, u32[]{:S(2)}) async-start(bf16[32,32,768]{2,1,0:T(8,128)(2,1)} %bitcast.5), calls=%async_computation.3 | async-start | bytes 3145728 | tf_op jit(solution)/shard_map/all_to_all | solution.py:216
  131.0 0.6 reshape.74.g
  131.6 18.3 %all-to-all-done.3.h_ref = bf16[32,32,768]{2,1,0:T(8,128)(2,1)S(1)} async-done(((bf16[32,32,768]{2,1,0:T(8,128)(2,1)}), bf16[32,32,768]{2,1,0:T(8,128)(2,1)S(1)}, u32[]{:S(2)}, u32[]{:S(2)}) %all-to-all-start.3) | async-done | bytes 1572896 | tf_op jit(solution)/shard_map/all_to_all | solution.py:216
  149.9 1.1 copy-done.4
  151.0 16.1 %column.1 = bf16[32,32,768]{2,1,0:T(8,128)(2,1)} custom-call(bf16[32,32,768]{2,1,0:T(8,128)(2,1)} %copy-done.4, f32[1,768]{1,0:T(1,128)} %reshape.74.g, bf16[768,768]{1,0:T(8,128)(2,1)} %wq.1, bf16[768,768]{1,0:T(8,128)(2,1)} %wk.1, bf16[768,768]{1,0:T(8,128)(2,1)} %wv.1, bf16[768,768]{1,0:T(8,128)(2,1)} %wo.3), custom_call_target="tpu_custom_call" | custom-call | tf_op jit(solution)/shard_map/column/pallas_call | solution.py:206
  167.2 27.1 %all_to_all.27 = bf16[32,32,768]{2,1,0:T(8,128)(2,1)S(1)} all-to-all(bf16[32,32,768]{2,1,0:T(8,128)(2,1)} %column.1), channel_id=1, replica_groups=mesh['seq'=32,'res'=4] {'seq'}, dimensions={0} | all-to-all | bytes 3145728 | tf_op jit(solution)/shard_map/all_to_all | solution.py:216
  194.3 1.4 copy.15
  (8 shorter events, 0.0 us)
Async XLA Ops:
  0.0 5.5 %collective-permute-start.1 = (bf16[8,128,768]{2,1,0:T(8,128)(2,1)}, bf16[8,128,768]{2,1,0:T(8,128)(2,1)S(1)}, u32[]{:S(2)}, u32[]{:S(2)}) collective-permute-start(bf16[8,128,768]{2,1,0:T(8,128)(2,1)} %x.1), channel_id=1, source_target_pairs={{0,1},{1,0},{2,3},{3,2},{4,5},{5,4},{6,7},{7,6},{8,9},{9,8},{10,11... | collective-permute-start | bytes 4718600 | tf_op jit(solution)/shard_map/ppermute | solution.py:229
  1.4 50.2 %collective-permute-start = (bf16[8,128,768]{2,1,0:T(8,128)(2,1)}, bf16[8,128,768]{2,1,0:T(8,128)(2,1)S(1)}, u32[]{:S(2)}, u32[]{:S(2)}) collective-permute-start(bf16[8,128,768]{2,1,0:T(8,128)(2,1)} %x.1), channel_id=1, source_target_pairs={{0,2},{1,3},{2,0},{3,1},{4,6},{5,7},{6,4},{7,5},{8,10},{9,11},{10,... | collective-permute-start | bytes 4718600 | tf_op jit(solution)/shard_map/ppermute | solution.py:228
  5.5 1.1 copy-start
  51.6 4.6 %copy-start.1 = (bf16[8,128,768]{2,1,0:T(8,128)(2,1)}, bf16[8,128,768]{2,1,0:T(8,128)(2,1)S(1)}, u32[]{:S(2)}) copy-start(bf16[8,128,768]{2,1,0:T(8,128)(2,1)S(1)} %collective-permute-done.refs_0_.refs_2_) | copy-start | bytes 4718596
  51.6 4.6 %collective-permute-start.2 = (bf16[8,128,768]{2,1,0:T(8,128)(2,1)S(1)}, bf16[8,128,768]{2,1,0:T(8,128)(2,1)S(1)}, u32[]{:S(2)}, u32[]{:S(2)}) collective-permute-start(bf16[8,128,768]{2,1,0:T(8,128)(2,1)S(1)} %collective-permute-done.refs_0_.refs_2_), channel_id=1, source_target_pairs={{0,1},{1,0},{2,3},{3,2},{4,5},{5,4},{6,7},{7,6},{8,9},{9,8},{10,11... | collective-permute-start | bytes 4718600 | tf_op jit(solution)/shard_map/ppermute | solution.py:233
  56.2 1.2 copy-start.2
  85.6 24.5 %all-to-all-start.2 = ((bf16[32,48,512]{2,1,0:T(8,128)(2,1)}), bf16[32,48,512]{2,1,0:T(8,128)(2,1)S(1)}, u32[]{:S(2)}, u32[]{:S(2)}) async-start(bf16[32,48,512]{2,1,0:T(8,128)(2,1)} %broadcast_in_dim.2), calls=%async_computation.2 | async-start | bytes 3145728 | tf_op jit(solution)/shard_map/all_to_all | solution.py:216
  110.1 1.1 copy-start.3
  123.7 7.2 %copy-start.5 = (f32[768]{0:T(1024)S(1)}, f32[768]{0:T(1024)}, u32[]{:S(2)}) copy-start(f32[768]{0:T(1024)} %param.17) | copy-start | bytes 9220
  123.7 26.2 %all-to-all-start.3 = ((bf16[32,32,768]{2,1,0:T(8,128)(2,1)}), bf16[32,32,768]{2,1,0:T(8,128)(2,1)S(1)}, u32[]{:S(2)}, u32[]{:S(2)}) async-start(bf16[32,32,768]{2,1,0:T(8,128)(2,1)} %bitcast.5), calls=%async_computation.3 | async-start | bytes 3145728 | tf_op jit(solution)/shard_map/all_to_all | solution.py:216
  149.9 1.1 copy-start.4

commit v2 on v1

--- a/solution.py
+++ b/solution.py
@@ -15,7 +15,7 @@
 XHI_SWAP = [(0, 2), (1, 3), (2, 0), (3, 1)]
 F32 = jnp.float32
 BF16 = jnp.bfloat16
-PARAMS = pltpu.CompilerParams(vmem_limit_bytes=56 * 1024 * 1024)
+PARAMS = pltpu.CompilerParams(vmem_limit_bytes=40 * 1024 * 1024)
 
 
 def norm(x, gain):
@@ -35,6 +35,14 @@
 
 def head(x, h):
     return x[:, h * D : (h + 1) * D]
+
+
+def near(*arrays):
+    return [pltpu.with_memory_space_constraint(a, pltpu.VMEM) for a in arrays]
+
+
+def far(*arrays):
+    return [pltpu.with_memory_space_constraint(a, pltpu.HBM) for a in arrays]
 
 
 def whole(shape):
@@ -91,7 +99,7 @@
         scratch_shapes=[pltpu.VMEM((HEADS, 2 * n, s * D), BF16)],
         compiler_params=PARAMS,
         name="logits",
-    )(xa, xb, g, wk, wq if first else q)
+    )(*(far(xa, xb) if first else near(xa, xb)), *far(g, wk, wq if first else q))
 
 
 def values_kernel(*refs):
@@ -117,7 +125,7 @@
         out_shape=jax.ShapeDtypeStruct((HEADS, total, s * D), BF16),
         compiler_params=PARAMS,
         name="values",
-    )(*pieces, g, wv)
+    )(*far(*pieces, g, wv))
 
 
 def mix_kernel(p, v, x, wo, out, ms):
@@ -150,7 +158,7 @@
         scratch_shapes=[pltpu.VMEM((s, n, f), BF16)],
         compiler_params=PARAMS,
         name="mix",
-    )(p, v, x, wo)
+    )(*near(p), *far(v, x, wo))
 
 
 def column_kernel(h_ref, g, wq, wk, wv, wo, out, xs, ns, qs, ks, vs, ms):
@@ -209,7 +217,7 @@
         scratch_shapes=[pltpu.VMEM((m, f), F32)] + [pltpu.VMEM((m, f), BF16)] * 5,
         compiler_params=PARAMS,
         name="column",
-    )(hc, g, wq, wk, wv, wo)
+    )(*near(hc), *far(g, wq, wk, wv, wo))
 
 
 def a2a(x):
@@ -227,16 +235,29 @@
 
     xh = lax.ppermute(x, "res", XHI_SWAP)
     sib = lax.ppermute(x, "res", CORE_SWAP)
+
+    def reduce_yz(l):
+        half = SEQ // 2
+        l = l.reshape(2, half, HEADS * N // SEQ, l.shape[-1]).transpose(1, 0, 2, 3)
+        groups = [list(range(half)), list(range(half, SEQ))]
+        l = lax.all_to_all(l, "seq", split_axis=0, concat_axis=0, tiled=True, axis_index_groups=groups)
+        l = jnp.sum(l.astype(F32), axis=0)
+        me = lax.axis_index("seq") // half
+        other = lax.dynamic_index_in_dim(l, 1 - me, 0, keepdims=False).astype(BF16)
+        mine = lax.dynamic_index_in_dim(l, me, 0, keepdims=False)
+        return mine, lax.ppermute(other, "seq", [(i, (i + half) % SEQ) for i in range(SEQ)])
+
     q, l1 = logits(x, sib, hg, wk, wq=wq)
-    r1 = jnp.sum(reduce(l1).astype(F32), axis=0)
-    xh, r1 = barrier((xh, r1))
+    r1 = reduce_yz(l1)
+    xh, mine = barrier((xh, r1[0]))
     xhs = lax.ppermute(xh, "res", CORE_SWAP)
     (l2,) = logits(xh, xhs, hg, wk, q=q)
+    l2, theirs = barrier((l2, r1[1]))
     r2 = jnp.sum(reduce(l2).astype(F32), axis=0)
     x_late, l2 = barrier((x, l2))
     v = values((x_late, sib, xh, xhs), hg, wv)
     scale = 1.0 / (math.sqrt(D) * math.sqrt(S * SEQ))
-    tied = jnp.concatenate([r1, r2], axis=-1) * scale
+    tied = jnp.concatenate([mine + theirs.astype(F32), r2], axis=-1) * scale
     probs = jax.nn.softmax(tied, axis=-1).astype(BF16)
     probs = a2a(jnp.broadcast_to(probs[None], (SEQ,) + probs.shape)).reshape(HEADS, N, 4 * N)
     hid = mix(probs, v, x, wo)

time: 199 us -> 181 us (0.910)
  blocking collectives: 79.3 us -> 26.9 us
  waiting for transfers between devices: 29.8 us -> 53 us
  starting transfers between devices: 18.3 us -> 34.8 us
  Pallas kernels: 54.8 us -> 49.6 us
    all_to_all x3 -> x1, blocking collectives: 79.3 us -> 26.9 us  [a2a(): return lax.all_to_all(x, 'seq', split_axis=0, concat_axis=0, tiled=True)]
    all_to_all x0 -> x1, waiting for transfers between devices: none -> 12.7 us  [reduce_yz(): lax.all_to_all(l, 'seq', split_axis=0, concat_axis=0, tiled=True, axis_in...]
    all_to_all x2 -> x3, waiting for transfers between devices: 26.8 us -> 36.7 us  [a2a(): return lax.all_to_all(x, 'seq', split_axis=0, concat_axis=0, tiled=True)]
    all_to_all x2 -> x3, starting transfers between devices: 12.5 us -> 20.4 us  [a2a(): return lax.all_to_all(x, 'seq', split_axis=0, concat_axis=0, tiled=True)]
    all_to_all x0 -> x1, starting transfers between devices: none -> 7.77 us  [reduce_yz(): lax.all_to_all(l, 'seq', split_axis=0, concat_axis=0, tiled=True, axis_in...]
    pallas_call x2, Pallas kernels: 18.9 us -> 16.9 us  [logits(): pl.pallas_call(functools.partial(logits_kernel, first), grid=(s // 2,), i...]
    unnamed x12 -> x14, local copies, waits for them, and re-layouts: 4.67 us -> 5.86 us
  transfers between devices with their start and end apart: 5 -> 8, of which waited for: 3 -> 6; matrix products, arithmetic and copies ran while one was open for 1% -> 2% of each run, Pallas kernels for 11% -> 15%
where the time goes in v2:
time: 181 us; the launch traced here: 179 us
  waiting for transfers between devices  53 us (29%)
  Pallas kernels  49.6 us (27%)
  starting transfers between devices  34.8 us (19%)
  blocking collectives  26.9 us (15%)
  local copies, waits for them, and re-layouts  13.5 us (7%)
    all_to_all x3, waiting for transfers between devices, a2a(): return lax.all_to_all(x, 'seq', split_axis=0, concat_axis=0, tiled=True)  36.7 us
    all_to_all x1, blocking collectives, a2a(): return lax.all_to_all(x, 'seq', split_axis=0, concat_axis=0, tiled=True)  26.9 us
    all_to_all x3, starting transfers between devices, a2a(): return lax.all_to_all(x, 'seq', split_axis=0, concat_axis=0, tiled=True)  20.4 us
    pallas_call x2, Pallas kernels, logits(): pl.pallas_call(functools.partial(logits_kernel, first), grid=(s // 2,), i...  16.9 us
    pallas_call x1, Pallas kernels, column(): pl.pallas_call(column_kernel, out_shape=jax.ShapeDtypeStruct(hc.shape, BF...  14.5 us
    all_to_all x1, waiting for transfers between devices, reduce_yz(): lax.all_to_all(l, 'seq', split_axis=0, concat_axis=0, tiled=True, axis_in...  12.7 us
    pallas_call x1, Pallas kernels, values(): pl.pallas_call(values_kernel, grid=(s // 2,), in_specs=specs + [whole(g.s...  10.6 us
    all_to_all x1, starting transfers between devices, reduce_yz(): lax.all_to_all(l, 'seq', split_axis=0, concat_axis=0, tiled=True, axis_in...  7.77 us
  transfers between devices with their start and end apart: 8, of which 6 were waited for; matrix products, arithmetic and copies ran while one was open for 2% of the time, Pallas kernels for 15%

profile of v2, /device:TPU:1, one launch (start us, length us, event | category | flops | bytes accessed | tf_op | source)
XLA Modules:
  0.0 178.6 jit_solution(6674654220718733572)
XLA Ops:
  0.0 1.4 collective-permute-start.1
  1.4 2.8 %collective-permute-start = (bf16[8,128,768]{2,1,0:T(8,128)(2,1)}, bf16[8,128,768]{2,1,0:T(8,128)(2,1)S(1)}, u32[]{:S(2)}, u32[]{:S(2)}) collective-permute-start(bf16[8,128,768]{2,1,0:T(8,128)(2,1)} %x.1), channel_id=1, source_target_pairs={{0,2},{1,3},{2,0},{3,1},{4,6},{5,7},{6,4},{7,5},{8,10},{9,11},{10,... | collective-permute-start | bytes 4718600 | tf_op jit(solution)/shard_map/ppermute | solution.py:236
  4.2 1.3 reshape.69.refs_2_.refs_4_
  5.5 1.1 copy-done.5
  6.7 8.7 %logits.2 = (bf16[12,128,512]{2,1,0:T(8,128)(2,1)S(1)}, bf16[12,128,256]{2,1,0:T(8,128)(2,1)S(1)}) custom-call(bf16[8,128,768]{2,1,0:T(8,128)(2,1)} %x.1, bf16[8,128,768]{2,1,0:T(8,128)(2,1)} %copy-done.5, f32[1,768]{1,0:T(1,128)} %reshape.69.refs_2_.refs_4_, bf16[768,768]{1,0:T(8,128)(2,1)} %refs_3_.3, bf16[768,768]{1,0:T(8,128)(2,1)} %refs_4_.1), custom_call_target="tpu_custom_call" | custom-call | tf_op jit(solution)/shard_map/logits/pallas_call | solution.py:93
  15.4 1.2 copy-done.4
  16.5 1.0 copy.20
  17.5 7.8 %all-to-all-start = ((bf16[16,2,48,256]{3,2,1,0:T(8,128)(2,1)}), bf16[16,2,48,256]{3,2,1,0:T(8,128)(2,1)S(1)}, u32[]{:S(2)}, u32[]{:S(2)}) async-start(bf16[16,2,48,256]{3,2,1,0:T(8,128)(2,1)} %bitcast.19), calls=%async_computation | async-start | bytes 1572864 | tf_op jit(solution)/shard_map/all_to_all | solution.py:243
  25.3 12.7 %all-to-all-done = bf16[16,2,48,256]{3,2,1,0:T(8,128)(2,1)S(1)} async-done(((bf16[16,2,48,256]{3,2,1,0:T(8,128)(2,1)}), bf16[16,2,48,256]{3,2,1,0:T(8,128)(2,1)S(1)}, u32[]{:S(2)}, u32[]{:S(2)}) %all-to-all-start) | async-done | bytes 786464 | tf_op jit(solution)/shard_map/all_to_all | solution.py:243
  38.1 1.1 collective-permute-done.refs_0_.refs_2_
  39.2 1.9 %collective-permute-start.2 = (bf16[8,128,768]{2,1,0:T(8,128)(2,1)S(1)}, bf16[8,128,768]{2,1,0:T(8,128)(2,1)S(1)}, u32[]{:S(2)}, u32[]{:S(2)}) collective-permute-start(bf16[8,128,768]{2,1,0:T(8,128)(2,1)S(1)} %collective-permute-done.refs_0_.refs_2_), channel_id=1, source_target_pairs={{0,1},{1,0},{2,3},{3,2},{4,5},{5,4},{6,7},{7,6},{8,9},{9,8},{10,11... | collective-permute-start | bytes 4718600 | tf_op jit(solution)/shard_map/ppermute | solution.py:253
  41.1 0.4 collective-permute-start.3
  41.5 2.6 %collective-permute-done.2.refs_1_.refs_3_ = bf16[8,128,768]{2,1,0:T(8,128)(2,1)S(1)} collective-permute-done((bf16[8,128,768]{2,1,0:T(8,128)(2,1)S(1)}, bf16[8,128,768]{2,1,0:T(8,128)(2,1)S(1)}, u32[]{:S(2)}, u32[]{:S(2)}) %collective-permute-start.2) | collective-permute-done | bytes 1572896 | tf_op jit(solution)/shard_map/ppermute | solution.py:253
  44.1 8.2 %logits.3 = bf16[12,128,256]{2,1,0:T(8,128)(2,1)S(1)} custom-call(bf16[8,128,768]{2,1,0:T(8,128)(2,1)S(1)} %collective-permute-done.refs_0_.refs_2_, bf16[8,128,768]{2,1,0:T(8,128)(2,1)S(1)} %collective-permute-done.2.refs_1_.refs_3_, f32[1,768]{1,0:T(1,128)} %reshape.69.refs_2_.refs_4_, bf16[768,768]{1,0:T(8,128)(2,1)} %refs_3_.3, ...), custom_call_target="tpu_custom_call" | custom-call | tf_op jit(solution)/shard_map/logits/pallas_call | solution.py:93
  52.4 0.9 copy-done.3
  53.2 7.9 %all-to-all-start.1 = ((bf16[32,48,256]{2,1,0:T(8,128)(2,1)}), bf16[32,48,256]{2,1,0:T(8,128)(2,1)S(1)}, u32[]{:S(2)}, u32[]{:S(2)}) async-start(bf16[32,48,256]{2,1,0:T(8,128)(2,1)} %bitcast.21), calls=%async_computation.1 | async-start | bytes 1572864 | tf_op jit(solution)/shard_map/all_to_all | solution.py:224
  61.2 12.4 %all-to-all-done.1 = bf16[32,48,256]{2,1,0:T(8,128)(2,1)S(1)} async-done(((bf16[32,48,256]{2,1,0:T(8,128)(2,1)}), bf16[32,48,256]{2,1,0:T(8,128)(2,1)S(1)}, u32[]{:S(2)}, u32[]{:S(2)}) %all-to-all-start.1) | async-done | bytes 786464 | tf_op jit(solution)/shard_map/all_to_all | solution.py:224
  73.6 0.1 convert_reduce_fusion
  73.8 0.2 fusion
  74.1 1.3 broadcast_in_dim.2
  75.5 5.3 %all-to-all-start.2 = ((bf16[32,48,512]{2,1,0:T(8,128)(2,1)}), bf16[32,48,512]{2,1,0:T(8,128)(2,1)S(1)}, u32[]{:S(2)}, u32[]{:S(2)}) async-start(bf16[32,48,512]{2,1,0:T(8,128)(2,1)} %broadcast_in_dim.2), calls=%async_computation.2 | async-start | bytes 3145728 | tf_op jit(solution)/shard_map/all_to_all | solution.py:224
  80.7 10.6 %values.1.v = bf16[12,512,512]{2,1,0:T(8,128)(2,1)S(1)} custom-call(bf16[8,128,768]{2,1,0:T(8,128)(2,1)} %x.1, bf16[8,128,768]{2,1,0:T(8,128)(2,1)} %copy-done.5, bf16[8,128,768]{2,1,0:T(8,128)(2,1)} %copy-done.1, bf16[8,128,768]{2,1,0:T(8,128)(2,1)} %copy-done.2, f32[1,768]{1,0:T(1,128)} %reshape.69.refs_2_.refs_4_, bf16[768,768]{1,0:T(8,128)(2,1)} %refs_5_.1), custom_call_target="tpu_custom_call" | custom-call | tf_op jit(solution)/shard_map/values/pallas_call | solution.py:120
  91.3 2.7 %copy-done = bf16[12,512,512]{2,1,0:T(8,128)(2,1)} copy-done((bf16[12,512,512]{2,1,0:T(8,128)(2,1)}, bf16[12,512,512]{2,1,0:T(8,128)(2,1)S(1)}, u32[]{:S(2)}) %copy-start) | copy-done | bytes 6291480
  94.0 6.0 %all-to-all-done.2 = bf16[32,48,512]{2,1,0:T(8,128)(2,1)S(1)} async-done(((bf16[32,48,512]{2,1,0:T(8,128)(2,1)}), bf16[32,48,512]{2,1,0:T(8,128)(2,1)S(1)}, u32[]{:S(2)}, u32[]{:S(2)}) %all-to-all-start.2) | async-done | bytes 1572896 | tf_op jit(solution)/shard_map/all_to_all | solution.py:224
  99.9 7.7 %mix.1 = bf16[8,128,768]{2,1,0:T(8,128)(2,1)S(1)} custom-call(bf16[12,128,512]{2,1,0:T(8,128)(2,1)S(1)} %bitcast.20, bf16[12,512,512]{2,1,0:T(8,128)(2,1)} %copy-done, bf16[8,128,768]{2,1,0:T(8,128)(2,1)} %x.1, bf16[768,768]{1,0:T(8,128)(2,1)} %wo.2), custom_call_target="tpu_custom_call" | custom-call | tf_op jit(solution)/shard_map/mix/pallas_call | solution.py:147
  107.6 2.0 %copy.17 = bf16[8,128,768]{2,0,1:T(8,128)(2,1)} copy(bf16[8,128,768]{2,1,0:T(8,128)(2,1)S(1)} %mix.1) | data formatting | bytes 3145728 | tf_op jit(solution)/shard_map/reshape | solution.py:265
  109.6 7.2 %all-to-all-start.3 = ((bf16[32,32,768]{2,1,0:T(8,128)(2,1)}), bf16[32,32,768]{2,1,0:T(8,128)(2,1)S(1)}, u32[]{:S(2)}, u32[]{:S(2)}) async-start(bf16[32,32,768]{2,1,0:T(8,128)(2,1)} %bitcast.8), calls=%async_computation.3 | async-start | bytes 3145728 | tf_op jit(solution)/shard_map/all_to_all | solution.py:224
  116.9 0.6 reshape.75.g
  117.5 18.3 %all-to-all-done.3.h_ref = bf16[32,32,768]{2,1,0:T(8,128)(2,1)S(1)} async-done(((bf16[32,32,768]{2,1,0:T(8,128)(2,1)}), bf16[32,32,768]{2,1,0:T(8,128)(2,1)S(1)}, u32[]{:S(2)}, u32[]{:S(2)}) %all-to-all-start.3) | async-done | bytes 1572896 | tf_op jit(solution)/shard_map/all_to_all | solution.py:224
  135.8 14.5 %column.1 = bf16[32,32,768]{2,1,0:T(8,128)(2,1)S(1)} custom-call(bf16[32,32,768]{2,1,0:T(8,128)(2,1)S(1)} %all-to-all-done.3.h_ref, f32[1,768]{1,0:T(1,128)} %reshape.75.g, bf16[768,768]{1,0:T(8,128)(2,1)} %wq.1, bf16[768,768]{1,0:T(8,128)(2,1)} %wk.1, bf16[768,768]{1,0:T(8,128)(2,1)} %wv.1, bf16[768,768]{1,0:T(8,128)(2,1)} %wo.3), custom_call_target="tpu_custom_call" | custom-call | tf_op jit(solution)/shard_map/column/pallas_call | solution.py:214
  150.3 26.9 %all_to_all.25 = bf16[32,32,768]{2,1,0:T(8,128)(2,1)S(1)} all-to-all(bf16[32,32,768]{2,1,0:T(8,128)(2,1)S(1)} %column.1), channel_id=1, replica_groups=mesh['seq'=32,'res'=4] {'seq'}, dimensions={0} | all-to-all | bytes 3145728 | tf_op jit(solution)/shard_map/all_to_all | solution.py:224
  177.2 1.4 copy.18
  (18 shorter events, 0.4 us)
Async XLA Ops:
  0.0 5.5 %collective-permute-start.1 = (bf16[8,128,768]{2,1,0:T(8,128)(2,1)}, bf16[8,128,768]{2,1,0:T(8,128)(2,1)S(1)}, u32[]{:S(2)}, u32[]{:S(2)}) collective-permute-start(bf16[8,128,768]{2,1,0:T(8,128)(2,1)} %x.1), channel_id=1, source_target_pairs={{0,1},{1,0},{2,3},{3,2},{4,5},{5,4},{6,7},{7,6},{8,9},{9,8},{10,11... | collective-permute-start | bytes 4718600 | tf_op jit(solution)/shard_map/ppermute | solution.py:237
  1.4 37.7 %collective-permute-start = (bf16[8,128,768]{2,1,0:T(8,128)(2,1)}, bf16[8,128,768]{2,1,0:T(8,128)(2,1)S(1)}, u32[]{:S(2)}, u32[]{:S(2)}) collective-permute-start(bf16[8,128,768]{2,1,0:T(8,128)(2,1)} %x.1), channel_id=1, source_target_pairs={{0,2},{1,3},{2,0},{3,1},{4,6},{5,7},{6,4},{7,5},{8,10},{9,11},{10,... | collective-permute-start | bytes 4718600 | tf_op jit(solution)/shard_map/ppermute | solution.py:236
  5.5 1.1 copy-start.5
  15.4 1.2 copy-start.4
  17.5 20.5 %all-to-all-start = ((bf16[16,2,48,256]{3,2,1,0:T(8,128)(2,1)}), bf16[16,2,48,256]{3,2,1,0:T(8,128)(2,1)S(1)}, u32[]{:S(2)}, u32[]{:S(2)}) async-start(bf16[16,2,48,256]{3,2,1,0:T(8,128)(2,1)} %bitcast.19), calls=%async_computation | async-start | bytes 1572864 | tf_op jit(solution)/shard_map/all_to_all | solution.py:243
  39.2 13.2 %copy-start.1 = (bf16[8,128,768]{2,1,0:T(8,128)(2,1)}, bf16[8,128,768]{2,1,0:T(8,128)(2,1)S(1)}, u32[]{:S(2)}) copy-start(bf16[8,128,768]{2,1,0:T(8,128)(2,1)S(1)} %collective-permute-done.refs_0_.refs_2_) | copy-start | bytes 4718596
  39.2 5.0 %collective-permute-start.2 = (bf16[8,128,768]{2,1,0:T(8,128)(2,1)S(1)}, bf16[8,128,768]{2,1,0:T(8,128)(2,1)S(1)}, u32[]{:S(2)}, u32[]{:S(2)}) collective-permute-start(bf16[8,128,768]{2,1,0:T(8,128)(2,1)S(1)} %collective-permute-done.refs_0_.refs_2_), channel_id=1, source_target_pairs={{0,1},{1,0},{2,3},{3,2},{4,5},{5,4},{6,7},{7,6},{8,9},{9,8},{10,11... | collective-permute-start | bytes 4718600 | tf_op jit(solution)/shard_map/ppermute | solution.py:253
  41.1 12.2 %collective-permute-start.3 = (bf16[48,256]{1,0:T(8,128)(2,1)S(1)}, bf16[48,256]{1,0:T(8,128)(2,1)S(1)}, u32[]{:S(2)}, u32[]{:S(2)}) collective-permute-start(bf16[48,256]{1,0:T(8,128)(2,1)S(1)} %fusion.2), channel_id=1, source_target_pairs={{0,64},{4,68},{8,72},{12,76},{16,80},{20,84},{24,88},{28,92},{32,9... | collective-permute-start | bytes 73736 | tf_op jit(solution)/shard_map/ppermute | solution.py:248
  44.1 8.2 %copy-start.2 = (bf16[8,128,768]{2,1,0:T(8,128)(2,1)}, bf16[8,128,768]{2,1,0:T(8,128)(2,1)S(1)}, u32[]{:S(2)}) copy-start(bf16[8,128,768]{2,1,0:T(8,128)(2,1)S(1)} %collective-permute-done.2.refs_1_.refs_3_) | copy-start | bytes 4718596
  52.4 0.9 copy-start.3
  53.2 20.4 %all-to-all-start.1 = ((bf16[32,48,256]{2,1,0:T(8,128)(2,1)}), bf16[32,48,256]{2,1,0:T(8,128)(2,1)S(1)}, u32[]{:S(2)}, u32[]{:S(2)}) async-start(bf16[32,48,256]{2,1,0:T(8,128)(2,1)} %bitcast.21), calls=%async_computation.1 | async-start | bytes 1572864 | tf_op jit(solution)/shard_map/all_to_all | solution.py:224
  75.5 24.5 %all-to-all-start.2 = ((bf16[32,48,512]{2,1,0:T(8,128)(2,1)}), bf16[32,48,512]{2,1,0:T(8,128)(2,1)S(1)}, u32[]{:S(2)}, u32[]{:S(2)}) async-start(bf16[32,48,512]{2,1,0:T(8,128)(2,1)} %broadcast_in_dim.2), calls=%async_computation.2 | async-start | bytes 3145728 | tf_op jit(solution)/shard_map/all_to_all | solution.py:224
  91.3 2.7 %copy-start = (bf16[12,512,512]{2,1,0:T(8,128)(2,1)}, bf16[12,512,512]{2,1,0:T(8,128)(2,1)S(1)}, u32[]{:S(2)}) copy-start(bf16[12,512,512]{2,1,0:T(8,128)(2,1)S(1)} %values.1.v) | copy-start | bytes 18874372
  109.6 7.2 %copy-start.6 = (f32[768]{0:T(1024)S(1)}, f32[768]{0:T(1024)}, u32[]{:S(2)}) copy-start(f32[768]{0:T(1024)} %param.17) | copy-start | bytes 9220
  109.6 26.2 %all-to-all-start.3 = ((bf16[32,32,768]{2,1,0:T(8,128)(2,1)}), bf16[32,32,768]{2,1,0:T(8,128)(2,1)S(1)}, u32[]{:S(2)}, u32[]{:S(2)}) async-start(bf16[32,32,768]{2,1,0:T(8,128)(2,1)} %bitcast.8), calls=%async_computation.3 | async-start | bytes 3145728 | tf_op jit(solution)/shard_map/all_to_all | solution.py:224

commit v3 on v2

--- a/solution.py
+++ b/solution.py
@@ -55,48 +55,52 @@
 
 def logits_kernel(first, *refs):
     if first:
-        xa, xb, g, wk, wq, q, out, ks = refs
+        xa, xb, g, wk_h, wq_h, q, out, ks, wk, wq, sems = refs
+        copies = [pltpu.make_async_copy(wk_h, wk, sems.at[0]), pltpu.make_async_copy(wq_h, wq, sems.at[1])]
     else:
-        xa, xb, g, wk, q, out, ks = refs
-    t = pl.program_id(0)
-    n, f = xa.shape[1:]
-    lane = pl.multiple_of(t * 2 * D, 2 * D)
-    na = norm(xa[...].reshape(2 * n, f), g[...])
-    nb = norm(xb[...].reshape(2 * n, f), g[...])
-    ka = mm(na, wk[...]).astype(BF16)
-    kb = mm(nb, wk[...]).astype(BF16)
+        xa, xb, g, wk_h, q_h, out, ks, wk, q, sems = refs
+        copies = [pltpu.make_async_copy(wk_h, wk, sems.at[0]), pltpu.make_async_copy(q_h, q, sems.at[1])]
+    for c in copies:
+        c.start()
+    s, n, f = xa.shape
+    na = norm(xa[...].reshape(s * n, f), g[...])
+    nb = norm(xb[...].reshape(s * n, f), g[...])
+    copies[0].wait()
+
+    def put(ref, rows, y):
+        for j in range(0, s, 2):
+            z = y[j * n : (j + 2) * n]
+            for h in range(HEADS):
+                ref[h, rows, j * D : (j + 2) * D] = pair(z, n, h)
+
+    put(ks, slice(0, n), mm(na, wk[...]).astype(BF16))
+    put(ks, slice(n, 2 * n), mm(nb, wk[...]).astype(BF16))
+    copies[1].wait()
+    if first:
+        put(q, slice(0, n), mm(na, wq[...]).astype(BF16))
     for h in range(HEADS):
-        ks[h, 0:n, pl.ds(lane, 2 * D)] = pair(ka, n, h)
-        ks[h, n : 2 * n, pl.ds(lane, 2 * D)] = pair(kb, n, h)
-    if first:
-        qq = mm(na, wq[...]).astype(BF16)
-        for h in range(HEADS):
-            q[h, :, pl.ds(lane, 2 * D)] = pair(qq, n, h)
-
-    @pl.when(t == pl.num_programs(0) - 1)
-    def _():
-        for h in range(HEADS):
-            out[h] = mm_t(q[h], ks[h]).astype(BF16)
+        out[h] = mm_t(q[h], ks[h]).astype(BF16)
 
 
 def logits(xa, xb, g, wk, wq=None, q=None):
     s, n, f = xa.shape
     first = q is None
-    m = n if first else q.shape[1]
-    xs = pl.BlockSpec((2, n, f), lambda t: (t, 0, 0))
-    in_specs = [xs, xs, whole(g.shape), whole(wk.shape)]
-    qshape = (HEADS, m, s * D)
-    lshape = (HEADS, m, 2 * n)
-    in_specs += [whole(wq.shape)] if first else [whole(qshape)]
-    ospecs = [whole(qshape), whole(lshape)] if first else [whole(lshape)]
+    qshape = (HEADS, n, s * D)
+    lshape = (HEADS, n, 2 * n)
     oshape = [jax.ShapeDtypeStruct(qshape, BF16), jax.ShapeDtypeStruct(lshape, BF16)]
+    here = pl.BlockSpec(memory_space=pltpu.VMEM)
+    there = pl.BlockSpec(memory_space=pl.ANY)
     return pl.pallas_call(
         functools.partial(logits_kernel, first),
-        grid=(s // 2,),
-        in_specs=in_specs,
-        out_specs=ospecs,
+        in_specs=[here, here, here, there, there],
+        out_specs=[here, here] if first else [here],
         out_shape=oshape if first else oshape[1:],
-        scratch_shapes=[pltpu.VMEM((HEADS, 2 * n, s * D), BF16)],
+        scratch_shapes=[
+            pltpu.VMEM((HEADS, 2 * n, s * D), BF16),
+            pltpu.VMEM(wk.shape, BF16),
+            pltpu.VMEM(wq.shape if first else qshape, BF16),
+            pltpu.SemaphoreType.DMA((2,)),
+        ],
         compiler_params=PARAMS,
         name="logits",
     )(*(far(xa, xb) if first else near(xa, xb)), *far(g, wk, wq if first else q))
@@ -128,40 +132,52 @@
     )(*far(*pieces, g, wv))
 
 
-def mix_kernel(p, v, x, wo, out, ms):
-    t = pl.program_id(0)
+def mix_kernel(p, v_h, x_h, wo_h, out, ms, v, x, wo, sems):
+    pairs = HEADS // 2
     s = x.shape[0]
-    lane = pl.multiple_of(t * 2 * D, 2 * D)
-    o = [mm(p[h], v[h]).astype(BF16) for h in range(2)]
-    for r in range(s):
-        ms[r, :, pl.ds(lane, 2 * D)] = jnp.concatenate([head(o[0], r), head(o[1], r)], axis=1)
-
-    @pl.when(t == pl.num_programs(0) - 1)
-    def _():
+    copies = [
+        pltpu.make_async_copy(v_h.at[2 * t : 2 * t + 2], v.at[2 * t : 2 * t + 2], sems.at[t]) for t in range(pairs)
+    ]
+    copies += [pltpu.make_async_copy(x_h, x, sems.at[pairs]), pltpu.make_async_copy(wo_h, wo, sems.at[pairs + 1])]
+    for c in copies:
+        c.start()
+    for t in range(pairs):
+        copies[t].wait()
+        o = [mm(p[2 * t + h], v[2 * t + h]).astype(BF16) for h in range(2)]
         for r in range(s):
-            out[r] = (x[r].astype(F32) + mm(ms[r], wo[...])).astype(BF16)
+            ms[r, :, t * 2 * D : (t + 1) * 2 * D] = jnp.concatenate([head(o[0], r), head(o[1], r)], axis=1)
+    copies[pairs].wait()
+    copies[pairs + 1].wait()
+    y = mm(ms[...].reshape(-1, x.shape[2]), wo[...])
+    out[...] = (x[...].astype(F32) + y.reshape(x.shape)).astype(BF16)
 
 
 def mix(p, v, x, wo):
     s, n, f = x.shape
+    here = pl.BlockSpec(memory_space=pltpu.VMEM)
+    there = pl.BlockSpec(memory_space=pl.ANY)
     return pl.pallas_call(
         mix_kernel,
-        grid=(HEADS // 2,),
-        in_specs=[
-            pl.BlockSpec((2,) + p.shape[1:], lambda t: (t, 0, 0)),
-            pl.BlockSpec((2,) + v.shape[1:], lambda t: (t, 0, 0)),
-            whole(x.shape),
-            whole(wo.shape),
+        in_specs=[here, there, there, there],
+        out_specs=here,
+        out_shape=jax.ShapeDtypeStruct(x.shape, BF16),
+        scratch_shapes=[
+            pltpu.VMEM((s, n, f), BF16),
+            pltpu.VMEM(v.shape, BF16),
+            pltpu.VMEM((s, n, f), BF16),
+            pltpu.VMEM(wo.shape, BF16),
+            pltpu.SemaphoreType.DMA((HEADS // 2 + 2,)),
         ],
-        out_specs=whole(x.shape),
-        out_shape=jax.ShapeDtypeStruct(x.shape, BF16),
-        scratch_shapes=[pltpu.VMEM((s, n, f), BF16)],
         compiler_params=PARAMS,
         name="mix",
     )(*near(p), *far(v, x, wo))
 
 
-def column_kernel(h_ref, g, wq, wk, wv, wo, out, xs, ns, qs, ks, vs, ms):
+def column_kernel(h_ref, g, *refs):
+    away, (out, xs, ns, qs, ks, vs, ms, w, sems) = refs[:4], refs[4:]
+    copies = [pltpu.make_async_copy(z, w.at[i], sems.at[i]) for i, z in enumerate(away)]
+    for c in copies:
+        c.start()
     src, rows, f = h_ref.shape
     a = src * 8
     for i in range(0, rows, 16):
@@ -169,40 +185,41 @@
         for j in range(2):
             xs[pl.ds((i // 8 + j) * a, a)] = y[:, 8 * j : 8 * j + 8].reshape(a, f)
 
-    def project(p, carry):
+    def normed(p, carry):
         r = pl.ds(pl.multiple_of(p * a, a), a)
-        n = norm(xs[r], g[...])
-        qs[r] = (mm(n, wq[...]) * (1.0 / (math.sqrt(D) * math.log(2.0)))).astype(BF16)
-        ks[r] = mm(n, wk[...]).astype(BF16)
-        vs[r] = mm(n, wv[...]).astype(BF16)
+        ns[r] = norm(xs[r], g[...])
         return carry
 
     def attend(p, carry):
         r = pl.ds(pl.multiple_of(p * a, a), a)
         low = lax.broadcasted_iota(jnp.int32, (a, 2 * D), 1) < D
         zero = jnp.zeros((a, 2 * D), BF16)
-        ones = jnp.ones((a, 2 * D), BF16)
+        one = jnp.ones((a, 2 * D), BF16)
+        ones = jnp.concatenate([jnp.where(low, one, zero), jnp.where(low, zero, one)], axis=0)
         for hp in range(HEADS // 2):
             c = slice(hp * 2 * D, (hp + 1) * 2 * D)
-            q, k = qs[r, c], ks[r, c]
-            v = jnp.concatenate([vs[r, c], ones], axis=1)
-            o = []
-            for kh in (jnp.where(low, k, zero), jnp.where(low, zero, k)):
-                l = mm_t(q, kh)
-                e = jnp.exp2(l - jnp.max(l, axis=-1, keepdims=True)).astype(BF16)
-                w = mm(e, v)
-                o.append(w[:, : 2 * D] / w[:, 2 * D :])
-            ms[r, c] = jnp.where(low, o[0], o[1]).astype(BF16)
+            q, k, v = qs[r, c], ks[r, c], vs[r, c]
+            k = jnp.concatenate([jnp.where(low, k, zero), jnp.where(low, zero, k)], axis=0)
+            v = jnp.concatenate([jnp.where(low, v, zero), jnp.where(low, zero, v)], axis=0)
+            l = mm_t(q, k)
+            e = []
+            for z in (l[:, :a], l[:, a:]):
+                e.append(jnp.exp2(z - jnp.max(z, axis=-1, keepdims=True)).astype(BF16))
+            w = mm(jnp.concatenate(e, axis=1), jnp.concatenate([v, ones], axis=1))
+            ms[r, c] = (w[:, : 2 * D] / w[:, 2 * D :]).astype(BF16)
         return carry
 
-    def emit(p, carry):
-        r = pl.ds(pl.multiple_of(p * a, a), a)
-        xs[r] = xs[r] + mm(ms[r], wo[...])
-        return carry
-
-    lax.fori_loop(0, rows // 8, project, 0)
+    lax.fori_loop(0, rows // 8, normed, 0)
+    n = ns[...]
+    copies[0].wait()
+    qs[...] = (mm(n, w[0]) * (1.0 / (math.sqrt(D) * math.log(2.0)))).astype(BF16)
+    copies[1].wait()
+    ks[...] = mm(n, w[1]).astype(BF16)
+    copies[2].wait()
+    vs[...] = mm(n, w[2]).astype(BF16)
     lax.fori_loop(0, rows // 8, attend, 0)
-    lax.fori_loop(0, rows // 8, emit, 0)
+    copies[3].wait()
+    xs[...] = xs[...] + mm(ms[...], w[3])
     for i in range(0, rows, 16):
         y = [xs[pl.ds((i // 8 + j) * a, a)].reshape(src, 8, f) for j in range(2)]
         out[:, i : i + 16] = jnp.concatenate(y, axis=1).astype(BF16)
@@ -213,8 +230,12 @@
     m = src * rows
     return pl.pallas_call(
         column_kernel,
+        in_specs=[pl.BlockSpec(memory_space=pltpu.VMEM)] * 2 + [pl.BlockSpec(memory_space=pl.ANY)] * 4,
+        out_specs=pl.BlockSpec(memory_space=pltpu.VMEM),
         out_shape=jax.ShapeDtypeStruct(hc.shape, BF16),
-        scratch_shapes=[pltpu.VMEM((m, f), F32)] + [pltpu.VMEM((m, f), BF16)] * 5,
+        scratch_shapes=[pltpu.VMEM((m, f), F32)]
+        + [pltpu.VMEM((m, f), BF16)] * 5
+        + [pltpu.VMEM((4, f, f), BF16), pltpu.SemaphoreType.DMA((4,))],
         compiler_params=PARAMS,
         name="column",
     )(*near(hc), *far(g, wq, wk, wv, wo))

time: 181 us -> 176 us (0.972)
  Pallas kernels: 49.6 us -> 44.9 us
    pallas_call x4, Pallas kernels: 39.1 us -> 34.3 us  [the longest x2 16 us: logits(): pl.pallas_call(functools.partial(logits_kernel, first), in_specs=[here, h...]
where the time goes in v3:
time: 176 us; the launch traced here: 174 us
  waiting for transfers between devices  52.7 us (30%)
  Pallas kernels  44.9 us (26%)
  starting transfers between devices  34.8 us (20%)
  blocking collectives  26.9 us (15%)
  local copies, waits for them, and re-layouts  13.5 us (8%)
    all_to_all x3, waiting for transfers between devices, a2a(): return lax.all_to_all(x, 'seq', split_axis=0, concat_axis=0, tiled=True)  36.6 us
    all_to_all x1, blocking collectives, a2a(): return lax.all_to_all(x, 'seq', split_axis=0, concat_axis=0, tiled=True)  26.9 us
    all_to_all x3, starting transfers between devices, a2a(): return lax.all_to_all(x, 'seq', split_axis=0, concat_axis=0, tiled=True)  20.2 us
    pallas_call x2, Pallas kernels, logits(): pl.pallas_call(functools.partial(logits_kernel, first), in_specs=[here, h...  16 us
    pallas_call x1, Pallas kernels, column(): pl.pallas_call(column_kernel, in_specs=[pl.BlockSpec(memory_space=pltpu.V...  13.2 us
    all_to_all x1, waiting for transfers between devices, reduce_yz(): lax.all_to_all(l, 'seq', split_axis=0, concat_axis=0, tiled=True, axis_in...  12.7 us
    pallas_call x1, Pallas kernels, values(): pl.pallas_call(values_kernel, grid=(s // 2,), in_specs=specs + [whole(g.s...  10.6 us
    all_to_all x1, starting transfers between devices, reduce_yz(): lax.all_to_all(l, 'seq', split_axis=0, concat_axis=0, tiled=True, axis_in...  7.77 us
  transfers between devices with their start and end apart: 8, of which 6 were waited for; matrix products, arithmetic and copies ran while one was open for 2% of the time, Pallas kernels for 15%

profile of v3, /device:TPU:1, one launch (start us, length us, event | category | flops | bytes accessed | tf_op | source)
XLA Modules:
  0.0 173.6 jit_solution(10758203973819897981)
XLA Ops:
  0.0 1.4 collective-permute-start.1
  1.4 2.8 %collective-permute-start = (bf16[8,128,768]{2,1,0:T(8,128)(2,1)}, bf16[8,128,768]{2,1,0:T(8,128)(2,1)S(1)}, u32[]{:S(2)}, u32[]{:S(2)}) collective-permute-start(bf16[8,128,768]{2,1,0:T(8,128)(2,1)} %x_h.1), channel_id=1, source_target_pairs={{0,2},{1,3},{2,0},{3,1},{4,6},{5,7},{6,4},{7,5},{8,10},{9,11},{10,... | collective-permute-start | bytes 4718600 | tf_op jit(solution)/shard_map/ppermute | solution.py:257
  4.2 1.3 reshape.69.refs_2_.refs_4_
  5.5 1.1 copy-done.5
  6.7 8.9 %logits.2 = (bf16[12,128,512]{2,1,0:T(8,128)(2,1)S(1)}, bf16[12,128,256]{2,1,0:T(8,128)(2,1)S(1)}) custom-call(bf16[8,128,768]{2,1,0:T(8,128)(2,1)} %x_h.1, bf16[8,128,768]{2,1,0:T(8,128)(2,1)} %copy-done.5, f32[1,768]{1,0:T(1,128)} %reshape.69.refs_2_.refs_4_, bf16[768,768]{1,0:T(8,128)(2,1)} %refs_3_.4, bf16[768,768]{1,0:T(8,128)(2,1)} %refs_4_.1), custom_call_target="tpu_custom_call" | custom-call | tf_op jit(solution)/shard_map/logits/pallas_call | solution.py:93
  15.6 1.2 copy-done.4
  16.8 1.0 copy.20
  17.8 7.8 %all-to-all-start = ((bf16[16,2,48,256]{3,2,1,0:T(8,128)(2,1)}), bf16[16,2,48,256]{3,2,1,0:T(8,128)(2,1)S(1)}, u32[]{:S(2)}, u32[]{:S(2)}) async-start(bf16[16,2,48,256]{3,2,1,0:T(8,128)(2,1)} %bitcast.19), calls=%async_computation | async-start | bytes 1572864 | tf_op jit(solution)/shard_map/all_to_all | solution.py:264
  25.6 12.7 %all-to-all-done = bf16[16,2,48,256]{3,2,1,0:T(8,128)(2,1)S(1)} async-done(((bf16[16,2,48,256]{3,2,1,0:T(8,128)(2,1)}), bf16[16,2,48,256]{3,2,1,0:T(8,128)(2,1)S(1)}, u32[]{:S(2)}, u32[]{:S(2)}) %all-to-all-start) | async-done | bytes 786464 | tf_op jit(solution)/shard_map/all_to_all | solution.py:264
  38.4 0.8 collective-permute-done.refs_0_.refs_2_
  39.2 2.2 %collective-permute-start.2 = (bf16[8,128,768]{2,1,0:T(8,128)(2,1)S(1)}, bf16[8,128,768]{2,1,0:T(8,128)(2,1)S(1)}, u32[]{:S(2)}, u32[]{:S(2)}) collective-permute-start(bf16[8,128,768]{2,1,0:T(8,128)(2,1)S(1)} %collective-permute-done.refs_0_.refs_2_), channel_id=1, source_target_pairs={{0,1},{1,0},{2,3},{3,2},{4,5},{5,4},{6,7},{7,6},{8,9},{9,8},{10,11... | collective-permute-start | bytes 4718600 | tf_op jit(solution)/shard_map/ppermute | solution.py:274
  41.3 0.4 collective-permute-start.3
  41.7 2.6 %collective-permute-done.2.refs_1_.refs_3_ = bf16[8,128,768]{2,1,0:T(8,128)(2,1)S(1)} collective-permute-done((bf16[8,128,768]{2,1,0:T(8,128)(2,1)S(1)}, bf16[8,128,768]{2,1,0:T(8,128)(2,1)S(1)}, u32[]{:S(2)}, u32[]{:S(2)}) %collective-permute-start.2) | collective-permute-done | bytes 1572896 | tf_op jit(solution)/shard_map/ppermute | solution.py:274
  44.4 7.1 %logits.3 = bf16[12,128,256]{2,1,0:T(8,128)(2,1)S(1)} custom-call(bf16[8,128,768]{2,1,0:T(8,128)(2,1)S(1)} %collective-permute-done.refs_0_.refs_2_, bf16[8,128,768]{2,1,0:T(8,128)(2,1)S(1)} %collective-permute-done.2.refs_1_.refs_3_, f32[1,768]{1,0:T(1,128)} %reshape.69.refs_2_.refs_4_, bf16[768,768]{1,0:T(8,128)(2,1)} %refs_3_.4, ...), custom_call_target="tpu_custom_call" | custom-call | tf_op jit(solution)/shard_map/logits/pallas_call | solution.py:93
  51.5 0.9 copy-done.3
  52.4 7.7 %all-to-all-start.1 = ((bf16[32,48,256]{2,1,0:T(8,128)(2,1)}), bf16[32,48,256]{2,1,0:T(8,128)(2,1)S(1)}, u32[]{:S(2)}, u32[]{:S(2)}) async-start(bf16[32,48,256]{2,1,0:T(8,128)(2,1)} %bitcast.21), calls=%async_computation.1 | async-start | bytes 1572864 | tf_op jit(solution)/shard_map/all_to_all | solution.py:245
  60.1 12.4 %all-to-all-done.1 = bf16[32,48,256]{2,1,0:T(8,128)(2,1)S(1)} async-done(((bf16[32,48,256]{2,1,0:T(8,128)(2,1)}), bf16[32,48,256]{2,1,0:T(8,128)(2,1)S(1)}, u32[]{:S(2)}, u32[]{:S(2)}) %all-to-all-start.1) | async-done | bytes 786464 | tf_op jit(solution)/shard_map/all_to_all | solution.py:245
  72.5 0.1 convert_reduce_fusion
  72.7 0.2 fusion
  73.0 1.3 broadcast_in_dim.2
  74.4 5.3 %all-to-all-start.2 = ((bf16[32,48,512]{2,1,0:T(8,128)(2,1)}), bf16[32,48,512]{2,1,0:T(8,128)(2,1)S(1)}, u32[]{:S(2)}, u32[]{:S(2)}) async-start(bf16[32,48,512]{2,1,0:T(8,128)(2,1)} %broadcast_in_dim.2), calls=%async_computation.2 | async-start | bytes 3145728 | tf_op jit(solution)/shard_map/all_to_all | solution.py:245
  79.6 10.6 %values.1.v_h = bf16[12,512,512]{2,1,0:T(8,128)(2,1)S(1)} custom-call(bf16[8,128,768]{2,1,0:T(8,128)(2,1)} %x_h.1, bf16[8,128,768]{2,1,0:T(8,128)(2,1)} %copy-done.5, bf16[8,128,768]{2,1,0:T(8,128)(2,1)} %copy-done.1, bf16[8,128,768]{2,1,0:T(8,128)(2,1)} %copy-done.2, f32[1,768]{1,0:T(1,128)} %reshape.69.refs_2_.refs_4_, bf16[768,768]{1,0:T(8,128)(2,1)} %refs_5_.1), custom_call_target="tpu_custom_call" | custom-call | tf_op jit(solution)/shard_map/values/pallas_call | solution.py:124
  90.2 2.7 %copy-done = bf16[12,512,512]{2,1,0:T(8,128)(2,1)} copy-done((bf16[12,512,512]{2,1,0:T(8,128)(2,1)}, bf16[12,512,512]{2,1,0:T(8,128)(2,1)S(1)}, u32[]{:S(2)}) %copy-start) | copy-done | bytes 6291480
  92.9 6.0 %all-to-all-done.2 = bf16[32,48,512]{2,1,0:T(8,128)(2,1)S(1)} async-done(((bf16[32,48,512]{2,1,0:T(8,128)(2,1)}), bf16[32,48,512]{2,1,0:T(8,128)(2,1)S(1)}, u32[]{:S(2)}, u32[]{:S(2)}) %all-to-all-start.2) | async-done | bytes 1572896 | tf_op jit(solution)/shard_map/all_to_all | solution.py:245
  98.8 5.1 %mix.1 = bf16[8,128,768]{2,1,0:T(8,128)(2,1)S(1)} custom-call(bf16[12,128,512]{2,1,0:T(8,128)(2,1)S(1)} %bitcast.20, bf16[12,512,512]{2,1,0:T(8,128)(2,1)} %copy-done, bf16[8,128,768]{2,1,0:T(8,128)(2,1)} %x_h.1, bf16[768,768]{1,0:T(8,128)(2,1)} %wo_h.1), custom_call_target="tpu_custom_call" | custom-call | tf_op jit(solution)/shard_map/mix/pallas_call | solution.py:159
  103.9 2.0 %copy.17 = bf16[8,128,768]{2,0,1:T(8,128)(2,1)} copy(bf16[8,128,768]{2,1,0:T(8,128)(2,1)S(1)} %mix.1) | data formatting | bytes 3145728 | tf_op jit(solution)/shard_map/reshape | solution.py:286
  105.9 7.3 %all-to-all-start.3 = ((bf16[32,32,768]{2,1,0:T(8,128)(2,1)}), bf16[32,32,768]{2,1,0:T(8,128)(2,1)S(1)}, u32[]{:S(2)}, u32[]{:S(2)}) async-start(bf16[32,32,768]{2,1,0:T(8,128)(2,1)} %bitcast.8), calls=%async_computation.3 | async-start | bytes 3145728 | tf_op jit(solution)/shard_map/all_to_all | solution.py:245
  113.2 0.6 reshape.75.g
  113.8 18.2 %all-to-all-done.3.h_ref = bf16[32,32,768]{2,1,0:T(8,128)(2,1)S(1)} async-done(((bf16[32,32,768]{2,1,0:T(8,128)(2,1)}), bf16[32,32,768]{2,1,0:T(8,128)(2,1)S(1)}, u32[]{:S(2)}, u32[]{:S(2)}) %all-to-all-start.3) | async-done | bytes 1572896 | tf_op jit(solution)/shard_map/all_to_all | solution.py:245
  132.0 13.2 %column.1 = bf16[32,32,768]{2,1,0:T(8,128)(2,1)S(1)} custom-call(bf16[32,32,768]{2,1,0:T(8,128)(2,1)S(1)} %all-to-all-done.3.h_ref, f32[1,768]{1,0:T(1,128)} %reshape.75.g, bf16[768,768]{1,0:T(8,128)(2,1)} %refs_0_.4, bf16[768,768]{1,0:T(8,128)(2,1)} %refs_1_.1, bf16[768,768]{1,0:T(8,128)(2,1)} %refs_2_.1, bf16[768,768]{1,0:T(8,128)(2,1)} %refs_3_.5), custom_call_target="tpu_custom_call" | custom-call | tf_op jit(solution)/shard_map/column/pallas_call | solution.py:231
  145.3 26.9 %all_to_all.25 = bf16[32,32,768]{2,1,0:T(8,128)(2,1)S(1)} all-to-all(bf16[32,32,768]{2,1,0:T(8,128)(2,1)S(1)} %column.1), channel_id=1, replica_groups=mesh['seq'=32,'res'=4] {'seq'}, dimensions={0} | all-to-all | bytes 3145728 | tf_op jit(solution)/shard_map/all_to_all | solution.py:245
  172.2 1.4 copy.18
  (18 shorter events, 0.4 us)
Async XLA Ops:
  0.0 5.5 %collective-permute-start.1 = (bf16[8,128,768]{2,1,0:T(8,128)(2,1)}, bf16[8,128,768]{2,1,0:T(8,128)(2,1)S(1)}, u32[]{:S(2)}, u32[]{:S(2)}) collective-permute-start(bf16[8,128,768]{2,1,0:T(8,128)(2,1)} %x_h.1), channel_id=1, source_target_pairs={{0,1},{1,0},{2,3},{3,2},{4,5},{5,4},{6,7},{7,6},{8,9},{9,8},{10,11... | collective-permute-start | bytes 4718600 | tf_op jit(solution)/shard_map/ppermute | solution.py:258
  1.4 37.7 %collective-permute-start = (bf16[8,128,768]{2,1,0:T(8,128)(2,1)}, bf16[8,128,768]{2,1,0:T(8,128)(2,1)S(1)}, u32[]{:S(2)}, u32[]{:S(2)}) collective-permute-start(bf16[8,128,768]{2,1,0:T(8,128)(2,1)} %x_h.1), channel_id=1, source_target_pairs={{0,2},{1,3},{2,0},{3,1},{4,6},{5,7},{6,4},{7,5},{8,10},{9,11},{10,... | collective-permute-start | bytes 4718600 | tf_op jit(solution)/shard_map/ppermute | solution.py:257
  5.5 1.1 copy-start.5
  15.6 1.2 copy-start.4
  17.8 20.5 %all-to-all-start = ((bf16[16,2,48,256]{3,2,1,0:T(8,128)(2,1)}), bf16[16,2,48,256]{3,2,1,0:T(8,128)(2,1)S(1)}, u32[]{:S(2)}, u32[]{:S(2)}) async-start(bf16[16,2,48,256]{3,2,1,0:T(8,128)(2,1)} %bitcast.19), calls=%async_computation | async-start | bytes 1572864 | tf_op jit(solution)/shard_map/all_to_all | solution.py:264
  39.2 12.3 %copy-start.1 = (bf16[8,128,768]{2,1,0:T(8,128)(2,1)}, bf16[8,128,768]{2,1,0:T(8,128)(2,1)S(1)}, u32[]{:S(2)}) copy-start(bf16[8,128,768]{2,1,0:T(8,128)(2,1)S(1)} %collective-permute-done.refs_0_.refs_2_) | copy-start | bytes 4718596
  39.2 5.2 %collective-permute-start.2 = (bf16[8,128,768]{2,1,0:T(8,128)(2,1)S(1)}, bf16[8,128,768]{2,1,0:T(8,128)(2,1)S(1)}, u32[]{:S(2)}, u32[]{:S(2)}) collective-permute-start(bf16[8,128,768]{2,1,0:T(8,128)(2,1)S(1)} %collective-permute-done.refs_0_.refs_2_), channel_id=1, source_target_pairs={{0,1},{1,0},{2,3},{3,2},{4,5},{5,4},{6,7},{7,6},{8,9},{9,8},{10,11... | collective-permute-start | bytes 4718600 | tf_op jit(solution)/shard_map/ppermute | solution.py:274
  41.3 11.0 %collective-permute-start.3 = (bf16[48,256]{1,0:T(8,128)(2,1)S(1)}, bf16[48,256]{1,0:T(8,128)(2,1)S(1)}, u32[]{:S(2)}, u32[]{:S(2)}) collective-permute-start(bf16[48,256]{1,0:T(8,128)(2,1)S(1)} %fusion.2), channel_id=1, source_target_pairs={{0,64},{4,68},{8,72},{12,76},{16,80},{20,84},{24,88},{28,92},{32,9... | collective-permute-start | bytes 73736 | tf_op jit(solution)/shard_map/ppermute | solution.py:269
  44.4 7.1 %copy-start.2 = (bf16[8,128,768]{2,1,0:T(8,128)(2,1)}, bf16[8,128,768]{2,1,0:T(8,128)(2,1)S(1)}, u32[]{:S(2)}) copy-start(bf16[8,128,768]{2,1,0:T(8,128)(2,1)S(1)} %collective-permute-done.2.refs_1_.refs_3_) | copy-start | bytes 4718596
  51.5 0.9 copy-start.3
  52.4 20.1 %all-to-all-start.1 = ((bf16[32,48,256]{2,1,0:T(8,128)(2,1)}), bf16[32,48,256]{2,1,0:T(8,128)(2,1)S(1)}, u32[]{:S(2)}, u32[]{:S(2)}) async-start(bf16[32,48,256]{2,1,0:T(8,128)(2,1)} %bitcast.21), calls=%async_computation.1 | async-start | bytes 1572864 | tf_op jit(solution)/shard_map/all_to_all | solution.py:245
  74.4 24.5 %all-to-all-start.2 = ((bf16[32,48,512]{2,1,0:T(8,128)(2,1)}), bf16[32,48,512]{2,1,0:T(8,128)(2,1)S(1)}, u32[]{:S(2)}, u32[]{:S(2)}) async-start(bf16[32,48,512]{2,1,0:T(8,128)(2,1)} %broadcast_in_dim.2), calls=%async_computation.2 | async-start | bytes 3145728 | tf_op jit(solution)/shard_map/all_to_all | solution.py:245
  90.2 2.7 %copy-start = (bf16[12,512,512]{2,1,0:T(8,128)(2,1)}, bf16[12,512,512]{2,1,0:T(8,128)(2,1)S(1)}, u32[]{:S(2)}) copy-start(bf16[12,512,512]{2,1,0:T(8,128)(2,1)S(1)} %values.1.v_h) | copy-start | bytes 18874372
  105.9 7.3 %copy-start.6 = (f32[768]{0:T(1024)S(1)}, f32[768]{0:T(1024)}, u32[]{:S(2)}) copy-start(f32[768]{0:T(1024)} %param.17) | copy-start | bytes 9220
  105.9 26.1 %all-to-all-start.3 = ((bf16[32,32,768]{2,1,0:T(8,128)(2,1)}), bf16[32,32,768]{2,1,0:T(8,128)(2,1)S(1)}, u32[]{:S(2)}, u32[]{:S(2)}) async-start(bf16[32,32,768]{2,1,0:T(8,128)(2,1)} %bitcast.8), calls=%async_computation.3 | async-start | bytes 3145728 | tf_op jit(solution)/shard_map/all_to_all | solution.py:245

commit v4 on v3

--- a/solution.py
+++ b/solution.py
@@ -63,21 +63,27 @@
     for c in copies:
         c.start()
     s, n, f = xa.shape
-    na = norm(xa[...].reshape(s * n, f), g[...])
-    nb = norm(xb[...].reshape(s * n, f), g[...])
-    copies[0].wait()
-
-    def put(ref, rows, y):
-        for j in range(0, s, 2):
+    part = 4
+
+    def put(ref, rows, at, y):
+        for j in range(0, part, 2):
             z = y[j * n : (j + 2) * n]
             for h in range(HEADS):
-                ref[h, rows, j * D : (j + 2) * D] = pair(z, n, h)
-
-    put(ks, slice(0, n), mm(na, wk[...]).astype(BF16))
-    put(ks, slice(n, 2 * n), mm(nb, wk[...]).astype(BF16))
+                ref[h, rows, (at + j) * D : (at + j + 2) * D] = pair(z, n, h)
+
+    own = []
+    for at in range(0, s, part):
+        for i, x in enumerate((xa, xb)):
+            nx = norm(x[at : at + part].reshape(part * n, f), g[...])
+            if i == 0:
+                own.append(nx)
+            if i == 0 and at == 0:
+                copies[0].wait()
+            put(ks, slice(i * n, (i + 1) * n), at, mm(nx, wk[...]).astype(BF16))
     copies[1].wait()
     if first:
-        put(q, slice(0, n), mm(na, wq[...]).astype(BF16))
+        for i, nx in enumerate(own):
+            put(q, slice(0, n), i * part, mm(nx, wq[...]).astype(BF16))
     for h in range(HEADS):
         out[h] = mm_t(q[h], ks[h]).astype(BF16)
 
@@ -209,15 +215,19 @@
             ms[r, c] = (w[:, : 2 * D] / w[:, 2 * D :]).astype(BF16)
         return carry
 
-    lax.fori_loop(0, rows // 8, normed, 0)
-    n = ns[...]
-    copies[0].wait()
-    qs[...] = (mm(n, w[0]) * (1.0 / (math.sqrt(D) * math.log(2.0)))).astype(BF16)
-    copies[1].wait()
-    ks[...] = mm(n, w[1]).astype(BF16)
-    copies[2].wait()
-    vs[...] = mm(n, w[2]).astype(BF16)
-    lax.fori_loop(0, rows // 8, attend, 0)
+    for p in range(rows // 8):
+        r = slice(p * a, (p + 1) * a)
+        n = norm(xs[r], g[...])
+        if p == 0:
+            copies[0].wait()
+        qs[r] = (mm(n, w[0]) * (1.0 / (math.sqrt(D) * math.log(2.0)))).astype(BF16)
+        if p == 0:
+            copies[1].wait()
+        ks[r] = mm(n, w[1]).astype(BF16)
+        if p == 0:
+            copies[2].wait()
+        vs[r] = mm(n, w[2]).astype(BF16)
+    lax.fori_loop(0, rows // 8, attend, 0, unroll=2)
     copies[3].wait()
     xs[...] = xs[...] + mm(ms[...], w[3])
     for i in range(0, rows, 16):
@@ -273,12 +283,11 @@
     xh, mine = barrier((xh, r1[0]))
     xhs = lax.ppermute(xh, "res", CORE_SWAP)
     (l2,) = logits(xh, xhs, hg, wk, q=q)
-    l2, theirs = barrier((l2, r1[1]))
     r2 = jnp.sum(reduce(l2).astype(F32), axis=0)
     x_late, l2 = barrier((x, l2))
     v = values((x_late, sib, xh, xhs), hg, wv)
     scale = 1.0 / (math.sqrt(D) * math.sqrt(S * SEQ))
-    tied = jnp.concatenate([mine + theirs.astype(F32), r2], axis=-1) * scale
+    tied = jnp.concatenate([mine + r1[1].astype(F32), r2], axis=-1) * scale
     probs = jax.nn.softmax(tied, axis=-1).astype(BF16)
     probs = a2a(jnp.broadcast_to(probs[None], (SEQ,) + probs.shape)).reshape(HEADS, N, 4 * N)
     hid = mix(probs, v, x, wo)

time: 176 us -> 174 us (0.989)
    all_to_all x3, waiting for transfers between devices: 36.6 us -> 26 us  [a2a(): return lax.all_to_all(x, 'seq', split_axis=0, concat_axis=0, tiled=True)]
    ppermute x1, waiting for transfers between devices: 0.01 us -> 8.87 us  [reduce_yz(): lax.ppermute(other, 'seq', [(i, (i + half) % SEQ) for i in range(SEQ)])]
    unnamed x14 -> x12, local copies, waits for them, and re-layouts: 5.86 us -> 4.95 us
  transfers between devices with their start and end apart: 8 -> 8, of which waited for: 6 -> 7; matrix products, arithmetic and copies ran while one was open for 2% -> 2% of each run, Pallas kernels for 15% -> 11%
where the time goes in v4:
time: 174 us; the launch traced here: 171 us
  waiting for transfers between devices  51.7 us (30%)
  Pallas kernels  43.4 us (25%)
  starting transfers between devices  35.9 us (21%)
  blocking collectives  26.6 us (15%)
  local copies, waits for them, and re-layouts  12.6 us (7%)
    all_to_all x1, blocking collectives, a2a(): return lax.all_to_all(x, 'seq', split_axis=0, concat_axis=0, tiled=True)  26.6 us
    all_to_all x3, waiting for transfers between devices, a2a(): return lax.all_to_all(x, 'seq', split_axis=0, concat_axis=0, tiled=True)  26 us
    all_to_all x3, starting transfers between devices, a2a(): return lax.all_to_all(x, 'seq', split_axis=0, concat_axis=0, tiled=True)  20.5 us
    pallas_call x2, Pallas kernels, logits(): pl.pallas_call(functools.partial(logits_kernel, first), in_specs=[here, h...  15.8 us
    all_to_all x1, waiting for transfers between devices, reduce_yz(): lax.all_to_all(l, 'seq', split_axis=0, concat_axis=0, tiled=True, axis_in...  12.7 us
    pallas_call x1, Pallas kernels, column(): pl.pallas_call(column_kernel, in_specs=[pl.BlockSpec(memory_space=pltpu.V...  12 us
    pallas_call x1, Pallas kernels, values(): pl.pallas_call(values_kernel, grid=(s // 2,), in_specs=specs + [whole(g.s...  10.5 us
    ppermute x1, waiting for transfers between devices, reduce_yz(): lax.ppermute(other, 'seq', [(i, (i + half) % SEQ) for i in range(SEQ)])  8.87 us
  transfers between devices with their start and end apart: 8, of which 7 were waited for; matrix products, arithmetic and copies ran while one was open for 2% of the time, Pallas kernels for 11%

profile of v4, /device:TPU:1, one launch (start us, length us, event | category | flops | bytes accessed | tf_op | source)
XLA Modules:
  0.0 171.0 jit_solution(2828458274593111)
XLA Ops:
  0.0 1.4 collective-permute-start.1
  1.4 2.8 %collective-permute-start = (bf16[8,128,768]{2,1,0:T(8,128)(2,1)}, bf16[8,128,768]{2,1,0:T(8,128)(2,1)S(1)}, u32[]{:S(2)}, u32[]{:S(2)}) collective-permute-start(bf16[8,128,768]{2,1,0:T(8,128)(2,1)} %x_h.1), channel_id=1, source_target_pairs={{0,2},{1,3},{2,0},{3,1},{4,6},{5,7},{6,4},{7,5},{8,10},{9,11},{10,... | collective-permute-start | bytes 4718600 | tf_op jit(solution)/shard_map/ppermute | solution.py:267
  4.2 1.3 reshape.69.refs_2_.refs_4_
  5.5 1.1 copy-done.4
  6.7 8.6 %logits.2 = (bf16[12,128,512]{2,1,0:T(8,128)(2,1)S(1)}, bf16[12,128,256]{2,1,0:T(8,128)(2,1)S(1)}) custom-call(bf16[8,128,768]{2,1,0:T(8,128)(2,1)} %x_h.1, bf16[8,128,768]{2,1,0:T(8,128)(2,1)} %copy-done.4, f32[1,768]{1,0:T(1,128)} %reshape.69.refs_2_.refs_4_, bf16[768,768]{1,0:T(8,128)(2,1)} %refs_3_.4, bf16[768,768]{1,0:T(8,128)(2,1)} %refs_4_.1), custom_call_target="tpu_custom_call" | custom-call | tf_op jit(solution)/shard_map/logits/pallas_call | solution.py:99
  15.3 1.1 copy-done.3
  16.5 1.0 copy.20
  17.4 7.8 %all-to-all-start = ((bf16[16,2,48,256]{3,2,1,0:T(8,128)(2,1)}), bf16[16,2,48,256]{3,2,1,0:T(8,128)(2,1)S(1)}, u32[]{:S(2)}, u32[]{:S(2)}) async-start(bf16[16,2,48,256]{3,2,1,0:T(8,128)(2,1)} %bitcast.19), calls=%async_computation | async-start | bytes 1572864 | tf_op jit(solution)/shard_map/all_to_all | solution.py:274
  25.2 12.7 %all-to-all-done = bf16[16,2,48,256]{3,2,1,0:T(8,128)(2,1)S(1)} async-done(((bf16[16,2,48,256]{3,2,1,0:T(8,128)(2,1)}), bf16[16,2,48,256]{3,2,1,0:T(8,128)(2,1)S(1)}, u32[]{:S(2)}, u32[]{:S(2)}) %all-to-all-start) | async-done | bytes 786464 | tf_op jit(solution)/shard_map/all_to_all | solution.py:274
  38.0 1.1 collective-permute-done.refs_0_.refs_2_
  39.2 1.9 %collective-permute-start.3 = (bf16[8,128,768]{2,1,0:T(8,128)(2,1)S(1)}, bf16[8,128,768]{2,1,0:T(8,128)(2,1)S(1)}, u32[]{:S(2)}, u32[]{:S(2)}) collective-permute-start(bf16[8,128,768]{2,1,0:T(8,128)(2,1)S(1)} %collective-permute-done.refs_0_.refs_2_), channel_id=1, source_target_pairs={{0,1},{1,0},{2,3},{3,2},{4,5},{5,4},{6,7},{7,6},{8,9},{9,8},{10,11... | collective-permute-start | bytes 4718600 | tf_op jit(solution)/shard_map/ppermute | solution.py:284
  41.0 3.0 %collective-permute-done.3.refs_1_.refs_3_ = bf16[8,128,768]{2,1,0:T(8,128)(2,1)S(1)} collective-permute-done((bf16[8,128,768]{2,1,0:T(8,128)(2,1)S(1)}, bf16[8,128,768]{2,1,0:T(8,128)(2,1)S(1)}, u32[]{:S(2)}, u32[]{:S(2)}) %collective-permute-start.3) | collective-permute-done | bytes 1572896 | tf_op jit(solution)/shard_map/ppermute | solution.py:284
  44.1 7.1 %logits.3 = bf16[12,128,256]{2,1,0:T(8,128)(2,1)} custom-call(bf16[8,128,768]{2,1,0:T(8,128)(2,1)S(1)} %collective-permute-done.refs_0_.refs_2_, bf16[8,128,768]{2,1,0:T(8,128)(2,1)S(1)} %collective-permute-done.3.refs_1_.refs_3_, f32[1,768]{1,0:T(1,128)} %reshape.69.refs_2_.refs_4_, bf16[768,768]{1,0:T(8,128)(2,1)} %refs_3_.4, bf16[12,128,512]{2,1,0:T(8,128)(2,1)} %copy-done.3), custom_call_target="tpu_custom_call" | custom-call | tf_op jit(solution)/shard_map/logits/pallas_call | solution.py:99
  51.2 8.0 %all-to-all-start.1 = ((bf16[32,48,256]{2,1,0:T(8,128)(2,1)}), bf16[32,48,256]{2,1,0:T(8,128)(2,1)S(1)}, u32[]{:S(2)}, u32[]{:S(2)}) async-start(bf16[32,48,256]{2,1,0:T(8,128)(2,1)} %bitcast.4), calls=%async_computation.1 | async-start | bytes 1572864 | tf_op jit(solution)/shard_map/all_to_all | solution.py:255
  59.3 1.5 collective-permute-start.2
  60.8 8.9 %collective-permute-done.2 = bf16[48,256]{1,0:T(8,128)(2,1)S(1)} collective-permute-done((bf16[48,256]{1,0:T(8,128)(2,1)S(1)}, bf16[48,256]{1,0:T(8,128)(2,1)S(1)}, u32[]{:S(2)}, u32[]{:S(2)}) %collective-permute-start.2) | collective-permute-done | bytes 24608 | tf_op jit(solution)/shard_map/ppermute | solution.py:279
  69.6 2.0 %all-to-all-done.1 = bf16[32,48,256]{2,1,0:T(8,128)(2,1)S(1)} async-done(((bf16[32,48,256]{2,1,0:T(8,128)(2,1)}), bf16[32,48,256]{2,1,0:T(8,128)(2,1)S(1)}, u32[]{:S(2)}, u32[]{:S(2)}) %all-to-all-start.1) | async-done | bytes 786464 | tf_op jit(solution)/shard_map/all_to_all | solution.py:255
  71.7 0.1 convert_reduce_fusion
  71.9 0.2 fusion
  72.2 1.3 broadcast_in_dim.2
  73.5 5.2 %all-to-all-start.2 = ((bf16[32,48,512]{2,1,0:T(8,128)(2,1)}), bf16[32,48,512]{2,1,0:T(8,128)(2,1)S(1)}, u32[]{:S(2)}, u32[]{:S(2)}) async-start(bf16[32,48,512]{2,1,0:T(8,128)(2,1)} %broadcast_in_dim.2), calls=%async_computation.2 | async-start | bytes 3145728 | tf_op jit(solution)/shard_map/all_to_all | solution.py:255
  78.7 10.5 %values.1.v_h = bf16[12,512,512]{2,1,0:T(8,128)(2,1)S(1)} custom-call(bf16[8,128,768]{2,1,0:T(8,128)(2,1)} %x_h.1, bf16[8,128,768]{2,1,0:T(8,128)(2,1)} %copy-done.4, bf16[8,128,768]{2,1,0:T(8,128)(2,1)} %copy-done.1, bf16[8,128,768]{2,1,0:T(8,128)(2,1)} %copy-done.2, f32[1,768]{1,0:T(1,128)} %reshape.69.refs_2_.refs_4_, bf16[768,768]{1,0:T(8,128)(2,1)} %refs_5_.1), custom_call_target="tpu_custom_call" | custom-call | tf_op jit(solution)/shard_map/values/pallas_call | solution.py:130
  89.3 2.6 %copy-done = bf16[12,512,512]{2,1,0:T(8,128)(2,1)} copy-done((bf16[12,512,512]{2,1,0:T(8,128)(2,1)}, bf16[12,512,512]{2,1,0:T(8,128)(2,1)S(1)}, u32[]{:S(2)}) %copy-start) | copy-done | bytes 6291480
  91.9 5.9 %all-to-all-done.2 = bf16[32,48,512]{2,1,0:T(8,128)(2,1)S(1)} async-done(((bf16[32,48,512]{2,1,0:T(8,128)(2,1)}), bf16[32,48,512]{2,1,0:T(8,128)(2,1)S(1)}, u32[]{:S(2)}, u32[]{:S(2)}) %all-to-all-start.2) | async-done | bytes 1572896 | tf_op jit(solution)/shard_map/all_to_all | solution.py:255
  97.8 5.1 %mix.1 = bf16[8,128,768]{2,1,0:T(8,128)(2,1)S(1)} custom-call(bf16[12,128,512]{2,1,0:T(8,128)(2,1)S(1)} %bitcast.20, bf16[12,512,512]{2,1,0:T(8,128)(2,1)} %copy-done, bf16[8,128,768]{2,1,0:T(8,128)(2,1)} %x_h.1, bf16[768,768]{1,0:T(8,128)(2,1)} %wo_h.1), custom_call_target="tpu_custom_call" | custom-call | tf_op jit(solution)/shard_map/mix/pallas_call | solution.py:165
  102.9 2.0 %copy.17 = bf16[8,128,768]{2,0,1:T(8,128)(2,1)} copy(bf16[8,128,768]{2,1,0:T(8,128)(2,1)S(1)} %mix.1) | data formatting | bytes 3145728 | tf_op jit(solution)/shard_map/reshape | solution.py:295
  104.9 7.3 %all-to-all-start.3 = ((bf16[32,32,768]{2,1,0:T(8,128)(2,1)}), bf16[32,32,768]{2,1,0:T(8,128)(2,1)S(1)}, u32[]{:S(2)}, u32[]{:S(2)}) async-start(bf16[32,32,768]{2,1,0:T(8,128)(2,1)} %bitcast.8), calls=%async_computation.3 | async-start | bytes 3145728 | tf_op jit(solution)/shard_map/all_to_all | solution.py:255
  112.2 0.6 reshape.75.g
  112.8 18.1 %all-to-all-done.3.h_ref = bf16[32,32,768]{2,1,0:T(8,128)(2,1)S(1)} async-done(((bf16[32,32,768]{2,1,0:T(8,128)(2,1)}), bf16[32,32,768]{2,1,0:T(8,128)(2,1)S(1)}, u32[]{:S(2)}, u32[]{:S(2)}) %all-to-all-start.3) | async-done | bytes 1572896 | tf_op jit(solution)/shard_map/all_to_all | solution.py:255
  130.9 12.0 %column.1 = bf16[32,32,768]{2,1,0:T(8,128)(2,1)S(1)} custom-call(bf16[32,32,768]{2,1,0:T(8,128)(2,1)S(1)} %all-to-all-done.3.h_ref, f32[1,768]{1,0:T(1,128)} %reshape.75.g, bf16[768,768]{1,0:T(8,128)(2,1)} %refs_0_.4, bf16[768,768]{1,0:T(8,128)(2,1)} %refs_1_.1, bf16[768,768]{1,0:T(8,128)(2,1)} %refs_2_.1, bf16[768,768]{1,0:T(8,128)(2,1)} %refs_3_.5), custom_call_target="tpu_custom_call" | custom-call | tf_op jit(solution)/shard_map/column/pallas_call | solution.py:241
  143.0 26.6 %all_to_all.25 = bf16[32,32,768]{2,1,0:T(8,128)(2,1)S(1)} all-to-all(bf16[32,32,768]{2,1,0:T(8,128)(2,1)S(1)} %column.1), channel_id=1, replica_groups=mesh['seq'=32,'res'=4] {'seq'}, dimensions={0} | all-to-all | bytes 3145728 | tf_op jit(solution)/shard_map/all_to_all | solution.py:255
  169.6 1.4 copy.18
  (16 shorter events, 0.4 us)
Async XLA Ops:
  0.0 5.5 %collective-permute-start.1 = (bf16[8,128,768]{2,1,0:T(8,128)(2,1)}, bf16[8,128,768]{2,1,0:T(8,128)(2,1)S(1)}, u32[]{:S(2)}, u32[]{:S(2)}) collective-permute-start(bf16[8,128,768]{2,1,0:T(8,128)(2,1)} %x_h.1), channel_id=1, source_target_pairs={{0,1},{1,0},{2,3},{3,2},{4,5},{5,4},{6,7},{7,6},{8,9},{9,8},{10,11... | collective-permute-start | bytes 4718600 | tf_op jit(solution)/shard_map/ppermute | solution.py:268
  1.4 37.7 %collective-permute-start = (bf16[8,128,768]{2,1,0:T(8,128)(2,1)}, bf16[8,128,768]{2,1,0:T(8,128)(2,1)S(1)}, u32[]{:S(2)}, u32[]{:S(2)}) collective-permute-start(bf16[8,128,768]{2,1,0:T(8,128)(2,1)} %x_h.1), channel_id=1, source_target_pairs={{0,2},{1,3},{2,0},{3,1},{4,6},{5,7},{6,4},{7,5},{8,10},{9,11},{10,... | collective-permute-start | bytes 4718600 | tf_op jit(solution)/shard_map/ppermute | solution.py:267
  5.5 1.1 copy-start.4
  15.3 1.2 copy-start.3
  17.4 20.5 %all-to-all-start = ((bf16[16,2,48,256]{3,2,1,0:T(8,128)(2,1)}), bf16[16,2,48,256]{3,2,1,0:T(8,128)(2,1)S(1)}, u32[]{:S(2)}, u32[]{:S(2)}) async-start(bf16[16,2,48,256]{3,2,1,0:T(8,128)(2,1)} %bitcast.19), calls=%async_computation | async-start | bytes 1572864 | tf_op jit(solution)/shard_map/all_to_all | solution.py:274
  39.2 12.1 %copy-start.1 = (bf16[8,128,768]{2,1,0:T(8,128)(2,1)}, bf16[8,128,768]{2,1,0:T(8,128)(2,1)S(1)}, u32[]{:S(2)}) copy-start(bf16[8,128,768]{2,1,0:T(8,128)(2,1)S(1)} %collective-permute-done.refs_0_.refs_2_) | copy-start | bytes 4718596
  39.2 4.9 %collective-permute-start.3 = (bf16[8,128,768]{2,1,0:T(8,128)(2,1)S(1)}, bf16[8,128,768]{2,1,0:T(8,128)(2,1)S(1)}, u32[]{:S(2)}, u32[]{:S(2)}) collective-permute-start(bf16[8,128,768]{2,1,0:T(8,128)(2,1)S(1)} %collective-permute-done.refs_0_.refs_2_), channel_id=1, source_target_pairs={{0,1},{1,0},{2,3},{3,2},{4,5},{5,4},{6,7},{7,6},{8,9},{9,8},{10,11... | collective-permute-start | bytes 4718600 | tf_op jit(solution)/shard_map/ppermute | solution.py:284
  44.1 7.2 %copy-start.2 = (bf16[8,128,768]{2,1,0:T(8,128)(2,1)}, bf16[8,128,768]{2,1,0:T(8,128)(2,1)S(1)}, u32[]{:S(2)}) copy-start(bf16[8,128,768]{2,1,0:T(8,128)(2,1)S(1)} %collective-permute-done.3.refs_1_.refs_3_) | copy-start | bytes 4718596
  51.2 20.4 %all-to-all-start.1 = ((bf16[32,48,256]{2,1,0:T(8,128)(2,1)}), bf16[32,48,256]{2,1,0:T(8,128)(2,1)S(1)}, u32[]{:S(2)}, u32[]{:S(2)}) async-start(bf16[32,48,256]{2,1,0:T(8,128)(2,1)} %bitcast.4), calls=%async_computation.1 | async-start | bytes 1572864 | tf_op jit(solution)/shard_map/all_to_all | solution.py:255
  59.3 10.4 %collective-permute-start.2 = (bf16[48,256]{1,0:T(8,128)(2,1)S(1)}, bf16[48,256]{1,0:T(8,128)(2,1)S(1)}, u32[]{:S(2)}, u32[]{:S(2)}) collective-permute-start(bf16[48,256]{1,0:T(8,128)(2,1)S(1)} %fusion.2), channel_id=1, source_target_pairs={{0,64},{4,68},{8,72},{12,76},{16,80},{20,84},{24,88},{28,92},{32,9... | collective-permute-start | bytes 73736 | tf_op jit(solution)/shard_map/ppermute | solution.py:279
  73.5 24.3 %all-to-all-start.2 = ((bf16[32,48,512]{2,1,0:T(8,128)(2,1)}), bf16[32,48,512]{2,1,0:T(8,128)(2,1)S(1)}, u32[]{:S(2)}, u32[]{:S(2)}) async-start(bf16[32,48,512]{2,1,0:T(8,128)(2,1)} %broadcast_in_dim.2), calls=%async_computation.2 | async-start | bytes 3145728 | tf_op jit(solution)/shard_map/all_to_all | solution.py:255
  89.3 2.7 %copy-start = (bf16[12,512,512]{2,1,0:T(8,128)(2,1)}, bf16[12,512,512]{2,1,0:T(8,128)(2,1)S(1)}, u32[]{:S(2)}) copy-start(bf16[12,512,512]{2,1,0:T(8,128)(2,1)S(1)} %values.1.v_h) | copy-start | bytes 18874372
  104.9 7.4 %copy-start.5 = (f32[768]{0:T(1024)S(1)}, f32[768]{0:T(1024)}, u32[]{:S(2)}) copy-start(f32[768]{0:T(1024)} %param.17) | copy-start | bytes 9220
  104.9 26.1 %all-to-all-start.3 = ((bf16[32,32,768]{2,1,0:T(8,128)(2,1)}), bf16[32,32,768]{2,1,0:T(8,128)(2,1)S(1)}, u32[]{:S(2)}, u32[]{:S(2)}) async-start(bf16[32,32,768]{2,1,0:T(8,128)(2,1)} %bitcast.8), calls=%async_computation.3 | async-start | bytes 3145728 | tf_op jit(solution)/shard_map/all_to_all | solution.py:255

commit v5 on v4

--- a/solution.py
+++ b/solution.py
@@ -283,6 +283,11 @@
     xh, mine = barrier((xh, r1[0]))
     xhs = lax.ppermute(xh, "res", CORE_SWAP)
     (l2,) = logits(xh, xhs, hg, wk, q=q)
+    def late(l):
+        early = values((x, sib, xh, xhs), hg, wv)
+        return l + early[0, 0, 0] * 0
+
+    l2 = lax.cond(lax.axis_index("res") % 2 == 1, late, lambda l: l, l2)
     r2 = jnp.sum(reduce(l2).astype(F32), axis=0)
     x_late, l2 = barrier((x, l2))
     v = values((x_late, sib, xh, xhs), hg, wv)

time: 174 us -> 167 us (0.960); the launches traced: 171 us -> 166 us
  waiting for transfers between devices: 51.7 us -> 39.5 us
  Pallas kernels: 43.4 us -> 55.2 us
  blocking collectives: 26.6 us -> 19.2 us
  other arithmetic: 0.65 us -> 2.74 us
    pallas_call x1 -> x2, Pallas kernels: 10.5 us -> 21.1 us  [values(): pl.pallas_call(values_kernel, grid=(s // 2,), in_specs=specs + [whole(g.s...]
    all_to_all x3, waiting for transfers between devices: 26 us -> 16.9 us  [a2a(): return lax.all_to_all(x, 'seq', split_axis=0, concat_axis=0, tiled=True)]
    all_to_all x1, blocking collectives: 26.6 us -> 19.2 us  [a2a(): return lax.all_to_all(x, 'seq', split_axis=0, concat_axis=0, tiled=True)]
    ppermute x1, waiting for transfers between devices: 8.87 us -> 5.41 us  [reduce_yz(): lax.ppermute(other, 'seq', [(i, (i + half) % SEQ) for i in range(SEQ)])]
    add x0 -> x1, other arithmetic: none -> 2.09 us  [late(): return l + early[0, 0, 0] * 0]
    unnamed x12 -> x8, local copies, waits for them, and re-layouts: 4.95 us -> 4.94 us
  transfers between devices with their start and end apart: 8 -> 8, of which waited for: 7 -> 7; matrix products, arithmetic and copies ran while one was open for 2% -> 2% of each run, Pallas kernels for 11% -> 12%
where the time goes in v5:
time: 167 us; the launch traced here: 166 us
  Pallas kernels  55.2 us (33%)
  waiting for transfers between devices  39.5 us (24%)
  starting transfers between devices  35.2 us (21%)
  blocking collectives  19.2 us (11%)
  local copies, waits for them, and re-layouts  13.1 us (8%)
  other arithmetic  2.74 us (2%)
    pallas_call x2, Pallas kernels, values(): pl.pallas_call(values_kernel, grid=(s // 2,), in_specs=specs + [whole(g.s...  21.1 us
    all_to_all x3, starting transfers between devices, a2a(): return lax.all_to_all(x, 'seq', split_axis=0, concat_axis=0, tiled=True)  20.1 us
    all_to_all x1, blocking collectives, a2a(): return lax.all_to_all(x, 'seq', split_axis=0, concat_axis=0, tiled=True)  19.2 us
    pallas_call x2, Pallas kernels, logits(): pl.pallas_call(functools.partial(logits_kernel, first), in_specs=[here, h...  17 us
    all_to_all x3, waiting for transfers between devices, a2a(): return lax.all_to_all(x, 'seq', split_axis=0, concat_axis=0, tiled=True)  16.9 us
    all_to_all x1, waiting for transfers between devices, reduce_yz(): lax.all_to_all(l, 'seq', split_axis=0, concat_axis=0, tiled=True, axis_in...  12.7 us
    pallas_call x1, Pallas kernels, column(): pl.pallas_call(column_kernel, in_specs=[pl.BlockSpec(memory_space=pltpu.V...  12 us
    all_to_all x1, starting transfers between devices, reduce_yz(): lax.all_to_all(l, 'seq', split_axis=0, concat_axis=0, tiled=True, axis_in...  7.77 us
  transfers between devices with their start and end apart: 8, of which 7 were waited for; matrix products, arithmetic and copies ran while one was open for 2% of the time, Pallas kernels for 12%

profile of v5, /device:TPU:1, one launch (start us, length us, event | category | flops | bytes accessed | tf_op | source)
XLA Modules:
  0.0 165.8 jit_solution(10619125705220694882)
XLA Ops:
  0.0 1.4 collective-permute-start.1
  1.4 2.8 %collective-permute-start = (bf16[8,128,768]{2,1,0:T(8,128)(2,1)}, bf16[8,128,768]{2,1,0:T(8,128)(2,1)}, u32[]{:S(2)}, u32[]{:S(2)}) collective-permute-start(bf16[8,128,768]{2,1,0:T(8,128)(2,1)} %x_h.1), channel_id=1, source_target_pairs={{0,2},{1,3},{2,0},{3,1},{4,6},{5,7},{6,4},{7,5},{8,10},{9,11},{10,... | collective-permute-start | bytes 4718600 | tf_op jit(solution)/shard_map/ppermute | solution.py:267
  4.2 1.3 reshape.71.refs_2_.refs_4_
  5.5 1.1 copy-done.2
  6.7 8.6 %logits.2 = (bf16[12,128,512]{2,1,0:T(8,128)(2,1)S(1)}, bf16[12,128,256]{2,1,0:T(8,128)(2,1)S(1)}) custom-call(bf16[8,128,768]{2,1,0:T(8,128)(2,1)} %x_h.1, bf16[8,128,768]{2,1,0:T(8,128)(2,1)} %copy-done.2, f32[1,768]{1,0:T(1,128)} %reshape.71.refs_2_.refs_4_, bf16[768,768]{1,0:T(8,128)(2,1)} %refs_3_.4, bf16[768,768]{1,0:T(8,128)(2,1)} %refs_4_.1), custom_call_target="tpu_custom_call" | custom-call | tf_op jit(solution)/shard_map/logits/pallas_call | solution.py:99
  15.3 1.1 copy-done.1
  16.5 1.0 copy.20
  17.5 7.8 %all-to-all-start = ((bf16[16,2,48,256]{3,2,1,0:T(8,128)(2,1)}), bf16[16,2,48,256]{3,2,1,0:T(8,128)(2,1)S(1)}, u32[]{:S(2)}, u32[]{:S(2)}) async-start(bf16[16,2,48,256]{3,2,1,0:T(8,128)(2,1)} %bitcast.20), calls=%async_computation | async-start | bytes 1572864 | tf_op jit(solution)/shard_map/all_to_all | solution.py:274
  25.3 12.7 %all-to-all-done = bf16[16,2,48,256]{3,2,1,0:T(8,128)(2,1)S(1)} async-done(((bf16[16,2,48,256]{3,2,1,0:T(8,128)(2,1)}), bf16[16,2,48,256]{3,2,1,0:T(8,128)(2,1)S(1)}, u32[]{:S(2)}, u32[]{:S(2)}) %all-to-all-start) | async-done | bytes 786464 | tf_op jit(solution)/shard_map/all_to_all | solution.py:274
  38.0 1.2 collective-permute-done.refs_0_.refs_2_
  39.3 1.8 %collective-permute-start.3 = (bf16[8,128,768]{2,1,0:T(8,128)(2,1)}, bf16[8,128,768]{2,1,0:T(8,128)(2,1)}, u32[]{:S(2)}, u32[]{:S(2)}) collective-permute-start(bf16[8,128,768]{2,1,0:T(8,128)(2,1)} %collective-permute-done.refs_0_.refs_2_), channel_id=1, source_target_pairs={{0,1},{1,0},{2,3},{3,2},{4,5},{5,4},{6,7},{7,6},{8,9},{9,8},{10,11... | collective-permute-start | bytes 4718600 | tf_op jit(solution)/shard_map/ppermute | solution.py:284
  41.0 3.4 %collective-permute-done.3.refs_1_.refs_3_ = bf16[8,128,768]{2,1,0:T(8,128)(2,1)} collective-permute-done((bf16[8,128,768]{2,1,0:T(8,128)(2,1)}, bf16[8,128,768]{2,1,0:T(8,128)(2,1)}, u32[]{:S(2)}, u32[]{:S(2)}) %collective-permute-start.3) | collective-permute-done | bytes 1572896 | tf_op jit(solution)/shard_map/ppermute | solution.py:284
  44.4 8.3 %logits.3 = bf16[12,128,256]{2,1,0:T(8,128)(2,1)} custom-call(bf16[8,128,768]{2,1,0:T(8,128)(2,1)} %collective-permute-done.refs_0_.refs_2_, bf16[8,128,768]{2,1,0:T(8,128)(2,1)} %collective-permute-done.3.refs_1_.refs_3_, f32[1,768]{1,0:T(1,128)} %reshape.71.refs_2_.refs_4_, bf16[768,768]{1,0:T(8,128)(2,1)} %refs_3_.4, bf16[12,128,512]{2,1,0:T(8,128)(2,1)} %copy-done.1), custom_call_target="tpu_custom_call" | custom-call | tf_op jit(solution)/shard_map/logits/pallas_call | solution.py:99
  52.8 13.9 %conditional.1 = (bf16[12,128,256]{2,1,0:T(8,128)(2,1)}) conditional(s32[]{:T(128)} %convert_element_type.29, bf16[12,128,256]{2,1,0:T(8,128)(2,1)} %logits.3, (bf16[8,128,768]{2,1,0:T(8,128)(2,1)}, bf16[8,128,768]{2,1,0:T(8,128)(2,1)}, bf16[8,128,768]{2,1,0:T(8,128)(2,1)}, bf16[8,128,768]{2,1,0:T(8,128)(2,1)}, f32[1,768]{1,0:T(1,128)}, ...), branch_computations={%region_1.2_spmd, %region_2.3_spmd} | conditional | flops 393217 | bytes 1572884 | solution.py:290
  53.0 10.5 %values.2 = bf16[12,512,512]{2,1,0:T(8,128)(2,1)S(1)} custom-call(bf16[8,128,768]{2,1,0:T(8,128)(2,1)} %get-tuple-element.24.refs_0_, bf16[8,128,768]{2,1,0:T(8,128)(2,1)} %get-tuple-element.25.refs_1_, bf16[8,128,768]{2,1,0:T(8,128)(2,1)} %get-tuple-element.26.refs_2_, bf16[8,128,768]{2,1,0:T(8,128)(2,1)} %get-tuple-element.27.refs_3_, ...), custom_call_target="tpu_custom_call" | custom-call | tf_op jit(solution)/shard_map/cond/branch_1_fun/values/pallas_call | solution.py:130
  64.6 2.1 %broadcast_add_fusion = bf16[12,128,256]{2,1,0:T(8,128)(2,1)} fusion(bf16[12,128,256]{2,1,0:T(8,128)(2,1)} %get-tuple-element.23, bf16[]{:T(256)} %bitcast), kind=kLoop, calls=%fused_computation | loop fusion | flops 393216 | bytes 1572866 | tf_op jit(solution)/shard_map/cond/branch_1_fun/add | solution.py:288
  66.7 8.1 %all-to-all-start.1 = ((bf16[32,48,256]{2,1,0:T(8,128)(2,1)}), bf16[32,48,256]{2,1,0:T(8,128)(2,1)S(1)}, u32[]{:S(2)}, u32[]{:S(2)}) async-start(bf16[32,48,256]{2,1,0:T(8,128)(2,1)} %bitcast.5), calls=%async_computation.1 | async-start | bytes 1572864 | tf_op jit(solution)/shard_map/all_to_all | solution.py:255
  74.8 1.3 collective-permute-start.2
  76.2 5.4 %collective-permute-done.2 = bf16[48,256]{1,0:T(8,128)(2,1)S(1)} collective-permute-done((bf16[48,256]{1,0:T(8,128)(2,1)S(1)}, bf16[48,256]{1,0:T(8,128)(2,1)S(1)}, u32[]{:S(2)}, u32[]{:S(2)}) %collective-permute-start.2) | collective-permute-done | bytes 24608 | tf_op jit(solution)/shard_map/ppermute | solution.py:279
  81.6 3.2 %all-to-all-done.1 = bf16[32,48,256]{2,1,0:T(8,128)(2,1)S(1)} async-done(((bf16[32,48,256]{2,1,0:T(8,128)(2,1)}), bf16[32,48,256]{2,1,0:T(8,128)(2,1)S(1)}, u32[]{:S(2)}, u32[]{:S(2)}) %all-to-all-start.1) | async-done | bytes 786464 | tf_op jit(solution)/shard_map/all_to_all | solution.py:255
  85.4 1.3 broadcast_in_dim.2
  86.7 4.5 %all-to-all-start.2 = ((bf16[32,48,512]{2,1,0:T(8,128)(2,1)}), bf16[32,48,512]{2,1,0:T(8,128)(2,1)S(1)}, u32[]{:S(2)}, u32[]{:S(2)}) async-start(bf16[32,48,512]{2,1,0:T(8,128)(2,1)} %broadcast_in_dim.2), calls=%async_computation.2 | async-start | bytes 3145728 | tf_op jit(solution)/shard_map/all_to_all | solution.py:255
  91.2 10.6 %values.3.v_h = bf16[12,512,512]{2,1,0:T(8,128)(2,1)S(1)} custom-call(bf16[8,128,768]{2,1,0:T(8,128)(2,1)} %x_h.1, bf16[8,128,768]{2,1,0:T(8,128)(2,1)} %copy-done.2, bf16[8,128,768]{2,1,0:T(8,128)(2,1)} %collective-permute-done.refs_0_.refs_2_, bf16[8,128,768]{2,1,0:T(8,128)(2,1)} %collective-permute-done.3.refs_1_.refs_3_, ...), custom_call_target="tpu_custom_call" | custom-call | tf_op jit(solution)/shard_map/values/pallas_call | solution.py:130
  101.8 2.6 %copy-done = bf16[12,512,512]{2,1,0:T(8,128)(2,1)} copy-done((bf16[12,512,512]{2,1,0:T(8,128)(2,1)}, bf16[12,512,512]{2,1,0:T(8,128)(2,1)S(1)}, u32[]{:S(2)}) %copy-start) | copy-done | bytes 6291480
  104.4 0.6 all-to-all-done.2
  105.0 5.1 %mix.1 = bf16[8,128,768]{2,1,0:T(8,128)(2,1)S(1)} custom-call(bf16[12,128,512]{2,1,0:T(8,128)(2,1)S(1)} %bitcast.21, bf16[12,512,512]{2,1,0:T(8,128)(2,1)} %copy-done, bf16[8,128,768]{2,1,0:T(8,128)(2,1)} %x_h.1, bf16[768,768]{1,0:T(8,128)(2,1)} %wo_h.1), custom_call_target="tpu_custom_call" | custom-call | tf_op jit(solution)/shard_map/mix/pallas_call | solution.py:165
  110.1 2.0 %copy.17 = bf16[8,128,768]{2,0,1:T(8,128)(2,1)} copy(bf16[8,128,768]{2,1,0:T(8,128)(2,1)S(1)} %mix.1) | data formatting | bytes 3145728 | tf_op jit(solution)/shard_map/reshape | solution.py:300
  112.1 7.5 %all-to-all-start.3 = ((bf16[32,32,768]{2,1,0:T(8,128)(2,1)}), bf16[32,32,768]{2,1,0:T(8,128)(2,1)S(1)}, u32[]{:S(2)}, u32[]{:S(2)}) async-start(bf16[32,32,768]{2,1,0:T(8,128)(2,1)} %bitcast.9), calls=%async_computation.3 | async-start | bytes 3145728 | tf_op jit(solution)/shard_map/all_to_all | solution.py:255
  120.2 13.0 %all-to-all-done.3.h_ref = bf16[32,32,768]{2,1,0:T(8,128)(2,1)S(1)} async-done(((bf16[32,32,768]{2,1,0:T(8,128)(2,1)}), bf16[32,32,768]{2,1,0:T(8,128)(2,1)S(1)}, u32[]{:S(2)}, u32[]{:S(2)}) %all-to-all-start.3) | async-done | bytes 1572896 | tf_op jit(solution)/shard_map/all_to_all | solution.py:255
  133.2 12.0 %column.1 = bf16[32,32,768]{2,1,0:T(8,128)(2,1)S(1)} custom-call(bf16[32,32,768]{2,1,0:T(8,128)(2,1)S(1)} %all-to-all-done.3.h_ref, f32[1,768]{1,0:T(1,128)} %reshape.77.g, bf16[768,768]{1,0:T(8,128)(2,1)} %refs_0_.4, bf16[768,768]{1,0:T(8,128)(2,1)} %refs_1_.1, bf16[768,768]{1,0:T(8,128)(2,1)} %refs_2_.1, bf16[768,768]{1,0:T(8,128)(2,1)} %refs_3_.5), custom_call_target="tpu_custom_call" | custom-call | tf_op jit(solution)/shard_map/column/pallas_call | solution.py:241
  145.2 19.2 %all_to_all.25 = bf16[32,32,768]{2,1,0:T(8,128)(2,1)S(1)} all-to-all(bf16[32,32,768]{2,1,0:T(8,128)(2,1)S(1)} %column.1), channel_id=1, replica_groups=mesh['seq'=32,'res'=4] {'seq'}, dimensions={0} | all-to-all | bytes 3145728 | tf_op jit(solution)/shard_map/all_to_all | solution.py:255
  164.4 1.4 copy.18
  (16 shorter events, 1.8 us)
Async XLA Ops:
  0.0 5.5 %collective-permute-start.1 = (bf16[8,128,768]{2,1,0:T(8,128)(2,1)}, bf16[8,128,768]{2,1,0:T(8,128)(2,1)S(1)}, u32[]{:S(2)}, u32[]{:S(2)}) collective-permute-start(bf16[8,128,768]{2,1,0:T(8,128)(2,1)} %x_h.1), channel_id=1, source_target_pairs={{0,1},{1,0},{2,3},{3,2},{4,5},{5,4},{6,7},{7,6},{8,9},{9,8},{10,11... | collective-permute-start | bytes 4718600 | tf_op jit(solution)/shard_map/ppermute | solution.py:268
  1.4 37.8 %collective-permute-start = (bf16[8,128,768]{2,1,0:T(8,128)(2,1)}, bf16[8,128,768]{2,1,0:T(8,128)(2,1)}, u32[]{:S(2)}, u32[]{:S(2)}) collective-permute-start(bf16[8,128,768]{2,1,0:T(8,128)(2,1)} %x_h.1), channel_id=1, source_target_pairs={{0,2},{1,3},{2,0},{3,1},{4,6},{5,7},{6,4},{7,5},{8,10},{9,11},{10,... | collective-permute-start | bytes 4718600 | tf_op jit(solution)/shard_map/ppermute | solution.py:267
  5.5 1.1 copy-start.2
  15.3 1.2 copy-start.1
  17.5 20.5 %all-to-all-start = ((bf16[16,2,48,256]{3,2,1,0:T(8,128)(2,1)}), bf16[16,2,48,256]{3,2,1,0:T(8,128)(2,1)S(1)}, u32[]{:S(2)}, u32[]{:S(2)}) async-start(bf16[16,2,48,256]{3,2,1,0:T(8,128)(2,1)} %bitcast.20), calls=%async_computation | async-start | bytes 1572864 | tf_op jit(solution)/shard_map/all_to_all | solution.py:274
  39.3 5.1 %collective-permute-start.3 = (bf16[8,128,768]{2,1,0:T(8,128)(2,1)}, bf16[8,128,768]{2,1,0:T(8,128)(2,1)}, u32[]{:S(2)}, u32[]{:S(2)}) collective-permute-start(bf16[8,128,768]{2,1,0:T(8,128)(2,1)} %collective-permute-done.refs_0_.refs_2_), channel_id=1, source_target_pairs={{0,1},{1,0},{2,3},{3,2},{4,5},{5,4},{6,7},{7,6},{8,9},{9,8},{10,11... | collective-permute-start | bytes 4718600 | tf_op jit(solution)/shard_map/ppermute | solution.py:284
  66.7 18.1 %all-to-all-start.1 = ((bf16[32,48,256]{2,1,0:T(8,128)(2,1)}), bf16[32,48,256]{2,1,0:T(8,128)(2,1)S(1)}, u32[]{:S(2)}, u32[]{:S(2)}) async-start(bf16[32,48,256]{2,1,0:T(8,128)(2,1)} %bitcast.5), calls=%async_computation.1 | async-start | bytes 1572864 | tf_op jit(solution)/shard_map/all_to_all | solution.py:255
  74.8 6.7 %collective-permute-start.2 = (bf16[48,256]{1,0:T(8,128)(2,1)S(1)}, bf16[48,256]{1,0:T(8,128)(2,1)S(1)}, u32[]{:S(2)}, u32[]{:S(2)}) collective-permute-start(bf16[48,256]{1,0:T(8,128)(2,1)S(1)} %fusion.2), channel_id=1, source_target_pairs={{0,64},{4,68},{8,72},{12,76},{16,80},{20,84},{24,88},{28,92},{32,9... | collective-permute-start | bytes 73736 | tf_op jit(solution)/shard_map/ppermute | solution.py:279
  86.7 18.3 %all-to-all-start.2 = ((bf16[32,48,512]{2,1,0:T(8,128)(2,1)}), bf16[32,48,512]{2,1,0:T(8,128)(2,1)S(1)}, u32[]{:S(2)}, u32[]{:S(2)}) async-start(bf16[32,48,512]{2,1,0:T(8,128)(2,1)} %broadcast_in_dim.2), calls=%async_computation.2 | async-start | bytes 3145728 | tf_op jit(solution)/shard_map/all_to_all | solution.py:255
  101.7 2.7 %copy-start = (bf16[12,512,512]{2,1,0:T(8,128)(2,1)}, bf16[12,512,512]{2,1,0:T(8,128)(2,1)S(1)}, u32[]{:S(2)}) copy-start(bf16[12,512,512]{2,1,0:T(8,128)(2,1)S(1)} %values.3.v_h) | copy-start | bytes 18874372
  112.1 7.5 %copy-start.3 = (f32[768]{0:T(1024)S(1)}, f32[768]{0:T(1024)}, u32[]{:S(2)}) copy-start(f32[768]{0:T(1024)} %param.19) | copy-start | bytes 9220
  112.1 21.1 %all-to-all-start.3 = ((bf16[32,32,768]{2,1,0:T(8,128)(2,1)}), bf16[32,32,768]{2,1,0:T(8,128)(2,1)S(1)}, u32[]{:S(2)}, u32[]{:S(2)}) async-start(bf16[32,32,768]{2,1,0:T(8,128)(2,1)} %bitcast.9), calls=%async_computation.3 | async-start | bytes 3145728 | tf_op jit(solution)/shard_map/all_to_all | solution.py:255

commit v6 on v4

--- a/solution.py
+++ b/solution.py
@@ -132,7 +132,7 @@
         grid=(s // 2,),
         in_specs=specs + [whole(g.shape), whole(wv.shape)],
         out_specs=pl.BlockSpec((HEADS, total, 2 * D), lambda t: (0, 0, t)),
-        out_shape=jax.ShapeDtypeStruct((HEADS, total, s * D), BF16),
+        out_shape=pltpu.HBM((HEADS, total, s * D), BF16),
         compiler_params=PARAMS,
         name="values",
     )(*far(*pieces, g, wv))
@@ -283,11 +283,16 @@
     xh, mine = barrier((xh, r1[0]))
     xhs = lax.ppermute(xh, "res", CORE_SWAP)
     (l2,) = logits(xh, xhs, hg, wk, q=q)
+    odd = lax.axis_index("res") % 2 == 1
+    early = lax.cond(
+        odd, lambda l: values((x, sib, xh, xhs), hg, wv)[0, 0, 0] + l * 0, lambda l: jnp.zeros_like(l), l2[0, 0, 0]
+    )
+    l2, early = barrier((l2, early))
     r2 = jnp.sum(reduce(l2).astype(F32), axis=0)
     x_late, l2 = barrier((x, l2))
     v = values((x_late, sib, xh, xhs), hg, wv)
     scale = 1.0 / (math.sqrt(D) * math.sqrt(S * SEQ))
-    tied = jnp.concatenate([mine + r1[1].astype(F32), r2], axis=-1) * scale
+    tied = jnp.concatenate([mine + r1[1].astype(F32), r2 + early.astype(F32) * 0], axis=-1) * scale
     probs = jax.nn.softmax(tied, axis=-1).astype(BF16)
     probs = a2a(jnp.broadcast_to(probs[None], (SEQ,) + probs.shape)).reshape(HEADS, N, 4 * N)
     hid = mix(probs, v, x, wo)

time: 174 us -> 166 us (0.954); the launches traced: 171 us -> 165 us
  Pallas kernels: 43.4 us -> 55.5 us
  waiting for transfers between devices: 51.7 us -> 42 us
  blocking collectives: 26.6 us -> 19.2 us
  starting transfers between devices: 35.9 us -> 33.4 us
    pallas_call x1 -> x2, Pallas kernels: 10.5 us -> 21.4 us  [values(): pl.pallas_call(values_kernel, grid=(s // 2,), in_specs=specs + [whole(g.s...]
    all_to_all x1, blocking collectives: 26.6 us -> 19.2 us  [a2a(): return lax.all_to_all(x, 'seq', split_axis=0, concat_axis=0, tiled=True)]
    all_to_all x3, waiting for transfers between devices: 26 us -> 19.4 us  [a2a(): return lax.all_to_all(x, 'seq', split_axis=0, concat_axis=0, tiled=True)]
    ppermute x1, waiting for transfers between devices: 8.87 us -> 5.41 us  [reduce_yz(): lax.ppermute(other, 'seq', [(i, (i + half) % SEQ) for i in range(SEQ)])]
    unnamed x12 -> x6, local copies, waits for them, and re-layouts: 4.95 us -> 2.29 us
    slice x0 -> x2, local copies, waits for them, and re-layouts: none -> 2.45 us  [the longest x1 1.27 us: shards(): values((x, sib, xh, xhs), hg, wv)[0, 0, 0] + l * 0]
    all_to_all x3, starting transfers between devices: 20.5 us -> 18.3 us  [a2a(): return lax.all_to_all(x, 'seq', split_axis=0, concat_axis=0, tiled=True)]
  transfers between devices with their start and end apart: 8 -> 8, of which waited for: 7 -> 7; matrix products, arithmetic and copies ran while one was open for 2% -> 2% of each run, Pallas kernels for 11% -> 12%
where the time goes in v6:
time: 166 us; the launch traced here: 165 us
  Pallas kernels  55.5 us (33%)
  waiting for transfers between devices  42 us (25%)
  starting transfers between devices  33.4 us (20%)
  blocking collectives  19.2 us (12%)
  local copies, waits for them, and re-layouts  12.4 us (7%)
    pallas_call x2, Pallas kernels, values(): pl.pallas_call(values_kernel, grid=(s // 2,), in_specs=specs + [whole(g.s...  21.4 us
    all_to_all x3, waiting for transfers between devices, a2a(): return lax.all_to_all(x, 'seq', split_axis=0, concat_axis=0, tiled=True)  19.4 us
    all_to_all x1, blocking collectives, a2a(): return lax.all_to_all(x, 'seq', split_axis=0, concat_axis=0, tiled=True)  19.2 us
    all_to_all x3, starting transfers between devices, a2a(): return lax.all_to_all(x, 'seq', split_axis=0, concat_axis=0, tiled=True)  18.3 us
    pallas_call x2, Pallas kernels, logits(): pl.pallas_call(functools.partial(logits_kernel, first), in_specs=[here, h...  17 us
    all_to_all x1, waiting for transfers between devices, reduce_yz(): lax.all_to_all(l, 'seq', split_axis=0, concat_axis=0, tiled=True, axis_in...  12.7 us
    pallas_call x1, Pallas kernels, column(): pl.pallas_call(column_kernel, in_specs=[pl.BlockSpec(memory_space=pltpu.V...  12 us
    all_to_all x1, starting transfers between devices, reduce_yz(): lax.all_to_all(l, 'seq', split_axis=0, concat_axis=0, tiled=True, axis_in...  7.77 us
  transfers between devices with their start and end apart: 8, of which 7 were waited for; matrix products, arithmetic and copies ran while one was open for 2% of the time, Pallas kernels for 12%

profile of v6, /device:TPU:1, one launch (start us, length us, event | category | flops | bytes accessed | tf_op | source)
XLA Modules:
  0.0 164.8 jit_solution(841867499626210279)
XLA Ops:
  0.0 1.4 collective-permute-start.1
  1.4 2.8 %collective-permute-start = (bf16[8,128,768]{2,1,0:T(8,128)(2,1)}, bf16[8,128,768]{2,1,0:T(8,128)(2,1)}, u32[]{:S(2)}, u32[]{:S(2)}) collective-permute-start(bf16[8,128,768]{2,1,0:T(8,128)(2,1)} %x_h.1), channel_id=1, source_target_pairs={{0,2},{1,3},{2,0},{3,1},{4,6},{5,7},{6,4},{7,5},{8,10},{9,11},{10,... | collective-permute-start | bytes 4718600 | tf_op jit(solution)/shard_map/ppermute | solution.py:267
  4.2 1.3 reshape.68.refs_2_.refs_4_
  5.5 1.1 copy-done.1
  6.7 8.7 %logits.2 = (bf16[12,128,512]{2,1,0:T(8,128)(2,1)S(1)}, bf16[12,128,256]{2,1,0:T(8,128)(2,1)S(1)}) custom-call(bf16[8,128,768]{2,1,0:T(8,128)(2,1)} %x_h.1, bf16[8,128,768]{2,1,0:T(8,128)(2,1)} %copy-done.1, f32[1,768]{1,0:T(1,128)} %reshape.68.refs_2_.refs_4_, bf16[768,768]{1,0:T(8,128)(2,1)} %refs_3_.4, bf16[768,768]{1,0:T(8,128)(2,1)} %refs_4_.1), custom_call_target="tpu_custom_call" | custom-call | tf_op jit(solution)/shard_map/logits/pallas_call | solution.py:99
  15.3 1.1 copy-done
  16.5 1.0 copy.20
  17.5 7.8 %all-to-all-start = ((bf16[16,2,48,256]{3,2,1,0:T(8,128)(2,1)}), bf16[16,2,48,256]{3,2,1,0:T(8,128)(2,1)S(1)}, u32[]{:S(2)}, u32[]{:S(2)}) async-start(bf16[16,2,48,256]{3,2,1,0:T(8,128)(2,1)} %bitcast.20), calls=%async_computation | async-start | bytes 1572864 | tf_op jit(solution)/shard_map/all_to_all | solution.py:274
  25.3 12.7 %all-to-all-done = bf16[16,2,48,256]{3,2,1,0:T(8,128)(2,1)S(1)} async-done(((bf16[16,2,48,256]{3,2,1,0:T(8,128)(2,1)}), bf16[16,2,48,256]{3,2,1,0:T(8,128)(2,1)S(1)}, u32[]{:S(2)}, u32[]{:S(2)}) %all-to-all-start) | async-done | bytes 786464 | tf_op jit(solution)/shard_map/all_to_all | solution.py:274
  38.1 1.2 collective-permute-done.refs_0_.refs_2_
  39.3 1.8 %collective-permute-start.3 = (bf16[8,128,768]{2,1,0:T(8,128)(2,1)}, bf16[8,128,768]{2,1,0:T(8,128)(2,1)}, u32[]{:S(2)}, u32[]{:S(2)}) collective-permute-start(bf16[8,128,768]{2,1,0:T(8,128)(2,1)} %collective-permute-done.refs_0_.refs_2_), channel_id=1, source_target_pairs={{0,1},{1,0},{2,3},{3,2},{4,5},{5,4},{6,7},{7,6},{8,9},{9,8},{10,11... | collective-permute-start | bytes 4718600 | tf_op jit(solution)/shard_map/ppermute | solution.py:284
  41.0 3.4 %collective-permute-done.3.refs_1_.refs_3_ = bf16[8,128,768]{2,1,0:T(8,128)(2,1)} collective-permute-done((bf16[8,128,768]{2,1,0:T(8,128)(2,1)}, bf16[8,128,768]{2,1,0:T(8,128)(2,1)}, u32[]{:S(2)}, u32[]{:S(2)}) %collective-permute-start.3) | collective-permute-done | bytes 1572896 | tf_op jit(solution)/shard_map/ppermute | solution.py:284
  44.4 8.3 %logits.3 = bf16[12,128,256]{2,1,0:T(8,128)(2,1)} custom-call(bf16[8,128,768]{2,1,0:T(8,128)(2,1)} %collective-permute-done.refs_0_.refs_2_, bf16[8,128,768]{2,1,0:T(8,128)(2,1)} %collective-permute-done.3.refs_1_.refs_3_, f32[1,768]{1,0:T(1,128)} %reshape.68.refs_2_.refs_4_, bf16[768,768]{1,0:T(8,128)(2,1)} %refs_3_.4, bf16[12,128,512]{2,1,0:T(8,128)(2,1)} %copy-done), custom_call_target="tpu_custom_call" | custom-call | tf_op jit(solution)/shard_map/logits/pallas_call | solution.py:99
  52.7 14.6 %conditional.1 = (bf16[]{:T(256)}) conditional(s32[]{:T(128)} %convert_element_type.32, () %tuple.15, (bf16[8,128,768]{2,1,0:T(8,128)(2,1)}, bf16[8,128,768]{2,1,0:T(8,128)(2,1)}, bf16[8,128,768]{2,1,0:T(8,128)(2,1)}, bf16[8,128,768]{2,1,0:T(8,128)(2,1)}, f32[1,768]{1,0:T(1,128)}, /*index=5*/bf16[768,768]{1,0:T(8,128)(2,1)}, ...), branch_computations={%region_1.2_spmd, %region_2.3_spmd} | conditional | flops 2 | bytes 28 | solution.py:287
  52.9 10.7 %values.2 = bf16[12,512,512]{2,1,0:T(8,128)(2,1)} custom-call(bf16[8,128,768]{2,1,0:T(8,128)(2,1)} %get-tuple-element.22.refs_0_, bf16[8,128,768]{2,1,0:T(8,128)(2,1)} %get-tuple-element.23.refs_1_, bf16[8,128,768]{2,1,0:T(8,128)(2,1)} %get-tuple-element.24.refs_2_, bf16[8,128,768]{2,1,0:T(8,128)(2,1)} %get-tuple-element.25.refs_3_, ...), custom_call_target="tpu_custom_call" | custom-call | tf_op jit(solution)/shard_map/cond/branch_1_fun/values/pallas_call | solution.py:130
  63.6 1.3 slice.8
  64.9 1.2 slice.7
  67.4 8.1 %all-to-all-start.1 = ((bf16[32,48,256]{2,1,0:T(8,128)(2,1)}), bf16[32,48,256]{2,1,0:T(8,128)(2,1)S(1)}, u32[]{:S(2)}, u32[]{:S(2)}) async-start(bf16[32,48,256]{2,1,0:T(8,128)(2,1)} %bitcast.5), calls=%async_computation.1 | async-start | bytes 1572864 | tf_op jit(solution)/shard_map/all_to_all | solution.py:255
  75.5 1.3 collective-permute-start.2
  76.8 5.4 %collective-permute-done.2 = bf16[48,256]{1,0:T(8,128)(2,1)S(1)} collective-permute-done((bf16[48,256]{1,0:T(8,128)(2,1)S(1)}, bf16[48,256]{1,0:T(8,128)(2,1)S(1)}, u32[]{:S(2)}, u32[]{:S(2)}) %collective-permute-start.2) | collective-permute-done | bytes 24608 | tf_op jit(solution)/shard_map/ppermute | solution.py:279
  82.2 3.2 %all-to-all-done.1 = bf16[32,48,256]{2,1,0:T(8,128)(2,1)S(1)} async-done(((bf16[32,48,256]{2,1,0:T(8,128)(2,1)}), bf16[32,48,256]{2,1,0:T(8,128)(2,1)S(1)}, u32[]{:S(2)}, u32[]{:S(2)}) %all-to-all-start.1) | async-done | bytes 786464 | tf_op jit(solution)/shard_map/all_to_all | solution.py:255
  86.1 1.3 broadcast_in_dim.2
  87.4 5.0 %all-to-all-start.2 = ((bf16[32,48,512]{2,1,0:T(8,128)(2,1)}), bf16[32,48,512]{2,1,0:T(8,128)(2,1)S(1)}, u32[]{:S(2)}, u32[]{:S(2)}) async-start(bf16[32,48,512]{2,1,0:T(8,128)(2,1)} %broadcast_in_dim.2), calls=%async_computation.2 | async-start | bytes 3145728 | tf_op jit(solution)/shard_map/all_to_all | solution.py:255
  92.4 10.7 %values.3.v_h = bf16[12,512,512]{2,1,0:T(8,128)(2,1)} custom-call(bf16[8,128,768]{2,1,0:T(8,128)(2,1)} %x_h.1, bf16[8,128,768]{2,1,0:T(8,128)(2,1)} %copy-done.1, bf16[8,128,768]{2,1,0:T(8,128)(2,1)} %collective-permute-done.refs_0_.refs_2_, bf16[8,128,768]{2,1,0:T(8,128)(2,1)} %collective-permute-done.3.refs_1_.refs_3_, f32[1,768]{1,0:T(1,128)} %reshape.68.refs_2_.refs_4_, ...), custom_call_target="tpu_custom_call" | custom-call | tf_op jit(solution)/shard_map/values/pallas_call | solution.py:130
  103.1 3.1 %all-to-all-done.2 = bf16[32,48,512]{2,1,0:T(8,128)(2,1)S(1)} async-done(((bf16[32,48,512]{2,1,0:T(8,128)(2,1)}), bf16[32,48,512]{2,1,0:T(8,128)(2,1)S(1)}, u32[]{:S(2)}, u32[]{:S(2)}) %all-to-all-start.2) | async-done | bytes 1572896 | tf_op jit(solution)/shard_map/all_to_all | solution.py:255
  106.3 5.1 %mix.1 = bf16[8,128,768]{2,1,0:T(8,128)(2,1)S(1)} custom-call(bf16[12,128,512]{2,1,0:T(8,128)(2,1)S(1)} %bitcast.21, bf16[12,512,512]{2,1,0:T(8,128)(2,1)} %values.3.v_h, bf16[8,128,768]{2,1,0:T(8,128)(2,1)} %x_h.1, bf16[768,768]{1,0:T(8,128)(2,1)} %wo_h.1), custom_call_target="tpu_custom_call" | custom-call | tf_op jit(solution)/shard_map/mix/pallas_call | solution.py:165
  111.3 2.0 %copy.17 = bf16[8,128,768]{2,0,1:T(8,128)(2,1)} copy(bf16[8,128,768]{2,1,0:T(8,128)(2,1)S(1)} %mix.1) | data formatting | bytes 3145728 | tf_op jit(solution)/shard_map/reshape | solution.py:300
  113.3 5.2 %all-to-all-start.3 = ((bf16[32,32,768]{2,1,0:T(8,128)(2,1)}), bf16[32,32,768]{2,1,0:T(8,128)(2,1)S(1)}, u32[]{:S(2)}, u32[]{:S(2)}) async-start(bf16[32,32,768]{2,1,0:T(8,128)(2,1)} %bitcast.9), calls=%async_computation.3 | async-start | bytes 3145728 | tf_op jit(solution)/shard_map/all_to_all | solution.py:255
  119.1 13.0 %all-to-all-done.3.h_ref = bf16[32,32,768]{2,1,0:T(8,128)(2,1)S(1)} async-done(((bf16[32,32,768]{2,1,0:T(8,128)(2,1)}), bf16[32,32,768]{2,1,0:T(8,128)(2,1)S(1)}, u32[]{:S(2)}, u32[]{:S(2)}) %all-to-all-start.3) | async-done | bytes 1572896 | tf_op jit(solution)/shard_map/all_to_all | solution.py:255
  132.1 12.0 %column.1 = bf16[32,32,768]{2,1,0:T(8,128)(2,1)S(1)} custom-call(bf16[32,32,768]{2,1,0:T(8,128)(2,1)S(1)} %all-to-all-done.3.h_ref, f32[1,768]{1,0:T(1,128)} %reshape.74.g, bf16[768,768]{1,0:T(8,128)(2,1)} %refs_0_.4, bf16[768,768]{1,0:T(8,128)(2,1)} %refs_1_.1, bf16[768,768]{1,0:T(8,128)(2,1)} %refs_2_.1, bf16[768,768]{1,0:T(8,128)(2,1)} %refs_3_.5), custom_call_target="tpu_custom_call" | custom-call | tf_op jit(solution)/shard_map/column/pallas_call | solution.py:241
  144.2 19.2 %all_to_all.25 = bf16[32,32,768]{2,1,0:T(8,128)(2,1)S(1)} all-to-all(bf16[32,32,768]{2,1,0:T(8,128)(2,1)S(1)} %column.1), channel_id=1, replica_groups=mesh['seq'=32,'res'=4] {'seq'}, dimensions={0} | all-to-all | bytes 3145728 | tf_op jit(solution)/shard_map/all_to_all | solution.py:255
  163.3 1.4 copy.18
  (15 shorter events, 1.3 us)
Async XLA Ops:
  0.0 5.5 %collective-permute-start.1 = (bf16[8,128,768]{2,1,0:T(8,128)(2,1)}, bf16[8,128,768]{2,1,0:T(8,128)(2,1)S(1)}, u32[]{:S(2)}, u32[]{:S(2)}) collective-permute-start(bf16[8,128,768]{2,1,0:T(8,128)(2,1)} %x_h.1), channel_id=1, source_target_pairs={{0,1},{1,0},{2,3},{3,2},{4,5},{5,4},{6,7},{7,6},{8,9},{9,8},{10,11... | collective-permute-start | bytes 4718600 | tf_op jit(solution)/shard_map/ppermute | solution.py:268
  1.4 37.8 %collective-permute-start = (bf16[8,128,768]{2,1,0:T(8,128)(2,1)}, bf16[8,128,768]{2,1,0:T(8,128)(2,1)}, u32[]{:S(2)}, u32[]{:S(2)}) collective-permute-start(bf16[8,128,768]{2,1,0:T(8,128)(2,1)} %x_h.1), channel_id=1, source_target_pairs={{0,2},{1,3},{2,0},{3,1},{4,6},{5,7},{6,4},{7,5},{8,10},{9,11},{10,... | collective-permute-start | bytes 4718600 | tf_op jit(solution)/shard_map/ppermute | solution.py:267
  5.5 1.1 copy-start.1
  15.3 1.2 copy-start
  17.5 20.5 %all-to-all-start = ((bf16[16,2,48,256]{3,2,1,0:T(8,128)(2,1)}), bf16[16,2,48,256]{3,2,1,0:T(8,128)(2,1)S(1)}, u32[]{:S(2)}, u32[]{:S(2)}) async-start(bf16[16,2,48,256]{3,2,1,0:T(8,128)(2,1)} %bitcast.20), calls=%async_computation | async-start | bytes 1572864 | tf_op jit(solution)/shard_map/all_to_all | solution.py:274
  39.3 5.1 %collective-permute-start.3 = (bf16[8,128,768]{2,1,0:T(8,128)(2,1)}, bf16[8,128,768]{2,1,0:T(8,128)(2,1)}, u32[]{:S(2)}, u32[]{:S(2)}) collective-permute-start(bf16[8,128,768]{2,1,0:T(8,128)(2,1)} %collective-permute-done.refs_0_.refs_2_), channel_id=1, source_target_pairs={{0,1},{1,0},{2,3},{3,2},{4,5},{5,4},{6,7},{7,6},{8,9},{9,8},{10,11... | collective-permute-start | bytes 4718600 | tf_op jit(solution)/shard_map/ppermute | solution.py:284
  67.4 18.1 %all-to-all-start.1 = ((bf16[32,48,256]{2,1,0:T(8,128)(2,1)}), bf16[32,48,256]{2,1,0:T(8,128)(2,1)S(1)}, u32[]{:S(2)}, u32[]{:S(2)}) async-start(bf16[32,48,256]{2,1,0:T(8,128)(2,1)} %bitcast.5), calls=%async_computation.1 | async-start | bytes 1572864 | tf_op jit(solution)/shard_map/all_to_all | solution.py:255
  75.5 6.7 %collective-permute-start.2 = (bf16[48,256]{1,0:T(8,128)(2,1)S(1)}, bf16[48,256]{1,0:T(8,128)(2,1)S(1)}, u32[]{:S(2)}, u32[]{:S(2)}) collective-permute-start(bf16[48,256]{1,0:T(8,128)(2,1)S(1)} %fusion.2), channel_id=1, source_target_pairs={{0,64},{4,68},{8,72},{12,76},{16,80},{20,84},{24,88},{28,92},{32,9... | collective-permute-start | bytes 73736 | tf_op jit(solution)/shard_map/ppermute | solution.py:279
  87.4 18.8 %all-to-all-start.2 = ((bf16[32,48,512]{2,1,0:T(8,128)(2,1)}), bf16[32,48,512]{2,1,0:T(8,128)(2,1)S(1)}, u32[]{:S(2)}, u32[]{:S(2)}) async-start(bf16[32,48,512]{2,1,0:T(8,128)(2,1)} %broadcast_in_dim.2), calls=%async_computation.2 | async-start | bytes 3145728 | tf_op jit(solution)/shard_map/all_to_all | solution.py:255
  113.3 5.2 %copy-start.2 = (f32[768]{0:T(1024)S(1)}, f32[768]{0:T(1024)}, u32[]{:S(2)}) copy-start(f32[768]{0:T(1024)} %param.19) | copy-start | bytes 9220
  113.3 18.8 %all-to-all-start.3 = ((bf16[32,32,768]{2,1,0:T(8,128)(2,1)}), bf16[32,32,768]{2,1,0:T(8,128)(2,1)S(1)}, u32[]{:S(2)}, u32[]{:S(2)}) async-start(bf16[32,32,768]{2,1,0:T(8,128)(2,1)} %bitcast.9), calls=%async_computation.3 | async-start | bytes 3145728 | tf_op jit(solution)/shard_map/all_to_all | solution.py:255

commit v7 on v6

--- a/solution.py
+++ b/solution.py
@@ -212,7 +212,9 @@
             for z in (l[:, :a], l[:, a:]):
                 e.append(jnp.exp2(z - jnp.max(z, axis=-1, keepdims=True)).astype(BF16))
             w = mm(jnp.concatenate(e, axis=1), jnp.concatenate([v, ones], axis=1))
-            ms[r, c] = (w[:, : 2 * D] / w[:, 2 * D :]).astype(BF16)
+            d = w[:, 2 * D :]
+            i = pl.reciprocal(d, approx=True)
+            ms[r, c] = (w[:, : 2 * D] * (i * (2.0 - d * i))).astype(BF16)
         return carry
 
     for p in range(rows // 8):

time: 166 us -> 166 us (level)
  no operation moved by 1% of the time
where the time goes in v7:
time: 166 us; the launch traced here: 165 us
  Pallas kernels  55.5 us (33%)
  waiting for transfers between devices  42 us (25%)
  starting transfers between devices  33.4 us (20%)
  blocking collectives  19.2 us (12%)
  local copies, waits for them, and re-layouts  12.4 us (7%)
    pallas_call x2, Pallas kernels, values(): pl.pallas_call(values_kernel, grid=(s // 2,), in_specs=specs + [whole(g.s...  21.4 us
    all_to_all x3, waiting for transfers between devices, a2a(): return lax.all_to_all(x, 'seq', split_axis=0, concat_axis=0, tiled=True)  19.4 us
    all_to_all x1, blocking collectives, a2a(): return lax.all_to_all(x, 'seq', split_axis=0, concat_axis=0, tiled=True)  19.2 us
    all_to_all x3, starting transfers between devices, a2a(): return lax.all_to_all(x, 'seq', split_axis=0, concat_axis=0, tiled=True)  18.3 us
    pallas_call x2, Pallas kernels, logits(): pl.pallas_call(functools.partial(logits_kernel, first), in_specs=[here, h...  17 us
    all_to_all x1, waiting for transfers between devices, reduce_yz(): lax.all_to_all(l, 'seq', split_axis=0, concat_axis=0, tiled=True, axis_in...  12.7 us
    pallas_call x1, Pallas kernels, column(): pl.pallas_call(column_kernel, in_specs=[pl.BlockSpec(memory_space=pltpu.V...  12.1 us
    all_to_all x1, starting transfers between devices, reduce_yz(): lax.all_to_all(l, 'seq', split_axis=0, concat_axis=0, tiled=True, axis_in...  7.77 us
  transfers between devices with their start and end apart: 8, of which 7 were waited for; matrix products, arithmetic and copies ran while one was open for 2% of the time, Pallas kernels for 12%

profile of v7, /device:TPU:1, one launch (start us, length us, event | category | flops | bytes accessed | tf_op | source)
XLA Modules:
  0.0 164.8 jit_solution(10950885670899808963)
XLA Ops:
  0.0 1.4 collective-permute-start.1
  1.4 2.8 %collective-permute-start = (bf16[8,128,768]{2,1,0:T(8,128)(2,1)}, bf16[8,128,768]{2,1,0:T(8,128)(2,1)}, u32[]{:S(2)}, u32[]{:S(2)}) collective-permute-start(bf16[8,128,768]{2,1,0:T(8,128)(2,1)} %x_h.1), channel_id=1, source_target_pairs={{0,2},{1,3},{2,0},{3,1},{4,6},{5,7},{6,4},{7,5},{8,10},{9,11},{10,... | collective-permute-start | bytes 4718600 | tf_op jit(solution)/shard_map/ppermute | solution.py:269
  4.2 1.3 reshape.68.refs_2_.refs_4_
  5.5 1.1 copy-done.1
  6.7 8.7 %logits.2 = (bf16[12,128,512]{2,1,0:T(8,128)(2,1)S(1)}, bf16[12,128,256]{2,1,0:T(8,128)(2,1)S(1)}) custom-call(bf16[8,128,768]{2,1,0:T(8,128)(2,1)} %x_h.1, bf16[8,128,768]{2,1,0:T(8,128)(2,1)} %copy-done.1, f32[1,768]{1,0:T(1,128)} %reshape.68.refs_2_.refs_4_, bf16[768,768]{1,0:T(8,128)(2,1)} %refs_3_.4, bf16[768,768]{1,0:T(8,128)(2,1)} %refs_4_.1), custom_call_target="tpu_custom_call" | custom-call | tf_op jit(solution)/shard_map/logits/pallas_call | solution.py:99
  15.3 1.1 copy-done
  16.5 1.0 copy.20
  17.5 7.8 %all-to-all-start = ((bf16[16,2,48,256]{3,2,1,0:T(8,128)(2,1)}), bf16[16,2,48,256]{3,2,1,0:T(8,128)(2,1)S(1)}, u32[]{:S(2)}, u32[]{:S(2)}) async-start(bf16[16,2,48,256]{3,2,1,0:T(8,128)(2,1)} %bitcast.20), calls=%async_computation | async-start | bytes 1572864 | tf_op jit(solution)/shard_map/all_to_all | solution.py:276
  25.3 12.7 %all-to-all-done = bf16[16,2,48,256]{3,2,1,0:T(8,128)(2,1)S(1)} async-done(((bf16[16,2,48,256]{3,2,1,0:T(8,128)(2,1)}), bf16[16,2,48,256]{3,2,1,0:T(8,128)(2,1)S(1)}, u32[]{:S(2)}, u32[]{:S(2)}) %all-to-all-start) | async-done | bytes 786464 | tf_op jit(solution)/shard_map/all_to_all | solution.py:276
  38.1 1.2 collective-permute-done.refs_0_.refs_2_
  39.3 1.8 %collective-permute-start.3 = (bf16[8,128,768]{2,1,0:T(8,128)(2,1)}, bf16[8,128,768]{2,1,0:T(8,128)(2,1)}, u32[]{:S(2)}, u32[]{:S(2)}) collective-permute-start(bf16[8,128,768]{2,1,0:T(8,128)(2,1)} %collective-permute-done.refs_0_.refs_2_), channel_id=1, source_target_pairs={{0,1},{1,0},{2,3},{3,2},{4,5},{5,4},{6,7},{7,6},{8,9},{9,8},{10,11... | collective-permute-start | bytes 4718600 | tf_op jit(solution)/shard_map/ppermute | solution.py:286
  41.0 3.4 %collective-permute-done.3.refs_1_.refs_3_ = bf16[8,128,768]{2,1,0:T(8,128)(2,1)} collective-permute-done((bf16[8,128,768]{2,1,0:T(8,128)(2,1)}, bf16[8,128,768]{2,1,0:T(8,128)(2,1)}, u32[]{:S(2)}, u32[]{:S(2)}) %collective-permute-start.3) | collective-permute-done | bytes 1572896 | tf_op jit(solution)/shard_map/ppermute | solution.py:286
  44.4 8.3 %logits.3 = bf16[12,128,256]{2,1,0:T(8,128)(2,1)} custom-call(bf16[8,128,768]{2,1,0:T(8,128)(2,1)} %collective-permute-done.refs_0_.refs_2_, bf16[8,128,768]{2,1,0:T(8,128)(2,1)} %collective-permute-done.3.refs_1_.refs_3_, f32[1,768]{1,0:T(1,128)} %reshape.68.refs_2_.refs_4_, bf16[768,768]{1,0:T(8,128)(2,1)} %refs_3_.4, bf16[12,128,512]{2,1,0:T(8,128)(2,1)} %copy-done), custom_call_target="tpu_custom_call" | custom-call | tf_op jit(solution)/shard_map/logits/pallas_call | solution.py:99
  52.7 14.6 %conditional.1 = (bf16[]{:T(256)}) conditional(s32[]{:T(128)} %convert_element_type.32, () %tuple.15, (bf16[8,128,768]{2,1,0:T(8,128)(2,1)}, bf16[8,128,768]{2,1,0:T(8,128)(2,1)}, bf16[8,128,768]{2,1,0:T(8,128)(2,1)}, bf16[8,128,768]{2,1,0:T(8,128)(2,1)}, f32[1,768]{1,0:T(1,128)}, /*index=5*/bf16[768,768]{1,0:T(8,128)(2,1)}, ...), branch_computations={%region_1.2_spmd, %region_2.3_spmd} | conditional | flops 2 | bytes 28 | solution.py:289
  52.9 10.7 %values.2 = bf16[12,512,512]{2,1,0:T(8,128)(2,1)} custom-call(bf16[8,128,768]{2,1,0:T(8,128)(2,1)} %get-tuple-element.22.refs_0_, bf16[8,128,768]{2,1,0:T(8,128)(2,1)} %get-tuple-element.23.refs_1_, bf16[8,128,768]{2,1,0:T(8,128)(2,1)} %get-tuple-element.24.refs_2_, bf16[8,128,768]{2,1,0:T(8,128)(2,1)} %get-tuple-element.25.refs_3_, ...), custom_call_target="tpu_custom_call" | custom-call | tf_op jit(solution)/shard_map/cond/branch_1_fun/values/pallas_call | solution.py:130
  63.6 1.3 slice.8
  64.9 1.2 slice.7
  67.4 8.1 %all-to-all-start.1 = ((bf16[32,48,256]{2,1,0:T(8,128)(2,1)}), bf16[32,48,256]{2,1,0:T(8,128)(2,1)S(1)}, u32[]{:S(2)}, u32[]{:S(2)}) async-start(bf16[32,48,256]{2,1,0:T(8,128)(2,1)} %bitcast.5), calls=%async_computation.1 | async-start | bytes 1572864 | tf_op jit(solution)/shard_map/all_to_all | solution.py:257
  75.5 1.3 collective-permute-start.2
  76.8 5.4 %collective-permute-done.2 = bf16[48,256]{1,0:T(8,128)(2,1)S(1)} collective-permute-done((bf16[48,256]{1,0:T(8,128)(2,1)S(1)}, bf16[48,256]{1,0:T(8,128)(2,1)S(1)}, u32[]{:S(2)}, u32[]{:S(2)}) %collective-permute-start.2) | collective-permute-done | bytes 24608 | tf_op jit(solution)/shard_map/ppermute | solution.py:281
  82.2 3.2 %all-to-all-done.1 = bf16[32,48,256]{2,1,0:T(8,128)(2,1)S(1)} async-done(((bf16[32,48,256]{2,1,0:T(8,128)(2,1)}), bf16[32,48,256]{2,1,0:T(8,128)(2,1)S(1)}, u32[]{:S(2)}, u32[]{:S(2)}) %all-to-all-start.1) | async-done | bytes 786464 | tf_op jit(solution)/shard_map/all_to_all | solution.py:257
  86.1 1.3 broadcast_in_dim.2
  87.4 5.0 %all-to-all-start.2 = ((bf16[32,48,512]{2,1,0:T(8,128)(2,1)}), bf16[32,48,512]{2,1,0:T(8,128)(2,1)S(1)}, u32[]{:S(2)}, u32[]{:S(2)}) async-start(bf16[32,48,512]{2,1,0:T(8,128)(2,1)} %broadcast_in_dim.2), calls=%async_computation.2 | async-start | bytes 3145728 | tf_op jit(solution)/shard_map/all_to_all | solution.py:257
  92.4 10.7 %values.3.v_h = bf16[12,512,512]{2,1,0:T(8,128)(2,1)} custom-call(bf16[8,128,768]{2,1,0:T(8,128)(2,1)} %x_h.1, bf16[8,128,768]{2,1,0:T(8,128)(2,1)} %copy-done.1, bf16[8,128,768]{2,1,0:T(8,128)(2,1)} %collective-permute-done.refs_0_.refs_2_, bf16[8,128,768]{2,1,0:T(8,128)(2,1)} %collective-permute-done.3.refs_1_.refs_3_, f32[1,768]{1,0:T(1,128)} %reshape.68.refs_2_.refs_4_, ...), custom_call_target="tpu_custom_call" | custom-call | tf_op jit(solution)/shard_map/values/pallas_call | solution.py:130
  103.1 3.1 %all-to-all-done.2 = bf16[32,48,512]{2,1,0:T(8,128)(2,1)S(1)} async-done(((bf16[32,48,512]{2,1,0:T(8,128)(2,1)}), bf16[32,48,512]{2,1,0:T(8,128)(2,1)S(1)}, u32[]{:S(2)}, u32[]{:S(2)}) %all-to-all-start.2) | async-done | bytes 1572896 | tf_op jit(solution)/shard_map/all_to_all | solution.py:257
  106.3 5.1 %mix.1 = bf16[8,128,768]{2,1,0:T(8,128)(2,1)S(1)} custom-call(bf16[12,128,512]{2,1,0:T(8,128)(2,1)S(1)} %bitcast.21, bf16[12,512,512]{2,1,0:T(8,128)(2,1)} %values.3.v_h, bf16[8,128,768]{2,1,0:T(8,128)(2,1)} %x_h.1, bf16[768,768]{1,0:T(8,128)(2,1)} %wo_h.1), custom_call_target="tpu_custom_call" | custom-call | tf_op jit(solution)/shard_map/mix/pallas_call | solution.py:165
  111.3 2.0 %copy.17 = bf16[8,128,768]{2,0,1:T(8,128)(2,1)} copy(bf16[8,128,768]{2,1,0:T(8,128)(2,1)S(1)} %mix.1) | data formatting | bytes 3145728 | tf_op jit(solution)/shard_map/reshape | solution.py:302
  113.3 5.2 %all-to-all-start.3 = ((bf16[32,32,768]{2,1,0:T(8,128)(2,1)}), bf16[32,32,768]{2,1,0:T(8,128)(2,1)S(1)}, u32[]{:S(2)}, u32[]{:S(2)}) async-start(bf16[32,32,768]{2,1,0:T(8,128)(2,1)} %bitcast.9), calls=%async_computation.3 | async-start | bytes 3145728 | tf_op jit(solution)/shard_map/all_to_all | solution.py:257
  119.1 13.0 %all-to-all-done.3.h_ref = bf16[32,32,768]{2,1,0:T(8,128)(2,1)S(1)} async-done(((bf16[32,32,768]{2,1,0:T(8,128)(2,1)}), bf16[32,32,768]{2,1,0:T(8,128)(2,1)S(1)}, u32[]{:S(2)}, u32[]{:S(2)}) %all-to-all-start.3) | async-done | bytes 1572896 | tf_op jit(solution)/shard_map/all_to_all | solution.py:257
  132.1 12.1 %column.1 = bf16[32,32,768]{2,1,0:T(8,128)(2,1)S(1)} custom-call(bf16[32,32,768]{2,1,0:T(8,128)(2,1)S(1)} %all-to-all-done.3.h_ref, f32[1,768]{1,0:T(1,128)} %reshape.74.g, bf16[768,768]{1,0:T(8,128)(2,1)} %refs_0_.4, bf16[768,768]{1,0:T(8,128)(2,1)} %refs_1_.1, bf16[768,768]{1,0:T(8,128)(2,1)} %refs_2_.1, bf16[768,768]{1,0:T(8,128)(2,1)} %refs_3_.5), custom_call_target="tpu_custom_call" | custom-call | tf_op jit(solution)/shard_map/column/pallas_call | solution.py:243
  144.2 19.2 %all_to_all.25 = bf16[32,32,768]{2,1,0:T(8,128)(2,1)S(1)} all-to-all(bf16[32,32,768]{2,1,0:T(8,128)(2,1)S(1)} %column.1), channel_id=1, replica_groups=mesh['seq'=32,'res'=4] {'seq'}, dimensions={0} | all-to-all | bytes 3145728 | tf_op jit(solution)/shard_map/all_to_all | solution.py:257
  163.3 1.4 copy.18
  (15 shorter events, 1.3 us)
Async XLA Ops:
  0.0 5.5 %collective-permute-start.1 = (bf16[8,128,768]{2,1,0:T(8,128)(2,1)}, bf16[8,128,768]{2,1,0:T(8,128)(2,1)S(1)}, u32[]{:S(2)}, u32[]{:S(2)}) collective-permute-start(bf16[8,128,768]{2,1,0:T(8,128)(2,1)} %x_h.1), channel_id=1, source_target_pairs={{0,1},{1,0},{2,3},{3,2},{4,5},{5,4},{6,7},{7,6},{8,9},{9,8},{10,11... | collective-permute-start | bytes 4718600 | tf_op jit(solution)/shard_map/ppermute | solution.py:270
  1.4 37.8 %collective-permute-start = (bf16[8,128,768]{2,1,0:T(8,128)(2,1)}, bf16[8,128,768]{2,1,0:T(8,128)(2,1)}, u32[]{:S(2)}, u32[]{:S(2)}) collective-permute-start(bf16[8,128,768]{2,1,0:T(8,128)(2,1)} %x_h.1), channel_id=1, source_target_pairs={{0,2},{1,3},{2,0},{3,1},{4,6},{5,7},{6,4},{7,5},{8,10},{9,11},{10,... | collective-permute-start | bytes 4718600 | tf_op jit(solution)/shard_map/ppermute | solution.py:269
  5.5 1.1 copy-start.1
  15.3 1.2 copy-start
  17.5 20.5 %all-to-all-start = ((bf16[16,2,48,256]{3,2,1,0:T(8,128)(2,1)}), bf16[16,2,48,256]{3,2,1,0:T(8,128)(2,1)S(1)}, u32[]{:S(2)}, u32[]{:S(2)}) async-start(bf16[16,2,48,256]{3,2,1,0:T(8,128)(2,1)} %bitcast.20), calls=%async_computation | async-start | bytes 1572864 | tf_op jit(solution)/shard_map/all_to_all | solution.py:276
  39.3 5.1 %collective-permute-start.3 = (bf16[8,128,768]{2,1,0:T(8,128)(2,1)}, bf16[8,128,768]{2,1,0:T(8,128)(2,1)}, u32[]{:S(2)}, u32[]{:S(2)}) collective-permute-start(bf16[8,128,768]{2,1,0:T(8,128)(2,1)} %collective-permute-done.refs_0_.refs_2_), channel_id=1, source_target_pairs={{0,1},{1,0},{2,3},{3,2},{4,5},{5,4},{6,7},{7,6},{8,9},{9,8},{10,11... | collective-permute-start | bytes 4718600 | tf_op jit(solution)/shard_map/ppermute | solution.py:286
  67.4 18.1 %all-to-all-start.1 = ((bf16[32,48,256]{2,1,0:T(8,128)(2,1)}), bf16[32,48,256]{2,1,0:T(8,128)(2,1)S(1)}, u32[]{:S(2)}, u32[]{:S(2)}) async-start(bf16[32,48,256]{2,1,0:T(8,128)(2,1)} %bitcast.5), calls=%async_computation.1 | async-start | bytes 1572864 | tf_op jit(solution)/shard_map/all_to_all | solution.py:257
  75.5 6.7 %collective-permute-start.2 = (bf16[48,256]{1,0:T(8,128)(2,1)S(1)}, bf16[48,256]{1,0:T(8,128)(2,1)S(1)}, u32[]{:S(2)}, u32[]{:S(2)}) collective-permute-start(bf16[48,256]{1,0:T(8,128)(2,1)S(1)} %fusion.2), channel_id=1, source_target_pairs={{0,64},{4,68},{8,72},{12,76},{16,80},{20,84},{24,88},{28,92},{32,9... | collective-permute-start | bytes 73736 | tf_op jit(solution)/shard_map/ppermute | solution.py:281
  87.4 18.8 %all-to-all-start.2 = ((bf16[32,48,512]{2,1,0:T(8,128)(2,1)}), bf16[32,48,512]{2,1,0:T(8,128)(2,1)S(1)}, u32[]{:S(2)}, u32[]{:S(2)}) async-start(bf16[32,48,512]{2,1,0:T(8,128)(2,1)} %broadcast_in_dim.2), calls=%async_computation.2 | async-start | bytes 3145728 | tf_op jit(solution)/shard_map/all_to_all | solution.py:257
  113.3 5.2 %copy-start.2 = (f32[768]{0:T(1024)S(1)}, f32[768]{0:T(1024)}, u32[]{:S(2)}) copy-start(f32[768]{0:T(1024)} %param.19) | copy-start | bytes 9220
  113.3 18.8 %all-to-all-start.3 = ((bf16[32,32,768]{2,1,0:T(8,128)(2,1)}), bf16[32,32,768]{2,1,0:T(8,128)(2,1)S(1)}, u32[]{:S(2)}, u32[]{:S(2)}) async-start(bf16[32,32,768]{2,1,0:T(8,128)(2,1)} %bitcast.9), calls=%async_computation.3 | async-start | bytes 3145728 | tf_op jit(solution)/shard_map/all_to_all | solution.py:257
